TPU v7x, 32 devices: a whole 2x2x4 slice. The times are simulated.
32 devices in a mesh: groups: 2 (over x), frame: 16 (over z, y, core).
Axes of the slice: x: 2, y: 2, z: 4, core: 2. Of those that a mesh axis runs over, the one named last changes fastest.
Arguments:
- frames_in: bfloat16 [32, 256, 2240], P(('groups', 'frame')), parts along dimension 0, may hold values from -16 to 16
- qkv_weight: bfloat16 [3, 2240, 1280], P(None, None, 'frame'), may hold values from -0.125 to 0.125
Outputs:
- attended: bfloat16 [32, 256, 1280], P(('groups', 'frame')), parts along dimension 0
There are 2 independent parts, one for each index of `groups`. A program takes and returns all parts, laid end to end along the dimension named above; an argument that names none is the same for every part. Nothing has to cross between parts.
All inputs are finite; a program needn't handle non-finite values.
Results may differ from a plain program's by a relative error of at most 0.0039.
Values may be sent and summed in bfloat16 or wider, within the bound.
No kernel may reach another device: no remote copies, remote signals or barrier semaphores. Data moves between devices by JAX's collectives and lax.ppermute only.
A program may use at most 128 MiB of HBM per device.

v0:
```python
import jax
import jax.numpy as jnp
from jax import lax
from jax.sharding import PartitionSpec as P

HEAD_DIM = 32
HEADS = 40


EPSILON = 1e-06


def entering(shard, axis, join, neutral):
    place = lax.axis_index(axis)
    gathered = jax.tree.map(
        lambda a, kind: lax.all_gather(a.astype(kind), axis), shard, (jnp.bfloat16, jnp.bfloat16)
    )
    state = jax.tree.map(lambda a, e: jnp.zeros_like(a) + jnp.asarray(e, a.dtype), shard, neutral)

    def one(hop, state):
        return join(
            state,
            jax.tree.map(
                lambda a, own: lax.dynamic_index_in_dim(a, hop, 0, False).astype(own.dtype),
                gathered,
                shard,
            ),
        )

    return lax.fori_loop(0, place, one, state)


def add_pair(earlier, later):
    return (earlier[0] + later[0], earlier[1] + later[1])


def carry_states(key_rows, value_rows):
    count = key_rows.shape[0]
    feature_k = jax.nn.relu(key_rows).reshape(count, HEADS, HEAD_DIM)
    values = value_rows.reshape(count, HEADS, HEAD_DIM)
    local_state = jnp.einsum("thi,thj->hij", feature_k, values, preferred_element_type=jnp.float32)
    local_keys = jnp.sum(feature_k.astype(jnp.float32), axis=0)
    prior_state, prior_keys = entering(
        (local_state, local_keys),
        "frame",
        add_pair,
        (jnp.zeros_like(local_state), jnp.zeros_like(local_keys)),
    )
    return (local_state, local_keys, prior_state, prior_keys)


def apply_state(feature_q, state, key_sum):
    numer = jnp.einsum("thi,hij->thj", feature_q, state, precision=lax.Precision.HIGHEST)
    denom = jnp.einsum("thi,hi->th", feature_q, key_sum, precision=lax.Precision.HIGHEST)
    return (numer, denom)


def shards(frames_in, qkv_weight):
    tokens = frames_in[0]
    count = tokens.shape[0]
    weights_all = lax.all_gather(qkv_weight, "frame", axis=2, tiled=True)
    projected = jnp.einsum("td,sdc->stc", tokens, weights_all, preferred_element_type=jnp.float32)
    queries = projected[0]
    key_rows = projected[1].astype(jnp.bfloat16)
    value_rows = projected[2].astype(jnp.bfloat16)
    local_state, local_keys, prior_state, prior_keys = carry_states(key_rows, value_rows)
    feature_q = jax.nn.relu(queries).reshape(count, HEADS, HEAD_DIM)
    own_numer, own_denom = apply_state(feature_q, local_state, local_keys)
    past_numer, past_denom = apply_state(feature_q, prior_state, prior_keys)
    numer = past_numer + own_numer
    denom = past_denom + own_denom
    attended = (numer / (denom[:, :, None] + EPSILON)).astype(jnp.bfloat16)
    return attended.reshape(1, count, HEADS * HEAD_DIM)


def solution(mesh):
    placed = (P(("groups", "frame"), None, None), P(None, None, "frame"))
    return jax.shard_map(
        shards,
        mesh=mesh,
        in_specs=placed,
        out_specs=P(("groups", "frame"), None, None),
        check_vma=False,
    )
```

profile of v0, /device:TPU:29, one launch (start us, length us, event | category | flops | bytes accessed | tf_op | source)
XLA Modules:
  0.0 198.7 jit_solution(12941034522131766999)
XLA Ops:
  6.5 0.0 copy-start
  6.5 0.0 all-gather.4.cloned.1.call-start
  6.5 0.7 all-gather.4.cloned.1.call-update
  7.3 0.0 all-gather.6.cloned.1.call-start
  7.3 95.5 %all-gather.4.cloned.1.call-done = bf16[3,2240,1280]{1,2,0:T(8,128)(2,1)} async-done(((bf16[3,2240,80]{1,2,0:T(8,128)(2,1)}), bf16[3,2240,1280]{1,2,0:T(8,128)(2,1)}) %all-gather.4.cloned.1.call-update) | async-done | bytes 17203216 | tf_op jit(solution)/shard_map/all_gather | solution.py:61
  102.8 0.0 copy-done
  102.8 8.5 %convolution_bitcast_fusion = f32[3,256,1280]{1,2,0:T(8,128)S(1)} fusion(bf16[3,2240,1280]{1,2,0:T(8,128)(2,1)} %all-gather.4.cloned.1.call-done, bf16[1,256,2240]{1,2,0:T(8,128)(2,1)S(1)} %copy-done), kind=kOutput, calls=%fused_computation.3 | convolution fusion | flops 4404019200 | bytes 22282240 | tf_op jit(solution)/shard_map/td,sdc->stc/dot_general | solution.py:62
  111.3 0.3 convert_reduce_fusion
  111.6 0.1 slice.21
  111.6 1.3 fusion.8
  112.9 0.0 all-gather.6.cloned.1.call-update
  113.0 0.1 reshape.41
  113.0 0.1 convert_element_type.51
  113.1 0.1 copy.9
  113.2 17.0 %all_gather.16 = bf16[16,40,32]{1,2,0:T(8,128)(2,1)S(1)} all-gather(bf16[1,40,32]{1,2,0:T(8,128)(2,1)S(1)} %copy.9), channel_id=1, replica_groups=mesh['groups'=2,'frame'=16] {'frame'}, dimensions={0}, use_global_device_ids=true | all-gather | bytes 43520 | tf_op jit(solution)/shard_map/all_gather | solution.py:16
  130.2 0.8 fusion.11
  130.9 37.0 %all-gather.6.cloned.1.call-done = bf16[640,32,32]{2,1,0:T(8,128)(2,1)} async-done(((bf16[40,32,32]{2,1,0:T(8,128)(2,1)}), bf16[640,32,32]{2,1,0:T(8,128)(2,1)}) %all-gather.6.cloned.1.call-update) | async-done | bytes 1310736 | tf_op jit(solution)/shard_map/all_gather | solution.py:16
  168.0 0.1 broadcast_in_dim.7
  168.1 19.2 %while.12 = (s32[]{:T(128)}, f32[40,32,32]{2,1,0:T(8,128)S(1)}, f32[40,32]{1,0:T(8,128)S(1)}, s32[]{:T(128)}, bf16[16,40,32,32]{3,2,1,0:T(8,128)(2,1)}, /*index=...) while((s32[]{:T(128)}, f32[40,32,32]{2,1,0:T(8,128)S(1)}, f32[40,32]{1,0:T(8,128)S(1)}, ...), condition=%wide.region_2.3_spmd, body=%wide.region_1.2_spmd.sunk | while | flops 84485 | bytes 432775 | solution.py:30
  168.1 1.1 convert_add_fusion.4
  169.2 0.1 copy.24
  169.4 1.1 convert_add_fusion.4
  170.5 0.1 copy.24
  170.6 1.1 convert_add_fusion.4
  171.8 0.1 copy.24
  171.9 1.1 convert_add_fusion.4
  173.1 0.1 copy.24
  173.2 1.1 convert_add_fusion.4
  174.4 0.1 copy.24
  174.5 1.1 convert_add_fusion.4
  175.6 0.1 copy.24
  175.8 1.1 convert_add_fusion.4
  176.9 0.1 copy.24
  177.0 1.1 convert_add_fusion.4
  178.2 0.1 copy.24
  178.3 1.1 convert_add_fusion.4
  179.5 0.1 copy.24
  179.6 1.1 convert_add_fusion.4
  180.8 0.1 copy.24
  180.9 1.1 convert_add_fusion.4
  182.0 0.1 copy.24
  182.2 1.1 convert_add_fusion.4
  183.3 0.1 copy.24
  183.4 1.1 convert_add_fusion.4
  184.6 0.1 copy.24
  184.7 1.1 convert_add_fusion.4
  185.9 0.1 copy.24
  186.0 1.1 convert_add_fusion.4
  187.2 0.1 copy.24
  187.3 0.8 fusion.10
  188.0 0.0 copy-start.1
  188.0 1.3 fusion.9
  189.4 0.0 copy-done.1
  189.4 1.4 fusion.2
  190.8 1.1 copy.13
  (33 shorter events, 0.3 us)
Async XLA Ops:
  6.5 96.2 %copy-start = (bf16[1,256,2240]{1,2,0:T(8,128)(2,1)S(1)}, bf16[1,256,2240]{1,2,0:T(8,128)(2,1)}, u32[]{:S(2)}) copy-start(bf16[1,256,2240]{1,2,0:T(8,128)(2,1)} %param.4) | copy-start | bytes 3440644
  6.5 96.2 %all-gather.4.cloned.1.call-start = ((), (), s32[]{:S(2)}) async-start(), calls=%async_computation | async-start | bytes 18800640 | tf_op jit(solution)/shard_map/all_gather | solution.py:61
  7.3 160.7 %all-gather.6.cloned.1.call-start = ((), (), s32[]{:S(2)}) async-start(), calls=%async_computation.1 | async-start | bytes 5570560 | tf_op jit(solution)/shard_map/all_gather | solution.py:16
  188.0 1.4 copy-start.1
Sparse Core Ops, SparseCore 0:
  8.9 93.8 all-gather.3
  113.1 54.8 all-gather.5
where the time goes:
time: 199 us
  waiting for transfers between devices  133 us (67%)
  other arithmetic  17.4 us (9%)
  blocking collectives  17 us (9%)
  matrix products  14 us (7%)
  between operations  13.5 us (7%)
  local copies, waits for them, and re-layouts  2.92 us (1%)
    all_gather x1, waiting for transfers between devices, shards(): weights_all = lax.all_gather(qkv_weight, 'frame', axis=2, tiled=True)  95.5 us
    all_gather x1, waiting for transfers between devices, entering(): lax.all_gather(a.astype(kind), axis)  37 us
    add x30, other arithmetic, add_pair(): return (earlier[0] + later[0], earlier[1] + later[1])  17.2 us
    all_gather x1, blocking collectives, entering(): lax.all_gather(a.astype(kind), axis)  17 us
    dot_general x1, matrix products, shards(): jnp.einsum('td,sdc->stc', tokens, weights_all, preferred_element_type=jnp...  8.53 us
  transfers between devices with their start and end apart: 2, of which 2 were waited for; matrix products, arithmetic and copies ran while one was open for 1% of the time, Pallas kernels for 0%

commit v1 on v0

v1 whole, which is shorter than its diff:
```python
import jax
import jax.numpy as jnp
from jax import lax
from jax.sharding import PartitionSpec as P

HEAD_DIM = 32
EPSILON = 1e-06
AXES = ("groups", "frame")


def dot(a, b, dims):
    return lax.dot_general(a, b, (dims, ((), ())), preferred_element_type=jnp.float32)


def gathered_plan(frames_in, qkv_weight):
    tokens = frames_in[0]
    count = tokens.shape[0]
    weights = lax.all_gather(qkv_weight, "frame", axis=2, tiled=True)
    projected = jnp.einsum("td,sdc->stc", tokens, weights, preferred_element_type=jnp.float32)
    heads = weights.shape[2] // HEAD_DIM
    split = lambda a: a.reshape(count, heads, HEAD_DIM)
    queries = split(jax.nn.relu(projected[0]))
    keys = split(jax.nn.relu(projected[1].astype(jnp.bfloat16)))
    values = split(projected[2].astype(jnp.bfloat16))
    state = jnp.einsum("thi,thj->hij", keys, values, preferred_element_type=jnp.float32)
    key_sum = jnp.sum(keys.astype(jnp.float32), axis=0)
    both = jnp.concatenate([state, key_sum[:, :, None]], axis=2)
    everyone = lax.all_gather(both.reshape(heads, -1), "frame")
    upto = jnp.arange(everyone.shape[0]) <= lax.axis_index("frame")
    total = jnp.sum(jnp.where(upto[:, None, None], everyone, 0.0), axis=0).reshape(both.shape)
    result = jnp.einsum("thi,hij->thj", queries, total, precision=lax.Precision.HIGHEST)
    attended = result[..., :HEAD_DIM] / (result[..., HEAD_DIM:] + EPSILON)
    return attended.astype(jnp.bfloat16).reshape(1, count, -1)


class Layout:
    def __init__(self, mesh):
        self.frames = mesh.shape["frame"]
        self.lows = 2
        self.highs = self.frames // 4

    def pairs(self, target, source=lambda g, hi, b, lo: True):
        out = []
        for g in range(2):
            for hi in range(self.highs):
                for b in range(2):
                    for lo in range(self.lows):
                        if source(g, hi, b, lo):
                            to = target(g, hi, b, lo)
                            out.append((self.place(g, hi, b, lo), self.place(*to)))
        return out

    def place(self, g, hi, b, lo):
        return ((g * self.highs + hi) * 2 + b) * self.lows + lo


def send(a, pairs):
    return lax.ppermute(a, AXES, pairs)


def shared_plan(layout, frames_in, qkv_weight):
    g = lax.axis_index("groups")
    place = lax.axis_index("frame")
    lo, b, hi = place % 2, (place // 2) % 2, place // 4
    weights = qkv_weight.transpose(0, 2, 1)
    width, depth = weights.shape[1:]
    half = HEAD_DIM // 2
    own = frames_in[0].T
    count = own.shape[1]

    keeper = lambda g, hi, b, lo: lo == g
    other = lambda g, hi, b, lo: lo != g
    along = lambda k: lambda g, hi, b, lo: (g, hi ^ k, b, lo)
    over_b = layout.pairs(lambda g, hi, b, lo: (g, hi, 1 - b, lo))
    over_g = layout.pairs(lambda g, hi, b, lo: (1 - g, hi, b, lo))
    over_gb = layout.pairs(lambda g, hi, b, lo: (1 - g, hi, 1 - b, lo))
    swap = lambda g, hi, b, lo: (g, hi, b, 1 - lo)
    over_lo = layout.pairs(swap)

    extra = lax.dynamic_slice_in_dim(weights[:2], g * (width - half), half, axis=1)
    mains, extras = [weights], [extra]
    for got, kind in ((mains, keeper), (extras, other)):
        far = send(got[0], layout.pairs(along(2), kind))
        near = send(got[0], layout.pairs(along(1), kind))
        got.extend([near, far, send(far, layout.pairs(along(1), kind))])
    mine = lo == g
    mains = [jnp.where(mine, a, send(a, layout.pairs(swap, keeper))) for a in mains]
    extras = [jnp.where(mine, send(a, layout.pairs(swap, other)), a) for a in extras]

    next_b = send(own, over_b)
    next_g = send(own, over_g)
    cut = depth // 2
    across = jnp.concatenate([send(next_b[:cut], over_g), send(next_g[cut:], over_b)], axis=0)
    tokens = [own, next_b, next_g, across]

    rows = jnp.arange(width + half)
    key_head = (4 * half * g + (rows + half * g) % (width + half)) // HEAD_DIM
    value_head = (width * g + jnp.arange(width)) // HEAD_DIM
    same = value_head[:, None] == key_head[None, :]

    def project(k, m):
        main = dot(mains[k].reshape(3 * width, depth), tokens[m], ((1,), (0,)))
        more = dot(extras[k].reshape(2 * half, depth), tokens[m], ((1,), (0,)))
        queries = jnp.concatenate([main[:width], more[:half]], axis=0)
        keys = jnp.concatenate([main[width : 2 * width], more[half:]], axis=0)
        return (
            jax.nn.relu(queries).astype(jnp.bfloat16),
            jax.nn.relu(keys).astype(jnp.bfloat16),
            main[2 * width :].astype(jnp.bfloat16),
        )

    queries = [[None] * 4 for _ in range(4)]
    states, key_sums = [], []
    for m in range(4):
        frame_states, frame_keys = [], []
        for k in range(4):
            queries[m][k], keys, values = project(k, m)
            full = dot(values, keys, ((1,), (1,)))
            full = jnp.where(same, full, 0.0)
            frame_states.append(full[:, :32] + full[:, 32:64] + full[:, 64:])
            frame_keys.append(jnp.sum(keys.astype(jnp.float32), axis=1))
        states.append(jnp.concatenate(frame_states, axis=1))
        key_sums.append(jnp.concatenate([jnp.pad(jnp.stack(frame_keys), ((0, 4), (0, 32)))], axis=1))
    mine_all = jnp.stack([jnp.concatenate([s, t], axis=0) for s, t in zip(states, key_sums)])
    other_all = send(mine_all, over_lo)
    both = mine_all + other_all
    plane = jnp.stack([both[0] + both[1], both[2] + both[3]])
    before = jnp.zeros_like(plane)
    for k in (1, 2, 3):
        got = send(plane, layout.pairs(along(k)))
        lanes = [got[:, :width, 32 * (j ^ k) : 32 * (j ^ k) + 32] for j in range(4)]
        sums = [got[:, width + (j ^ k)][:, None] for j in range(4)] + [got[:, width + 4 :]]
        got = jnp.concatenate([jnp.concatenate(lanes, axis=2)] + sums, axis=1)
        before = before + jnp.where((hi ^ k) < hi, got, 0.0)

    outs = []
    for m in range(4):
        this_b = b ^ (m & 1)
        upto = before[m // 2] + mine_all[m]
        upto = upto + jnp.where(lo == 1, other_all[m], 0.0) + jnp.where(this_b == 1, both[m ^ 1], 0.0)
        blocks = []
        for k in range(4):
            part = upto[:width, 32 * k : 32 * k + 32]
            state = jnp.where(same, jnp.concatenate([part] * 3, axis=1), 0.0)
            key_sum = jnp.where(same, upto[width + k, : width + half][None, :], 0.0)
            q = queries[m][k]
            numer = dot(state.astype(jnp.bfloat16), q, ((1,), (0,)))
            denom = dot(key_sum.astype(jnp.bfloat16), q, ((1,), (0,)))
            blocks.append((numer / (denom + EPSILON)).astype(jnp.bfloat16))
        outs.append(jnp.stack(blocks))
    got = [outs[0], send(outs[1], over_b), send(outs[2], over_g), send(outs[3], over_gb)]

    every = jnp.stack(got).reshape(2, 2, 2, 2, width, count)
    for axis, bit in ((0, g), (1, b), (2, hi // 2), (3, hi % 2)):
        every = jnp.where(bit == 1, jnp.flip(every, axis), every)
    return every.transpose(5, 2, 3, 1, 0, 4).reshape(1, count, -1)


def solution(mesh):
    placed = (P(AXES, None, None), P(None, None, "frame"))

    def shards(frames_in, qkv_weight):
        width = qkv_weight.shape[2]
        if mesh.shape["groups"] == 2 and mesh.shape["frame"] == 16 and width * 2 == 5 * HEAD_DIM:
            return shared_plan(Layout(mesh), frames_in, qkv_weight)
        return gathered_plan(frames_in, qkv_weight)

    return jax.shard_map(
        shards, mesh=mesh, in_specs=placed, out_specs=P(AXES, None, None), check_vma=False
    )
```

time: 199 us -> 135 us (0.68)
  the two profiles are of different devices: /device:TPU:29 before, /device:TPU:0 now
where the time goes in v1:
time: 135 us
  waiting for transfers between devices  62.2 us (46%)
  starting transfers between devices  38.9 us (29%)
  matrix products  21.2 us (16%)
  other arithmetic  7.46 us (6%)
  local copies, waits for them, and re-layouts  3.46 us (3%)
  between operations  1.45 us (1%)
    ppermute x25, waiting for transfers between devices, send(): return lax.ppermute(a, AXES, pairs)  62.2 us
    ppermute x25, starting transfers between devices, send(): return lax.ppermute(a, AXES, pairs)  38.9 us
    dot_general x80, matrix products, dot(): lax.dot_general(a, b, (dims, ((), ())), preferred_element_type=jnp.float32)  21.2 us
    select_n x4, other arithmetic, shared_plan(): jnp.where(mine, a, send(a, layout.pairs(swap, keeper)))  3.03 us
  transfers between devices with their start and end apart: 25, of which 14 were waited for; matrix products, arithmetic and copies ran while one was open for 18% of the time, Pallas kernels for 0%

profile of v1, /device:TPU:0, one launch (start us, length us, event | category | flops | bytes accessed | tf_op | source)
XLA Modules:
  0.0 134.7 jit_solution(16422981666525532041)
XLA Ops:
  0.0 6.1 %collective-permute-start.6 = (bf16[3,80,2240]{2,1,0:T(8,128)(2,1)}, bf16[3,80,2240]{2,1,0:T(8,128)(2,1)}, u32[]{:S(2)}, u32[]{:S(2)}) collective-permute-start(bf16[3,80,2240]{2,1,0:T(8,128)(2,1)} %bitcast.256), channel_id=1, source_target_pairs={{0,8},{2,10},{4,12},{6,14},{8,0},{10,2},{12,4},{14,6},{17,25},{19,... | collective-permute-start | bytes 3225608 | tf_op jit(solution)/shard_map/ppermute | solution.py:58
  6.1 1.2 slice.816
  7.3 0.7 collective-permute-start.8
  8.0 1.3 collective-permute-start.4
  9.3 3.5 %collective-permute-start.2 = (bf16[3,80,2240]{2,1,0:T(8,128)(2,1)S(1)}, bf16[3,80,2240]{2,1,0:T(8,128)(2,1)}, u32[]{:S(2)}, u32[]{:S(2)}) collective-permute-start(bf16[3,80,2240]{2,1,0:T(8,128)(2,1)S(1)} %bitcast.258), channel_id=1, source_target_pairs={{0,4},{2,6},{4,0},{6,2},{8,12},{10,14},{12,8},{14,10},{17,21},{19,... | collective-permute-start | bytes 3225608 | tf_op jit(solution)/shard_map/ppermute | solution.py:58
  12.8 1.3 collective-permute-start.1
  14.1 1.9 %collective-permute-done.1 = bf16[2,16,2240]{2,1,0:T(8,128)(2,1)S(1)} collective-permute-done((bf16[2,16,2240]{2,1,0:T(8,128)(2,1)S(1)}, bf16[2,16,2240]{2,1,0:T(8,128)(2,1)S(1)}, u32[]{:S(2)}, u32[]{:S(2)}) %collective-permute-start.1) | collective-permute-done | bytes 143392 | tf_op jit(solution)/shard_map/ppermute | solution.py:58
  16.0 2.1 %collective-permute-start = (bf16[3,80,2240]{2,1,0:T(8,128)(2,1)S(1)}, bf16[3,80,2240]{2,1,0:T(8,128)(2,1)S(1)}, u32[]{:S(2)}, u32[]{:S(2)}) collective-permute-start(bf16[3,80,2240]{2,1,0:T(8,128)(2,1)S(1)} %bitcast.259), channel_id=1, source_target_pairs={{0,1},{2,3},{4,5},{6,7},{8,9},{10,11},{12,13},{14,15},{17,16},{19,... | collective-permute-start | bytes 3225608 | tf_op jit(solution)/shard_map/ppermute | solution.py:58
  18.5 1.3 collective-permute-start.9
  19.9 1.6 %collective-permute-start.14 = (bf16[2240,256]{1,0:T(8,128)(2,1)S(1)}, bf16[2240,256]{1,0:T(8,128)(2,1)S(1)}, u32[]{:S(2)}, u32[]{:S(2)}) collective-permute-start(bf16[2240,256]{1,0:T(8,128)(2,1)S(1)} %bitcast.222), channel_id=1, source_target_pairs={{0,2},{1,3},{2,0},{3,1},{4,6},{5,7},{6,4},{7,5},{8,10},{9,11},{10,... | collective-permute-start | bytes 3440648 | tf_op jit(solution)/shard_map/ppermute | solution.py:58
  21.4 6.9 %collective-permute-done.9 = bf16[2,16,2240]{2,1,0:T(8,128)(2,1)S(1)} collective-permute-done((bf16[2,16,2240]{2,1,0:T(8,128)(2,1)S(1)}, bf16[2,16,2240]{2,1,0:T(8,128)(2,1)S(1)}, u32[]{:S(2)}, u32[]{:S(2)}) %collective-permute-start.9) | collective-permute-done | bytes 143392 | tf_op jit(solution)/shard_map/ppermute | solution.py:58
  28.3 1.3 collective-permute-start.5
  29.9 1.9 %collective-permute-done.5 = bf16[2,16,2240]{2,1,0:T(8,128)(2,1)S(1)} collective-permute-done((bf16[2,16,2240]{2,1,0:T(8,128)(2,1)}, bf16[2,16,2240]{2,1,0:T(8,128)(2,1)S(1)}, u32[]{:S(2)}, u32[]{:S(2)}) %collective-permute-start.5) | collective-permute-done | bytes 143392 | tf_op jit(solution)/shard_map/ppermute | solution.py:58
  31.8 0.7 collective-permute-start.12
  32.8 1.3 collective-permute-start.13
  34.1 7.8 %collective-permute-done.13 = bf16[2,16,2240]{2,1,0:T(8,128)(2,1)S(1)} collective-permute-done((bf16[2,16,2240]{2,1,0:T(8,128)(2,1)S(1)}, bf16[2,16,2240]{2,1,0:T(8,128)(2,1)S(1)}, u32[]{:S(2)}, u32[]{:S(2)}) %collective-permute-start.13) | collective-permute-done | bytes 143392 | tf_op jit(solution)/shard_map/ppermute | solution.py:58
  42.0 1.1 collective-permute-start.15
  43.4 1.9 %collective-permute-start.10 = (bf16[3,80,2240]{2,1,0:T(8,128)(2,1)}, bf16[3,80,2240]{2,1,0:T(8,128)(2,1)S(1)}, u32[]{:S(2)}, u32[]{:S(2)}) collective-permute-start(bf16[3,80,2240]{2,1,0:T(8,128)(2,1)} %collective-permute-done.6), channel_id=1, source_target_pairs={{0,4},{2,6},{4,0},{6,2},{8,12},{10,14},{12,8},{14,10},{17,21},{19,... | collective-permute-start | bytes 3225608 | tf_op jit(solution)/shard_map/ppermute | solution.py:58
  45.4 1.4 %collective-permute-start.7 = (bf16[3,80,2240]{2,1,0:T(8,128)(2,1)}, bf16[3,80,2240]{2,1,0:T(8,128)(2,1)S(1)}, u32[]{:S(2)}, u32[]{:S(2)}) collective-permute-start(bf16[3,80,2240]{2,1,0:T(8,128)(2,1)} %collective-permute-done.6), channel_id=1, source_target_pairs={{0,1},{2,3},{4,5},{6,7},{8,9},{10,11},{12,13},{14,15},{17,16},{19,... | collective-permute-start | bytes 3225608 | tf_op jit(solution)/shard_map/ppermute | solution.py:58
  46.7 1.4 %collective-permute-start.3 = (bf16[3,80,2240]{2,1,0:T(8,128)(2,1)}, bf16[3,80,2240]{2,1,0:T(8,128)(2,1)S(1)}, u32[]{:S(2)}, u32[]{:S(2)}) collective-permute-start(bf16[3,80,2240]{2,1,0:T(8,128)(2,1)} %collective-permute-done.2), channel_id=1, source_target_pairs={{0,1},{2,3},{4,5},{6,7},{8,9},{10,11},{12,13},{14,15},{17,16},{19,... | collective-permute-start | bytes 3225608 | tf_op jit(solution)/shard_map/ppermute | solution.py:58
  48.2 0.5 fusion.14
  49.3 0.3 fusion.492
  49.6 0.3 fusion.498
  50.0 0.3 fusion.496
  50.3 0.5 fusion.491
  50.8 18.5 %collective-permute-done.15 = bf16[2240,256]{1,0:T(8,128)(2,1)S(1)} collective-permute-done((bf16[2240,256]{1,0:T(8,128)(2,1)S(1)}, bf16[2240,256]{1,0:T(8,128)(2,1)S(1)}, u32[]{:S(2)}, u32[]{:S(2)}) %collective-permute-start.15) | collective-permute-done | bytes 1146912 | tf_op jit(solution)/shard_map/ppermute | solution.py:58
  69.6 0.3 fusion.500
  69.9 0.5 fusion.499
  70.5 1.4 %collective-permute-start.16 = (bf16[1120,256]{1,0:T(8,128)(2,1)S(1)}, bf16[1120,256]{1,0:T(8,128)(2,1)S(1)}, u32[]{:S(2)}, u32[]{:S(2)}) collective-permute-start(bf16[1120,256]{1,0:T(8,128)(2,1)S(1)} %slice.887), channel_id=1, source_target_pairs={{0,16},{1,17},{2,18},{3,19},{4,20},{5,21},{6,22},{7,23},{8,24},{9,... | collective-permute-start | bytes 1720328 | tf_op jit(solution)/shard_map/ppermute | solution.py:58
  71.9 1.6 %collective-permute-start.17 = (bf16[1120,256]{1,0:T(8,128)(2,1)S(1)}, bf16[1120,256]{1,0:T(8,128)(2,1)S(1)}, u32[]{:S(2)}, u32[]{:S(2)}) collective-permute-start(bf16[1120,256]{1,0:T(8,128)(2,1)S(1)} %slice.888), channel_id=1, source_target_pairs={{0,2},{1,3},{2,0},{3,1},{4,6},{5,7},{6,4},{7,5},{8,10},{9,11},{10,... | collective-permute-start | bytes 1720328 | tf_op jit(solution)/shard_map/ppermute | solution.py:58
  73.6 0.3 fusion.506
  73.9 0.3 fusion.504
  74.6 10.1 %collective-permute-done.16 = bf16[1120,256]{1,0:T(8,128)(2,1)S(1)} collective-permute-done((bf16[1120,256]{1,0:T(8,128)(2,1)S(1)}, bf16[1120,256]{1,0:T(8,128)(2,1)S(1)}, u32[]{:S(2)}, u32[]{:S(2)}) %collective-permute-start.16) | collective-permute-done | bytes 573472 | tf_op jit(solution)/shard_map/ppermute | solution.py:58
  84.8 1.3 collective-permute-done.17
  86.4 0.5 fusion.507
  87.2 0.3 fusion.512
  88.2 1.4 %broadcast_select_fusion.1 = bf16[3,80,2240]{2,1,0:T(8,128)(2,1)S(1)} fusion(bf16[3,80,2240]{2,1,0:T(8,128)(2,1)} %collective-permute-done.6, bf16[3,80,2240]{2,1,0:T(8,128)(2,1)S(1)} %collective-permute-done.7, pred[]{:T(512)S(6)} %eq.53), kind=kLoop, calls=%fused_computation.97 | loop fusion | flops 537600 | bytes 3225601 | tf_op jit(solution)/shard_map/jit(_where)/select_n | solution.py:87
  89.6 0.5 fusion.6
  90.3 1.4 %broadcast_select_fusion.2 = bf16[3,80,2240]{2,1,0:T(8,128)(2,1)S(1)} fusion(bf16[3,80,2240]{2,1,0:T(8,128)(2,1)} %collective-permute-done.2, bf16[3,80,2240]{2,1,0:T(8,128)(2,1)S(1)} %collective-permute-done.3, pred[]{:T(512)S(6)} %eq.53), kind=kLoop, calls=%fused_computation.98 | loop fusion | flops 537600 | bytes 3225601 | tf_op jit(solution)/shard_map/jit(_where)/select_n | solution.py:87
  91.7 0.5 fusion.10
  92.5 0.5 fusion.509
  93.0 0.5 fusion.511
  93.4 0.5 fusion.493
  93.9 0.5 fusion.495
  94.4 0.5 fusion.501
  94.9 0.5 fusion.503
  96.9 1.5 %collective-permute-start.11 = (bf16[3,80,2240]{2,1,0:T(8,128)(2,1)S(1)}, bf16[3,80,2240]{2,1,0:T(8,128)(2,1)S(1)}, u32[]{:S(2)}, u32[]{:S(2)}) collective-permute-start(bf16[3,80,2240]{2,1,0:T(8,128)(2,1)S(1)} %collective-permute-done.10), channel_id=1, source_target_pairs={{0,1},{2,3},{4,5},{6,7},{8,9},{10,11},{12,13},{14,15},{17,16},{19,... | collective-permute-start | bytes 3225608 | tf_op jit(solution)/shard_map/ppermute | solution.py:58
  99.1 1.5 %collective-permute-done.11 = bf16[3,80,2240]{2,1,0:T(8,128)(2,1)S(1)} collective-permute-done((bf16[3,80,2240]{2,1,0:T(8,128)(2,1)S(1)}, bf16[3,80,2240]{2,1,0:T(8,128)(2,1)S(1)}, u32[]{:S(2)}, u32[]{:S(2)}) %collective-permute-start.11) | collective-permute-done | bytes 1075232 | tf_op jit(solution)/shard_map/ppermute | solution.py:58
  100.7 0.5 fusion.2
  101.4 0.5 fusion.497
  102.2 0.5 fusion.505
  102.9 0.5 fusion.513
  104.7 0.4 collective-permute-start.18
  105.1 1.0 collective-permute-done.18
  106.4 2.5 %collective-permute-start.21 = (f32[2,88,128]{2,1,0:T(8,128)S(1)}, f32[2,88,128]{2,1,0:T(8,128)S(1)}, u32[]{:S(2)}, u32[]{:S(2)}) collective-permute-start(f32[2,88,128]{2,1,0:T(8,128)S(1)} %pad_maximum_fusion.5), channel_id=1, source_target_pairs={{0,12},{1,13},{2,14},{3,15},{4,8},{5,9},{6,10},{7,11},{8,4},{9,5},... | collective-permute-start | bytes 270344 | tf_op jit(solution)/shard_map/ppermute | solution.py:58
  108.9 0.9 collective-permute-start.20
  109.8 1.4 %collective-permute-done.19 = f32[2,88,128]{2,1,0:T(8,128)S(1)} collective-permute-done((f32[2,88,128]{2,1,0:T(8,128)S(1)}, f32[2,88,128]{2,1,0:T(8,128)S(1)}, u32[]{:S(2)}, u32[]{:S(2)}) %collective-permute-start.19) | collective-permute-done | bytes 90144 | tf_op jit(solution)/shard_map/ppermute | solution.py:58
  111.5 2.7 %collective-permute-done.21 = f32[2,88,128]{2,1,0:T(8,128)S(1)} collective-permute-done((f32[2,88,128]{2,1,0:T(8,128)S(1)}, f32[2,88,128]{2,1,0:T(8,128)S(1)}, u32[]{:S(2)}, u32[]{:S(2)}) %collective-permute-start.21) | collective-permute-done | bytes 90144 | tf_op jit(solution)/shard_map/ppermute | solution.py:58
  114.5 3.6 %collective-permute-done.20 = f32[2,88,128]{2,1,0:T(8,128)S(1)} collective-permute-done((f32[2,88,128]{2,1,0:T(8,128)S(1)}, f32[2,88,128]{2,1,0:T(8,128)S(1)}, u32[]{:S(2)}, u32[]{:S(2)}) %collective-permute-start.20) | collective-permute-done | bytes 90144 | tf_op jit(solution)/shard_map/ppermute | solution.py:58
  120.6 1.6 %collective-permute-start.22 = (bf16[4,80,256]{2,1,0:T(8,128)(2,1)S(1)}, bf16[4,80,256]{2,1,0:T(8,128)(2,1)S(1)}, u32[]{:S(2)}, u32[]{:S(2)}) collective-permute-start(bf16[4,80,256]{2,1,0:T(8,128)(2,1)S(1)} %pad_maximum_fusion.2), channel_id=1, source_target_pairs={{0,2},{1,3},{2,0},{3,1},{4,6},{5,7},{6,4},{7,5},{8,10},{9,11},{10,... | collective-permute-start | bytes 491528 | tf_op jit(solution)/shard_map/ppermute | solution.py:58
  125.7 2.0 %collective-permute-start.24 = (bf16[4,80,256]{2,1,0:T(8,128)(2,1)S(1)}, bf16[4,80,256]{2,1,0:T(8,128)(2,1)S(1)}, u32[]{:S(2)}, u32[]{:S(2)}) collective-permute-start(bf16[4,80,256]{2,1,0:T(8,128)(2,1)S(1)} %pad_maximum_fusion.4), channel_id=1, source_target_pairs={{0,18},{1,19},{2,16},{3,17},{4,22},{5,23},{6,20},{7,21},{8,26},{9,... | collective-permute-start | bytes 491528 | tf_op jit(solution)/shard_map/ppermute | solution.py:58
  129.4 1.7 %collective-permute-done.23 = bf16[4,80,256]{2,1,0:T(8,128)(2,1)S(1)} collective-permute-done((bf16[4,80,256]{2,1,0:T(8,128)(2,1)S(1)}, bf16[4,80,256]{2,1,0:T(8,128)(2,1)S(1)}, u32[]{:S(2)}, u32[]{:S(2)}) %collective-permute-start.23) | collective-permute-done | bytes 163872 | tf_op jit(solution)/shard_map/ppermute | solution.py:58
  131.1 1.9 %collective-permute-done.24 = bf16[4,80,256]{2,1,0:T(8,128)(2,1)S(1)} collective-permute-done((bf16[4,80,256]{2,1,0:T(8,128)(2,1)S(1)}, bf16[4,80,256]{2,1,0:T(8,128)(2,1)S(1)}, u32[]{:S(2)}, u32[]{:S(2)}) %collective-permute-start.24) | collective-permute-done | bytes 163872 | tf_op jit(solution)/shard_map/ppermute | solution.py:58
  133.6 1.1 copy.6
  (188 shorter events, 17.7 us)
Async XLA Ops:
  0.0 9.3 %copy-start.1 = (bf16[3,2240,80]{1,2,0:T(8,128)(2,1)S(1)}, bf16[3,2240,80]{1,2,0:T(8,128)(2,1)}, u32[]{:S(2)}) copy-start(bf16[3,2240,80]{1,2,0:T(8,128)(2,1)} %param.3) | copy-start | bytes 3225604
  0.0 18.2 %copy-start = (bf16[1,256,2240]{1,2,0:T(8,128)(2,1)S(1)}, bf16[1,256,2240]{1,2,0:T(8,128)(2,1)}, u32[]{:S(2)}) copy-start(bf16[1,256,2240]{1,2,0:T(8,128)(2,1)} %param.2) | copy-start | bytes 3440644
  0.0 43.4 %collective-permute-start.6 = (bf16[3,80,2240]{2,1,0:T(8,128)(2,1)}, bf16[3,80,2240]{2,1,0:T(8,128)(2,1)}, u32[]{:S(2)}, u32[]{:S(2)}) collective-permute-start(bf16[3,80,2240]{2,1,0:T(8,128)(2,1)} %bitcast.256), channel_id=1, source_target_pairs={{0,8},{2,10},{4,12},{6,14},{8,0},{10,2},{12,4},{14,6},{17,25},{19,... | collective-permute-start | bytes 3225608 | tf_op jit(solution)/shard_map/ppermute | solution.py:58
  7.3 11.2 %collective-permute-start.8 = (bf16[2,16,2240]{2,1,0:T(8,128)(2,1)S(1)}, bf16[2,16,2240]{2,1,0:T(8,128)(2,1)S(1)}, u32[]{:S(2)}, u32[]{:S(2)}) collective-permute-start(bf16[2,16,2240]{2,1,0:T(8,128)(2,1)S(1)} %constant_dynamic-slice_fusion), channel_id=1, source_target_pairs={{1,9},{3,11},{5,13},{7,15},{9,1},{11,3},{13,5},{15,7},{16,24},{18,... | collective-permute-start | bytes 430088 | tf_op jit(solution)/shard_map/ppermute | solution.py:58
  8.0 11.9 %collective-permute-start.4 = (bf16[2,16,2240]{2,1,0:T(8,128)(2,1)S(1)}, bf16[2,16,2240]{2,1,0:T(8,128)(2,1)}, u32[]{:S(2)}, u32[]{:S(2)}) collective-permute-start(bf16[2,16,2240]{2,1,0:T(8,128)(2,1)S(1)} %constant_dynamic-slice_fusion), channel_id=1, source_target_pairs={{1,5},{3,7},{5,1},{7,3},{9,13},{11,15},{13,9},{15,11},{16,20},{18,... | collective-permute-start | bytes 430088 | tf_op jit(solution)/shard_map/ppermute | solution.py:58
  9.3 36.1 %collective-permute-start.2 = (bf16[3,80,2240]{2,1,0:T(8,128)(2,1)S(1)}, bf16[3,80,2240]{2,1,0:T(8,128)(2,1)}, u32[]{:S(2)}, u32[]{:S(2)}) collective-permute-start(bf16[3,80,2240]{2,1,0:T(8,128)(2,1)S(1)} %bitcast.258), channel_id=1, source_target_pairs={{0,4},{2,6},{4,0},{6,2},{8,12},{10,14},{12,8},{14,10},{17,21},{19,... | collective-permute-start | bytes 3225608 | tf_op jit(solution)/shard_map/ppermute | solution.py:58
  12.8 3.3 %collective-permute-start.1 = (bf16[2,16,2240]{2,1,0:T(8,128)(2,1)S(1)}, bf16[2,16,2240]{2,1,0:T(8,128)(2,1)S(1)}, u32[]{:S(2)}, u32[]{:S(2)}) collective-permute-start(bf16[2,16,2240]{2,1,0:T(8,128)(2,1)S(1)} %constant_dynamic-slice_fusion), channel_id=1, source_target_pairs={{1,0},{3,2},{5,4},{7,6},{9,8},{11,10},{13,12},{15,14},{16,17},{18,... | collective-permute-start | bytes 430088 | tf_op jit(solution)/shard_map/ppermute | solution.py:58
  16.0 30.7 %collective-permute-start = (bf16[3,80,2240]{2,1,0:T(8,128)(2,1)S(1)}, bf16[3,80,2240]{2,1,0:T(8,128)(2,1)S(1)}, u32[]{:S(2)}, u32[]{:S(2)}) collective-permute-start(bf16[3,80,2240]{2,1,0:T(8,128)(2,1)S(1)} %bitcast.259), channel_id=1, source_target_pairs={{0,1},{2,3},{4,5},{6,7},{8,9},{10,11},{12,13},{14,15},{17,16},{19,... | collective-permute-start | bytes 3225608 | tf_op jit(solution)/shard_map/ppermute | solution.py:58
  18.5 9.8 %collective-permute-start.9 = (bf16[2,16,2240]{2,1,0:T(8,128)(2,1)S(1)}, bf16[2,16,2240]{2,1,0:T(8,128)(2,1)S(1)}, u32[]{:S(2)}, u32[]{:S(2)}) collective-permute-start(bf16[2,16,2240]{2,1,0:T(8,128)(2,1)S(1)} %collective-permute-done.8), channel_id=1, source_target_pairs={{1,0},{3,2},{5,4},{7,6},{9,8},{11,10},{13,12},{15,14},{16,17},{18,... | collective-permute-start | bytes 430088 | tf_op jit(solution)/shard_map/ppermute | solution.py:58
  19.9 29.1 %collective-permute-start.14 = (bf16[2240,256]{1,0:T(8,128)(2,1)S(1)}, bf16[2240,256]{1,0:T(8,128)(2,1)S(1)}, u32[]{:S(2)}, u32[]{:S(2)}) collective-permute-start(bf16[2240,256]{1,0:T(8,128)(2,1)S(1)} %bitcast.222), channel_id=1, source_target_pairs={{0,2},{1,3},{2,0},{3,1},{4,6},{5,7},{6,4},{7,5},{8,10},{9,11},{10,... | collective-permute-start | bytes 3440648 | tf_op jit(solution)/shard_map/ppermute | solution.py:58
  28.3 3.5 %collective-permute-start.5 = (bf16[2,16,2240]{2,1,0:T(8,128)(2,1)}, bf16[2,16,2240]{2,1,0:T(8,128)(2,1)S(1)}, u32[]{:S(2)}, u32[]{:S(2)}) collective-permute-start(bf16[2,16,2240]{2,1,0:T(8,128)(2,1)} %collective-permute-done.4), channel_id=1, source_target_pairs={{1,0},{3,2},{5,4},{7,6},{9,8},{11,10},{13,12},{15,14},{16,17},{18,... | collective-permute-start | bytes 430088 | tf_op jit(solution)/shard_map/ppermute | solution.py:58
  31.8 1.0 collective-permute-start.12
  32.8 9.2 %collective-permute-start.13 = (bf16[2,16,2240]{2,1,0:T(8,128)(2,1)S(1)}, bf16[2,16,2240]{2,1,0:T(8,128)(2,1)S(1)}, u32[]{:S(2)}, u32[]{:S(2)}) collective-permute-start(bf16[2,16,2240]{2,1,0:T(8,128)(2,1)S(1)} %collective-permute-done.12), channel_id=1, source_target_pairs={{1,0},{3,2},{5,4},{7,6},{9,8},{11,10},{13,12},{15,14},{16,17},{18,... | collective-permute-start | bytes 430088 | tf_op jit(solution)/shard_map/ppermute | solution.py:58
  42.0 27.3 %collective-permute-start.15 = (bf16[2240,256]{1,0:T(8,128)(2,1)S(1)}, bf16[2240,256]{1,0:T(8,128)(2,1)S(1)}, u32[]{:S(2)}, u32[]{:S(2)}) collective-permute-start(bf16[2240,256]{1,0:T(8,128)(2,1)S(1)} %bitcast.223), channel_id=1, source_target_pairs={{0,16},{1,17},{2,18},{3,19},{4,20},{5,21},{6,22},{7,23},{8,24},{9,... | collective-permute-start | bytes 3440648 | tf_op jit(solution)/shard_map/ppermute | solution.py:58
  43.4 53.5 %collective-permute-start.10 = (bf16[3,80,2240]{2,1,0:T(8,128)(2,1)}, bf16[3,80,2240]{2,1,0:T(8,128)(2,1)S(1)}, u32[]{:S(2)}, u32[]{:S(2)}) collective-permute-start(bf16[3,80,2240]{2,1,0:T(8,128)(2,1)} %collective-permute-done.6), channel_id=1, source_target_pairs={{0,4},{2,6},{4,0},{6,2},{8,12},{10,14},{12,8},{14,10},{17,21},{19,... | collective-permute-start | bytes 3225608 | tf_op jit(solution)/shard_map/ppermute | solution.py:58
  45.4 42.8 %collective-permute-start.7 = (bf16[3,80,2240]{2,1,0:T(8,128)(2,1)}, bf16[3,80,2240]{2,1,0:T(8,128)(2,1)S(1)}, u32[]{:S(2)}, u32[]{:S(2)}) collective-permute-start(bf16[3,80,2240]{2,1,0:T(8,128)(2,1)} %collective-permute-done.6), channel_id=1, source_target_pairs={{0,1},{2,3},{4,5},{6,7},{8,9},{10,11},{12,13},{14,15},{17,16},{19,... | collective-permute-start | bytes 3225608 | tf_op jit(solution)/shard_map/ppermute | solution.py:58
  46.7 43.6 %collective-permute-start.3 = (bf16[3,80,2240]{2,1,0:T(8,128)(2,1)}, bf16[3,80,2240]{2,1,0:T(8,128)(2,1)S(1)}, u32[]{:S(2)}, u32[]{:S(2)}) collective-permute-start(bf16[3,80,2240]{2,1,0:T(8,128)(2,1)} %collective-permute-done.2), channel_id=1, source_target_pairs={{0,1},{2,3},{4,5},{6,7},{8,9},{10,11},{12,13},{14,15},{17,16},{19,... | collective-permute-start | bytes 3225608 | tf_op jit(solution)/shard_map/ppermute | solution.py:58
  70.5 14.3 %collective-permute-start.16 = (bf16[1120,256]{1,0:T(8,128)(2,1)S(1)}, bf16[1120,256]{1,0:T(8,128)(2,1)S(1)}, u32[]{:S(2)}, u32[]{:S(2)}) collective-permute-start(bf16[1120,256]{1,0:T(8,128)(2,1)S(1)} %slice.887), channel_id=1, source_target_pairs={{0,16},{1,17},{2,18},{3,19},{4,20},{5,21},{6,22},{7,23},{8,24},{9,... | collective-permute-start | bytes 1720328 | tf_op jit(solution)/shard_map/ppermute | solution.py:58
  71.9 14.2 %collective-permute-start.17 = (bf16[1120,256]{1,0:T(8,128)(2,1)S(1)}, bf16[1120,256]{1,0:T(8,128)(2,1)S(1)}, u32[]{:S(2)}, u32[]{:S(2)}) collective-permute-start(bf16[1120,256]{1,0:T(8,128)(2,1)S(1)} %slice.888), channel_id=1, source_target_pairs={{0,2},{1,3},{2,0},{3,1},{4,6},{5,7},{6,4},{7,5},{8,10},{9,11},{10,... | collective-permute-start | bytes 1720328 | tf_op jit(solution)/shard_map/ppermute | solution.py:58
  96.9 3.6 %collective-permute-start.11 = (bf16[3,80,2240]{2,1,0:T(8,128)(2,1)S(1)}, bf16[3,80,2240]{2,1,0:T(8,128)(2,1)S(1)}, u32[]{:S(2)}, u32[]{:S(2)}) collective-permute-start(bf16[3,80,2240]{2,1,0:T(8,128)(2,1)S(1)} %collective-permute-done.10), channel_id=1, source_target_pairs={{0,1},{2,3},{4,5},{6,7},{8,9},{10,11},{12,13},{14,15},{17,16},{19,... | collective-permute-start | bytes 3225608 | tf_op jit(solution)/shard_map/ppermute | solution.py:58
  104.7 1.5 %collective-permute-start.18 = (f32[4,88,128]{2,1,0:T(8,128)S(1)}, f32[4,88,128]{2,1,0:T(8,128)S(1)}, u32[]{:S(2)}, u32[]{:S(2)}) collective-permute-start(f32[4,88,128]{2,1,0:T(8,128)S(1)} %pad_maximum_fusion.1), channel_id=1, source_target_pairs={{0,1},{1,0},{2,3},{3,2},{4,5},{5,4},{6,7},{7,6},{8,9},{9,8},{10,11... | collective-permute-start | bytes 540680 | tf_op jit(solution)/shard_map/ppermute | solution.py:58
  106.2 5.0 %collective-permute-start.19 = (f32[2,88,128]{2,1,0:T(8,128)S(1)}, f32[2,88,128]{2,1,0:T(8,128)S(1)}, u32[]{:S(2)}, u32[]{:S(2)}) collective-permute-start(f32[2,88,128]{2,1,0:T(8,128)S(1)} %pad_maximum_fusion.5), channel_id=1, source_target_pairs={{0,4},{1,5},{2,6},{3,7},{4,0},{5,1},{6,2},{7,3},{8,12},{9,13},{10,... | collective-permute-start | bytes 270344 | tf_op jit(solution)/shard_map/ppermute | solution.py:58
  106.4 7.8 %collective-permute-start.21 = (f32[2,88,128]{2,1,0:T(8,128)S(1)}, f32[2,88,128]{2,1,0:T(8,128)S(1)}, u32[]{:S(2)}, u32[]{:S(2)}) collective-permute-start(f32[2,88,128]{2,1,0:T(8,128)S(1)} %pad_maximum_fusion.5), channel_id=1, source_target_pairs={{0,12},{1,13},{2,14},{3,15},{4,8},{5,9},{6,10},{7,11},{8,4},{9,5},... | collective-permute-start | bytes 270344 | tf_op jit(solution)/shard_map/ppermute | solution.py:58
  108.9 9.3 %collective-permute-start.20 = (f32[2,88,128]{2,1,0:T(8,128)S(1)}, f32[2,88,128]{2,1,0:T(8,128)S(1)}, u32[]{:S(2)}, u32[]{:S(2)}) collective-permute-start(f32[2,88,128]{2,1,0:T(8,128)S(1)} %pad_maximum_fusion.5), channel_id=1, source_target_pairs={{0,8},{1,9},{2,10},{3,11},{4,12},{5,13},{6,14},{7,15},{8,0},{9,1},... | collective-permute-start | bytes 270344 | tf_op jit(solution)/shard_map/ppermute | solution.py:58
  120.6 8.8 %collective-permute-start.22 = (bf16[4,80,256]{2,1,0:T(8,128)(2,1)S(1)}, bf16[4,80,256]{2,1,0:T(8,128)(2,1)S(1)}, u32[]{:S(2)}, u32[]{:S(2)}) collective-permute-start(bf16[4,80,256]{2,1,0:T(8,128)(2,1)S(1)} %pad_maximum_fusion.2), channel_id=1, source_target_pairs={{0,2},{1,3},{2,0},{3,1},{4,6},{5,7},{6,4},{7,5},{8,10},{9,11},{10,... | collective-permute-start | bytes 491528 | tf_op jit(solution)/shard_map/ppermute | solution.py:58
  123.9 7.2 %collective-permute-start.23 = (bf16[4,80,256]{2,1,0:T(8,128)(2,1)S(1)}, bf16[4,80,256]{2,1,0:T(8,128)(2,1)S(1)}, u32[]{:S(2)}, u32[]{:S(2)}) collective-permute-start(bf16[4,80,256]{2,1,0:T(8,128)(2,1)S(1)} %pad_maximum_fusion.3), channel_id=1, source_target_pairs={{0,16},{1,17},{2,18},{3,19},{4,20},{5,21},{6,22},{7,23},{8,24},{9,... | collective-permute-start | bytes 491528 | tf_op jit(solution)/shard_map/ppermute | solution.py:58
  125.7 7.3 %collective-permute-start.24 = (bf16[4,80,256]{2,1,0:T(8,128)(2,1)S(1)}, bf16[4,80,256]{2,1,0:T(8,128)(2,1)S(1)}, u32[]{:S(2)}, u32[]{:S(2)}) collective-permute-start(bf16[4,80,256]{2,1,0:T(8,128)(2,1)S(1)} %pad_maximum_fusion.4), channel_id=1, source_target_pairs={{0,18},{1,19},{2,16},{3,17},{4,22},{5,23},{6,20},{7,21},{8,26},{9,... | collective-permute-start | bytes 491528 | tf_op jit(solution)/shard_map/ppermute | solution.py:58

commit v2 on v1

v2 whole, which is shorter than its diff:
```python
import jax
import jax.numpy as jnp
from jax import lax
from jax.experimental import pallas as pl
from jax.experimental.pallas import tpu as pltpu
from jax.sharding import PartitionSpec as P

HEAD_DIM = 32
EPSILON = 1e-06
AXES = ("groups", "frame")


def dot(a, b, dims):
    return lax.dot_general(a, b, (dims, ((), ())), preferred_element_type=jnp.float32)


def gathered_plan(frames_in, qkv_weight):
    tokens = frames_in[0]
    count = tokens.shape[0]
    weights = lax.all_gather(qkv_weight, "frame", axis=2, tiled=True)
    projected = jnp.einsum("td,sdc->stc", tokens, weights, preferred_element_type=jnp.float32)
    heads = weights.shape[2] // HEAD_DIM
    split = lambda a: a.reshape(count, heads, HEAD_DIM)
    queries = split(jax.nn.relu(projected[0]))
    keys = split(jax.nn.relu(projected[1].astype(jnp.bfloat16)))
    values = split(projected[2].astype(jnp.bfloat16))
    state = jnp.einsum("thi,thj->hij", keys, values, preferred_element_type=jnp.float32)
    key_sum = jnp.sum(keys.astype(jnp.float32), axis=0)
    both = jnp.concatenate([state, key_sum[:, :, None]], axis=2)
    everyone = lax.all_gather(both.reshape(heads, -1), "frame")
    upto = jnp.arange(everyone.shape[0]) <= lax.axis_index("frame")
    total = jnp.sum(jnp.where(upto[:, None, None], everyone, 0.0), axis=0).reshape(both.shape)
    result = jnp.einsum("thi,hij->thj", queries, total, precision=lax.Precision.HIGHEST)
    attended = result[..., :HEAD_DIM] / (result[..., HEAD_DIM:] + EPSILON)
    return attended.astype(jnp.bfloat16).reshape(1, count, -1)


class Layout:
    def __init__(self, mesh):
        self.frames = mesh.shape["frame"]
        self.lows = 2
        self.highs = self.frames // 4

    def pairs(self, target, source=lambda g, hi, b, lo: True):
        out = []
        for g in range(2):
            for hi in range(self.highs):
                for b in range(2):
                    for lo in range(self.lows):
                        if source(g, hi, b, lo):
                            to = target(g, hi, b, lo)
                            out.append((self.place(g, hi, b, lo), self.place(*to)))
        return out

    def place(self, g, hi, b, lo):
        return ((g * self.highs + hi) * 2 + b) * self.lows + lo


def send(a, pairs):
    return lax.ppermute(a, AXES, pairs)


ANY = pl.BlockSpec(memory_space=pl.ANY)
VMEM = pl.BlockSpec(memory_space=pltpu.VMEM)
SMEM = pl.BlockSpec(memory_space=pltpu.SMEM)
LIGHT = pl.CostEstimate(flops=1000, bytes_accessed=1000, transcendentals=0)


def call(body, out, ins, scratch, *operands):
    return pl.pallas_call(
        body,
        out_shape=out,
        in_specs=ins,
        out_specs=jax.tree.map(lambda _: VMEM, out),
        scratch_shapes=scratch,
        compiler_params=pltpu.CompilerParams(vmem_limit_bytes=48 * 2**20),
        cost_estimate=LIGHT,
    )(*operands)


def heads_of(g, width, half):
    shape = (width, width + half)
    row = lax.broadcasted_iota(jnp.int32, shape, 0)
    column = lax.broadcasted_iota(jnp.int32, shape, 1)
    turned = column + half * g
    turned = jnp.where(turned >= width + half, turned - (width + half), turned)
    return (width * g + row) // HEAD_DIM == (4 * half * g + turned) // HEAD_DIM


def project(place, weights, frames, ks, carried=None):
    main_rows, depth = weights[0][0].shape
    extra_rows = weights[0][2].shape[0]
    width, half = main_rows // 3, extra_rows // 2
    count = frames[0][0].shape[1]
    nk, nm, parts = len(weights), len(frames), [len(f) for f in frames]
    carried = carried or []

    def body(place_ref, *refs):
        refs = list(refs)
        w_refs = [[refs.pop(0) for _ in range(4)] for _ in range(nk)]
        x_refs = [[refs.pop(0) for _ in range(n)] for n in parts]
        c_refs = [refs.pop(0) for _ in carried]
        q_ref, s_ref, w_all, x_all, w_sem, x_sem = refs
        g, lo = place_ref[0], place_ref[3]
        mine = lo == g

        def copies(k, own):
            main, extra = (w_refs[k][0], w_refs[k][3]) if own else (w_refs[k][1], w_refs[k][2])
            return (
                pltpu.make_async_copy(main, w_all.at[k, :main_rows], w_sem.at[k, 0]),
                pltpu.make_async_copy(extra, w_all.at[k, main_rows:], w_sem.at[k, 1]),
            )

        def frame(m):
            size = depth // parts[m]
            return [
                pltpu.make_async_copy(x, x_all.at[m, size * i : size * (i + 1)], x_sem.at[m, i])
                for i, x in enumerate(x_refs[m])
            ]

        def start_weights(k):
            @pl.when(mine)
            def _():
                for c in copies(k, True):
                    c.start()

            @pl.when(jnp.logical_not(mine))
            def _():
                for c in copies(k, False):
                    c.start()

        start_weights(0)
        for m in range(nm):
            for c in frame(m):
                c.start()
        for k in range(1, nk):
            start_weights(k)
        same = heads_of(g, width, half)
        s_ref[...] = jnp.zeros_like(s_ref)
        done = 0
        for c_ref in c_refs:
            s_ref[done : done + c_ref.shape[0]] = c_ref[...]
            done += c_ref.shape[0]
        ones = jnp.ones((8, count), jnp.bfloat16)
        for k in range(nk):
            for c in copies(k, True):
                c.wait()
            at = 32 * ks[k]

            def one(m, _):
                made = dot(w_all[k], x_all[m], ((1,), (0,)))
                q_ref[m, k, :width] = jnp.maximum(made[:width], 0.0)
                q_ref[m, k, width:] = jnp.maximum(made[3 * width : 3 * width + half], 0.0)
                keys = jnp.concatenate([made[width : 2 * width], made[3 * width + half :]], axis=0)
                keys = jnp.maximum(keys, 0.0).astype(jnp.bfloat16)
                values = made[2 * width : 3 * width].astype(jnp.bfloat16)
                full = jnp.where(same, dot(values, keys, ((1,), (1,))), 0.0)
                s_ref[m, :width, at : at + 32] = full[:, :32] + full[:, 32:64] + full[:, 64:]
                s_ref[m, width + ks[k] : width + ks[k] + 1, : width + half] = dot(ones, keys, ((1,), (1,)))[:1]
                return 0

            if k == 0:
                for m in range(nm):
                    for c in frame(m):
                        c.wait()
            lax.fori_loop(0, nm, one, 0)

    out = (
        jax.ShapeDtypeStruct((nm, nk, width + half, count), jnp.float32),
        jax.ShapeDtypeStruct((nm, width + 8, 128), jnp.float32),
    )
    scratch = [
        pltpu.VMEM((nk, main_rows + extra_rows, depth), jnp.bfloat16),
        pltpu.VMEM((nm, depth, count), jnp.bfloat16),
        pltpu.SemaphoreType.DMA((nk, 2)),
        pltpu.SemaphoreType.DMA((nm, 2)),
    ]
    flat = [a for w in weights for a in w] + [a for f in frames for a in f]
    ins = [SMEM] + [ANY] * len(flat) + [VMEM] * len(carried)
    return call(body, out, ins, scratch, place, *flat, *carried)


def plane_sum(mine, others):
    def body(a_ref, b_ref, out_ref):
        both = a_ref[...] + b_ref[...]
        out_ref[0] = both[0] + both[1]
        out_ref[1] = both[2] + both[3]

    out = jax.ShapeDtypeStruct((2,) + mine.shape[1:], jnp.float32)
    return call(body, out, [VMEM] * 2, [], mine, others)


def apply(place, ms, queries, mine, others, planes):
    arrays = []
    for row in queries:
        for a, _, _ in row:
            if not any(a is b for b in arrays):
                arrays.append(a)
    where = [[([a is b for b in arrays].index(True), m, k) for a, m, k in row] for row in queries]
    rows, count = arrays[0].shape[2:]
    width = mine.shape[1] - 8
    half = rows - width

    def body(place_ref, *refs):
        q_refs = refs[: len(arrays)]
        mine_ref, others_ref, *plane_refs = refs[len(arrays) : len(arrays) + 5]
        outs = refs[len(arrays) + 5 :]
        g, hi, b, lo = (place_ref[i] for i in range(4))
        same = heads_of(g, width, half)
        factor = lambda yes: jnp.where(yes, 1.0, 0.0).astype(jnp.float32)
        earlier = [factor(jnp.bitwise_xor(hi, k) < hi) for k in (1, 2, 3)]
        second = factor(lo == 1)

        def split(a):
            high = a.astype(jnp.bfloat16)
            return high, (a - high.astype(jnp.float32)).astype(jnp.bfloat16)

        for out_ref, m in zip(outs, ms):
            after = factor(jnp.bitwise_xor(b, m & 1) == 1)
            upto = mine_ref[m] + second * others_ref[m] + after * (mine_ref[m ^ 1] + others_ref[m ^ 1])
            for j in range(4):
                part = upto[:width, 32 * j : 32 * j + 32]
                sums = upto[width + j : width + j + 1, :rows]
                for k in (1, 2, 3):
                    i = j ^ k
                    part += earlier[k - 1] * plane_refs[k - 1][m // 2, :width, 32 * i : 32 * i + 32]
                    sums += earlier[k - 1] * plane_refs[k - 1][m // 2, width + i : width + i + 1, :rows]
                state = jnp.where(same, jnp.concatenate([part] * 3, axis=1), 0.0)
                sums = jnp.where(same, jnp.broadcast_to(sums, (width, rows)), 0.0)
                left, left_low = split(jnp.concatenate([state, sums], axis=0))
                a, qm, qk = where[m][j]
                q, q_low = split(q_refs[a][qm, qk])
                both = dot(left, q, ((1,), (0,))) + dot(left_low, q, ((1,), (0,))) + dot(left, q_low, ((1,), (0,)))
                out_ref[j] = (both[:width] / (both[width:] + EPSILON)).astype(jnp.bfloat16)

    out = [jax.ShapeDtypeStruct((4, width, count), jnp.bfloat16)] * len(ms)
    ins = [SMEM] + [VMEM] * (len(arrays) + 5)
    return call(body, out, ins, [], place, *arrays, mine, others, *planes)


def assemble(place, got):
    blocks, width, count = got[0].shape

    def body(place_ref, *refs):
        *got_refs, out_ref, every = refs
        g, hi, b = (place_ref[i] for i in range(3))
        for m in range(4):
            this_g, this_b = jnp.bitwise_xor(g, m >> 1), jnp.bitwise_xor(b, m & 1)
            for k in range(blocks):
                at = ((jnp.bitwise_xor(hi, k) * 2 + this_b) * 2 + this_g) * width
                every[pl.ds(pl.multiple_of(at, 16), width)] = got_refs[m][k]
        out_ref[...] = every[...].T

    out = jax.ShapeDtypeStruct((count, 4 * blocks * width), jnp.bfloat16)
    scratch = [pltpu.VMEM((4 * blocks * width, count), jnp.bfloat16)]
    return call(body, out, [SMEM] + [VMEM] * 4, scratch, place, *got)


def shared_plan(layout, frames_in, qkv_weight):
    g = lax.axis_index("groups")
    frame = lax.axis_index("frame")
    lo, b, hi = frame % 2, (frame // 2) % 2, frame // 4
    place = jnp.stack([g, hi, b, lo]).astype(jnp.int32)
    weights = qkv_weight.transpose(0, 2, 1)
    width, depth = weights.shape[1:]
    half = HEAD_DIM // 2
    own = frames_in[0].T

    keeper = lambda g, hi, b, lo: lo == g
    other = lambda g, hi, b, lo: lo != g
    along = lambda k: lambda g, hi, b, lo: (g, hi ^ k, b, lo)
    over_b = layout.pairs(lambda g, hi, b, lo: (g, hi, 1 - b, lo))
    over_g = layout.pairs(lambda g, hi, b, lo: (1 - g, hi, b, lo))
    over_gb = layout.pairs(lambda g, hi, b, lo: (1 - g, hi, 1 - b, lo))
    swap = lambda g, hi, b, lo: (g, hi, b, 1 - lo)
    over_lo = layout.pairs(swap)

    next_b = send(own, over_b)
    next_g = send(own, over_g)
    cut = depth // 2
    across = [send(next_b[:cut], over_g), send(next_g[cut:], over_b)]
    frames = [[own], [next_b], [next_g], across]

    extra = lax.dynamic_slice_in_dim(weights[:2], g * (width - half), half, axis=1)
    mains, extras = [weights.reshape(3 * width, depth)], [extra.reshape(2 * half, depth)]
    for got, kind in ((mains, keeper), (extras, other)):
        far = send(got[0], layout.pairs(along(2), kind))
        near = send(got[0], layout.pairs(along(1), kind))
        got.extend([near, far, send(far, layout.pairs(along(1), kind))])
    blocks = [
        (main, send(main, layout.pairs(swap, keeper)), extra, send(extra, layout.pairs(swap, other)))
        for main, extra in zip(mains, extras)
    ]

    q1, s1 = project(place, blocks[:3], frames[:3], [0, 1, 2])
    q2, s2 = project(place, blocks[:3], frames[3:], [0, 1, 2])
    q3, mine = project(place, blocks[3:], frames, [3], [s1, s2])
    queries = [[(q1, m, k) for k in range(3)] + [(q3, m, 0)] for m in range(3)]
    queries += [[(q2, 0, k) for k in range(3)] + [(q3, 3, 0)]]
    others = send(mine, over_lo)
    plane = plane_sum(mine, others)
    planes = [send(plane, layout.pairs(along(k))) for k in (1, 2, 3)]
    out1, out2, out3 = apply(place, [1, 2, 3], queries, mine, others, planes)
    (out0,) = apply(place, [0], queries, mine, others, planes)
    got = [out0, send(out1, over_b), send(out2, over_g), send(out3, over_gb)]
    return assemble(place, got)[None]


def solution(mesh):
    placed = (P(AXES, None, None), P(None, None, "frame"))

    def shards(frames_in, qkv_weight):
        width = qkv_weight.shape[2]
        if mesh.shape["groups"] == 2 and mesh.shape["frame"] == 16 and width * 2 == 5 * HEAD_DIM:
            return shared_plan(Layout(mesh), frames_in, qkv_weight)
        return gathered_plan(frames_in, qkv_weight)

    return jax.shard_map(
        shards, mesh=mesh, in_specs=placed, out_specs=P(AXES, None, None), check_vma=False
    )
```

time: 135 us -> 135 us (level)
  Pallas kernels: 0 us -> 25.6 us
  matrix products: 21.2 us -> 0 us
  waiting for transfers between devices: 62.2 us -> 51.4 us
  local copies, waits for them, and re-layouts: 3.46 us -> 11.1 us
  other arithmetic: 7.46 us -> 0.08 us
  starting transfers between devices: 38.9 us -> 46.2 us
    pallas_call x0 -> x7, Pallas kernels: none -> 25.6 us  [call(): pl.pallas_call(body, out_shape=out, in_specs=ins, out_specs=jax.tree.map(...]
    dot_general x80 -> x0, matrix products: 21.2 us -> none  [dot(): lax.dot_general(a, b, (dims, ((), ())), preferred_element_type=jnp.float32)]
    ppermute x25, waiting for transfers between devices: 62.2 us -> 51.4 us  [send(): return lax.ppermute(a, AXES, pairs)]
    ppermute x25, starting transfers between devices: 38.9 us -> 46.2 us  [send(): return lax.ppermute(a, AXES, pairs)]
    unnamed x5 -> x32, local copies, waits for them, and re-layouts: 0.05 us -> 7.2 us
    select_n x14 -> x0, other arithmetic: 3.64 us -> none  [the longest x4 3.03 us: shared_plan(): jnp.where(mine, a, send(a, layout.pairs(swap, keeper)))]
    reduce_sum x16 -> x0, other arithmetic: 1.8 us -> none  [shared_plan(): frame_keys.append(jnp.sum(keys.astype(jnp.float32), axis=1))]
    slice x47 -> x2, local copies, waits for them, and re-layouts: 0.97 us -> 2.75 us  [shared_plan(): across = [send(next_b[:cut], over_g), send(next_g[cut:], over_b)]]
  transfers between devices with their start and end apart: 25 -> 25, of which waited for: 14 -> 11; matrix products, arithmetic and copies ran while one was open for 18% -> 3% of each run, Pallas kernels for 0% -> 12%
where the time goes in v2:
time: 135 us
  waiting for transfers between devices  51.4 us (38%)
  starting transfers between devices  46.2 us (34%)
  Pallas kernels  25.6 us (19%)
  local copies, waits for them, and re-layouts  11.1 us (8%)
    ppermute x25, waiting for transfers between devices, send(): return lax.ppermute(a, AXES, pairs)  51.4 us
    ppermute x25, starting transfers between devices, send(): return lax.ppermute(a, AXES, pairs)  46.2 us
    pallas_call x7, Pallas kernels, call(): pl.pallas_call(body, out_shape=out, in_specs=ins, out_specs=jax.tree.map(...  25.6 us
    unnamed x32, local copies, waits for them, and re-layouts  7.2 us
    slice x2, local copies, waits for them, and re-layouts, shared_plan(): across = [send(next_b[:cut], over_g), send(next_g[cut:], over_b)]  2.75 us
  transfers between devices with their start and end apart: 25, of which 11 were waited for; matrix products, arithmetic and copies ran while one was open for 3% of the time, Pallas kernels for 12%

profile of v2, /device:TPU:0, one launch (start us, length us, event | category | flops | bytes accessed | tf_op | source)
XLA Modules:
  0.0 134.7 jit_solution(15796490277402299630)
XLA Ops:
  0.0 6.1 %collective-permute-start.6 = (bf16[240,2240]{1,0:T(8,128)(2,1)}, bf16[240,2240]{1,0:T(8,128)(2,1)}, u32[]{:S(2)}, u32[]{:S(2)}) collective-permute-start(bf16[240,2240]{1,0:T(8,128)(2,1)} %bitcast.12), channel_id=1, source_target_pairs={{0,8},{2,10},{4,12},{6,14},{8,0},{10,2},{12,4},{14,6},{17,25},{19,... | collective-permute-start | bytes 3225608 | tf_op jit(solution)/shard_map/ppermute | solution.py:60
  6.1 3.5 %collective-permute-start.2 = (bf16[240,2240]{1,0:T(8,128)(2,1)}, bf16[240,2240]{1,0:T(8,128)(2,1)S(1)}, u32[]{:S(2)}, u32[]{:S(2)}) collective-permute-start(bf16[240,2240]{1,0:T(8,128)(2,1)} %bitcast.13), channel_id=1, source_target_pairs={{0,4},{2,6},{4,0},{6,2},{8,12},{10,14},{12,8},{14,10},{17,21},{19,... | collective-permute-start | bytes 3225608 | tf_op jit(solution)/shard_map/ppermute | solution.py:60
  9.6 1.6 %collective-permute-start.10 = (bf16[2240,256]{1,0:T(8,128)(2,1)}, bf16[2240,256]{1,0:T(8,128)(2,1)}, u32[]{:S(2)}, u32[]{:S(2)}) collective-permute-start(bf16[2240,256]{1,0:T(8,128)(2,1)} %bitcast.18), channel_id=1, source_target_pairs={{0,2},{1,3},{2,0},{3,1},{4,6},{5,7},{6,4},{7,5},{8,10},{9,11},{10,... | collective-permute-start | bytes 3440648 | tf_op jit(solution)/shard_map/ppermute | solution.py:60
  11.2 1.2 slice.12
  12.3 0.7 collective-permute-start.8
  13.0 21.9 %collective-permute-done.6.refs_8_ = bf16[240,2240]{1,0:T(8,128)(2,1)} collective-permute-done((bf16[240,2240]{1,0:T(8,128)(2,1)}, bf16[240,2240]{1,0:T(8,128)(2,1)}, u32[]{:S(2)}, u32[]{:S(2)}) %collective-permute-start.6) | collective-permute-done | bytes 1075232 | tf_op jit(solution)/shard_map/ppermute | solution.py:60
  34.9 2.8 %collective-permute-start.12 = (bf16[240,2240]{1,0:T(8,128)(2,1)}, bf16[240,2240]{1,0:T(8,128)(2,1)}, u32[]{:S(2)}, u32[]{:S(2)}) collective-permute-start(bf16[240,2240]{1,0:T(8,128)(2,1)} %collective-permute-done.6.refs_8_), channel_id=1, source_target_pairs={{0,4},{2,6},{4,0},{6,2},{8,12},{10,14},{12,8},{14,10},{17,21},{19,... | collective-permute-start | bytes 3225608 | tf_op jit(solution)/shard_map/ppermute | solution.py:60
  37.7 0.7 collective-permute-start.4
  38.4 0.0 collective-permute-done.8.refs_10_
  38.4 1.3 collective-permute-start.1
  39.7 0.0 collective-permute-done.4.refs_6_
  39.7 1.3 collective-permute-start.9
  41.0 0.7 collective-permute-done.1.refs_3_
  41.7 0.7 copy-done.7
  42.3 0.2 collective-permute-start.11
  42.5 0.5 collective-permute-done.9.refs_11_
  43.0 0.6 copy-done.10
  43.7 1.3 collective-permute-start.5
  45.0 0.7 copy-done.4
  45.6 1.3 collective-permute-done.5.refs_7_
  46.9 0.7 copy-done.12
  47.6 2.1 %collective-permute-start = (bf16[240,2240]{1,0:T(8,128)(2,1)S(1)}, bf16[240,2240]{1,0:T(8,128)(2,1)S(1)}, u32[]{:S(2)}, u32[]{:S(2)}) collective-permute-start(bf16[240,2240]{1,0:T(8,128)(2,1)S(1)} %bitcast.15), channel_id=1, source_target_pairs={{0,1},{2,3},{4,5},{6,7},{8,9},{10,11},{12,13},{14,15},{17,16},{19,... | collective-permute-start | bytes 3225608 | tf_op jit(solution)/shard_map/ppermute | solution.py:60
  49.7 0.0 collective-permute-done.2.refs_4_
  49.7 2.3 %collective-permute-start.7 = (bf16[240,2240]{1,0:T(8,128)(2,1)}, bf16[240,2240]{1,0:T(8,128)(2,1)}, u32[]{:S(2)}, u32[]{:S(2)}) collective-permute-start(bf16[240,2240]{1,0:T(8,128)(2,1)} %collective-permute-done.6.refs_8_), channel_id=1, source_target_pairs={{0,1},{2,3},{4,5},{6,7},{8,9},{10,11},{12,13},{14,15},{17,16},{19,... | collective-permute-start | bytes 3225608 | tf_op jit(solution)/shard_map/ppermute | solution.py:60
  52.0 2.3 %collective-permute-start.3 = (bf16[240,2240]{1,0:T(8,128)(2,1)S(1)}, bf16[240,2240]{1,0:T(8,128)(2,1)}, u32[]{:S(2)}, u32[]{:S(2)}) collective-permute-start(bf16[240,2240]{1,0:T(8,128)(2,1)S(1)} %collective-permute-done.2.refs_4_), channel_id=1, source_target_pairs={{0,1},{2,3},{4,5},{6,7},{8,9},{10,11},{12,13},{14,15},{17,16},{19,... | collective-permute-start | bytes 3225608 | tf_op jit(solution)/shard_map/ppermute | solution.py:60
  54.3 2.3 %collective-permute-start.13 = (bf16[240,2240]{1,0:T(8,128)(2,1)}, bf16[240,2240]{1,0:T(8,128)(2,1)}, u32[]{:S(2)}, u32[]{:S(2)}) collective-permute-start(bf16[240,2240]{1,0:T(8,128)(2,1)} %collective-permute-done.12.refs_0_), channel_id=1, source_target_pairs={{0,1},{2,3},{4,5},{6,7},{8,9},{10,11},{12,13},{14,15},{17,16},{19,... | collective-permute-start | bytes 3225608 | tf_op jit(solution)/shard_map/ppermute | solution.py:60
  56.7 13.6 %collective-permute-done.11.refs_14_.refs_6_ = bf16[2240,256]{1,0:T(8,128)(2,1)S(1)} collective-permute-done((bf16[2240,256]{1,0:T(8,128)(2,1)}, bf16[2240,256]{1,0:T(8,128)(2,1)S(1)}, u32[]{:S(2)}, u32[]{:S(2)}) %collective-permute-start.11) | collective-permute-done | bytes 1146912 | tf_op jit(solution)/shard_map/ppermute | solution.py:60
  70.2 1.3 collective-permute-start.14
  71.6 1.9 %slice.13 = bf16[1120,256]{1,0:T(8,128)(2,1)} slice(bf16[2240,256]{1,0:T(8,128)(2,1)} %collective-permute-done.10.refs_13_.refs_5_), slice={[0:1120], [0:256]} | slice | bytes 1146880 | tf_op jit(solution)/shard_map/slice | solution.py:281
  73.5 0.8 slice.14
  74.3 0.0 collective-permute-done.14.refs_2_
  74.3 3.3 %collective-permute-start.16 = (bf16[1120,256]{1,0:T(8,128)(2,1)}, bf16[1120,256]{1,0:T(8,128)(2,1)}, u32[]{:S(2)}, u32[]{:S(2)}) collective-permute-start(bf16[1120,256]{1,0:T(8,128)(2,1)} %slice.13), channel_id=1, source_target_pairs={{0,16},{1,17},{2,18},{3,19},{4,20},{5,21},{6,22},{7,23},{8,24},{9,... | collective-permute-start | bytes 1720328 | tf_op jit(solution)/shard_map/ppermute | solution.py:60
  77.6 1.5 %collective-permute-start.17 = (bf16[1120,256]{1,0:T(8,128)(2,1)}, bf16[1120,256]{1,0:T(8,128)(2,1)}, u32[]{:S(2)}, u32[]{:S(2)}) collective-permute-start(bf16[1120,256]{1,0:T(8,128)(2,1)} %slice.14), channel_id=1, source_target_pairs={{0,2},{1,3},{2,0},{3,1},{4,6},{5,7},{6,4},{7,5},{8,10},{9,11},{10,... | collective-permute-start | bytes 1720328 | tf_op jit(solution)/shard_map/ppermute | solution.py:60
  79.2 0.0 collective-permute-done.7.refs_9_
  79.2 1.3 collective-permute-start.15
  80.5 0.1 pad_add_fusion.place_ref
  80.6 0.9 copy-done.3
  81.5 0.9 copy-done.5
  82.4 0.9 copy-done.8
  83.3 0.9 copy-done.11
  84.2 0.9 copy-done.13
  85.1 9.8 %shard_map.28 = (f32[3,3,96,256]{3,2,1,0:T(8,128)S(1)}, f32[3,88,128]{2,1,0:T(8,128)S(1)}) custom-call(s32[4]{0:T(128)S(1)} %pad_add_fusion.place_ref, bf16[240,2240]{1,0:T(8,128)(2,1)S(1)} %bitcast.16, bf16[240,2240]{1,0:T(8,128)(2,1)S(1)} %collective-permute-done.refs_1_, bf16[32,2240]{1,0:T(8,128)(2,1)S(1)} %bitcast.25, bf16[32,2240]{1,0:T(8,128)(2,1)S(1)} %copy-done.8, ...), custom_call_target="tpu_custom_call" | custom-call | flops 1000 | bytes 1000 | tf_op jit(solution)/shard_map/pallas_call | solution.py:70
  94.9 0.0 copy-start.1
  95.0 0.0 collective-permute-done.17.refs_13_.refs_8_
  95.0 5.1 %shard_map.29 = (f32[1,3,96,256]{3,2,1,0:T(8,128)S(1)}, f32[1,88,128]{2,1,0:T(8,128)S(1)}) custom-call(s32[4]{0:T(128)S(1)} %pad_add_fusion.place_ref, bf16[240,2240]{1,0:T(8,128)(2,1)S(1)} %bitcast.17, bf16[240,2240]{1,0:T(8,128)(2,1)S(1)} %collective-permute-done.refs_1_, bf16[32,2240]{1,0:T(8,128)(2,1)S(1)} %bitcast.26, bf16[32,2240]{1,0:T(8,128)(2,1)S(1)} %copy-done.9, ...), custom_call_target="tpu_custom_call" | custom-call | flops 1000 | bytes 1000 | tf_op jit(solution)/shard_map/pallas_call | solution.py:70
  100.1 0.0 collective-permute-done.15.refs_3_
  100.1 6.1 %shard_map.30 = (f32[4,1,96,256]{3,2,1,0:T(8,128)S(1)}, f32[4,88,128]{2,1,0:T(8,128)S(1)}) custom-call(s32[4]{0:T(128)S(1)} %pad_add_fusion.place_ref, bf16[240,2240]{1,0:T(8,128)(2,1)} %collective-permute-done.12.refs_0_, bf16[240,2240]{1,0:T(8,128)(2,1)} %collective-permute-done.13.refs_1_, bf16[32,2240]{1,0:T(8,128)(2,1)} %collective-permute-done.14.refs_2_, ...), custom_call_target="tpu_custom_call" | custom-call | flops 1000 | bytes 1000 | tf_op jit(solution)/shard_map/pallas_call | solution.py:70
  106.2 1.8 %collective-permute-start.18 = (f32[4,88,128]{2,1,0:T(8,128)S(1)}, f32[4,88,128]{2,1,0:T(8,128)S(1)}, u32[]{:S(2)}, u32[]{:S(2)}) collective-permute-start(f32[4,88,128]{2,1,0:T(8,128)S(1)} %get-tuple-element.19.a_ref.refs_3_), channel_id=1, source_target_pairs={{0,1},{1,0},{2,3},{3,2},{4,5},{5,4},{6,7},{7,6},{8,9},{9,8},{10,11... | collective-permute-start | bytes 540680 | tf_op jit(solution)/shard_map/ppermute | solution.py:60
  108.0 1.0 collective-permute-done.18.b_ref.refs_4_
  109.1 1.5 %collective-permute-start.19 = (f32[2,88,128]{2,1,0:T(8,128)S(1)}, f32[2,88,128]{2,1,0:T(8,128)S(1)}, u32[]{:S(2)}, u32[]{:S(2)}) collective-permute-start(f32[2,88,128]{2,1,0:T(8,128)S(1)} %shard_map.31), channel_id=1, source_target_pairs={{0,4},{1,5},{2,6},{3,7},{4,0},{5,1},{6,2},{7,3},{8,12},{9,13},{10,... | collective-permute-start | bytes 270344 | tf_op jit(solution)/shard_map/ppermute | solution.py:60
  110.6 2.1 %collective-permute-start.20 = (f32[2,88,128]{2,1,0:T(8,128)S(1)}, f32[2,88,128]{2,1,0:T(8,128)S(1)}, u32[]{:S(2)}, u32[]{:S(2)}) collective-permute-start(f32[2,88,128]{2,1,0:T(8,128)S(1)} %shard_map.31), channel_id=1, source_target_pairs={{0,8},{1,9},{2,10},{3,11},{4,12},{5,13},{6,14},{7,15},{8,0},{9,1},... | collective-permute-start | bytes 270344 | tf_op jit(solution)/shard_map/ppermute | solution.py:60
  112.7 1.4 %collective-permute-start.21 = (f32[2,88,128]{2,1,0:T(8,128)S(1)}, f32[2,88,128]{2,1,0:T(8,128)S(1)}, u32[]{:S(2)}, u32[]{:S(2)}) collective-permute-start(f32[2,88,128]{2,1,0:T(8,128)S(1)} %shard_map.31), channel_id=1, source_target_pairs={{0,12},{1,13},{2,14},{3,15},{4,8},{5,9},{6,10},{7,11},{8,4},{9,5},... | collective-permute-start | bytes 270344 | tf_op jit(solution)/shard_map/ppermute | solution.py:60
  114.1 0.0 collective-permute-done.19.refs_5_
  114.1 2.0 %collective-permute-done.20.refs_6_ = f32[2,88,128]{2,1,0:T(8,128)S(1)} collective-permute-done((f32[2,88,128]{2,1,0:T(8,128)S(1)}, f32[2,88,128]{2,1,0:T(8,128)S(1)}, u32[]{:S(2)}, u32[]{:S(2)}) %collective-permute-start.20) | collective-permute-done | bytes 90144 | tf_op jit(solution)/shard_map/ppermute | solution.py:60
  116.1 4.8 %collective-permute-done.21.refs_7_ = f32[2,88,128]{2,1,0:T(8,128)S(1)} collective-permute-done((f32[2,88,128]{2,1,0:T(8,128)S(1)}, f32[2,88,128]{2,1,0:T(8,128)S(1)}, u32[]{:S(2)}, u32[]{:S(2)}) %collective-permute-start.21) | collective-permute-done | bytes 90144 | tf_op jit(solution)/shard_map/ppermute | solution.py:60
  120.9 1.8 %shard_map.33 = (bf16[4,80,256]{2,1,0:T(8,128)(2,1)S(1)}, bf16[4,80,256]{2,1,0:T(8,128)(2,1)S(1)}, bf16[4,80,256]{2,1,0:T(8,128)(2,1)S(1)}) custom-call(s32[4]{0:T(128)S(1)} %pad_add_fusion.place_ref, f32[3,3,96,256]{3,2,1,0:T(8,128)S(1)} %get-tuple-element.14.refs_0_, f32[4,1,96,256]{3,2,1,0:T(8,128)S(1)} %get-tuple-element.17.refs_1_, ...), custom_call_target="tpu_custom_call" | custom-call | flops 1000 | bytes 1000 | tf_op jit(solution)/shard_map/pallas_call | solution.py:70
  122.7 0.6 collective-permute-start.22
  123.2 0.0 collective-permute-start.23
  123.2 3.0 %collective-permute-start.24 = (bf16[4,80,256]{2,1,0:T(8,128)(2,1)S(1)}, bf16[4,80,256]{2,1,0:T(8,128)(2,1)S(1)}, u32[]{:S(2)}, u32[]{:S(2)}) collective-permute-start(bf16[4,80,256]{2,1,0:T(8,128)(2,1)S(1)} %get-tuple-element.22), channel_id=1, source_target_pairs={{0,18},{1,19},{2,16},{3,17},{4,22},{5,23},{6,20},{7,21},{8,26},{9,... | collective-permute-start | bytes 491528 | tf_op jit(solution)/shard_map/ppermute | solution.py:60
  126.2 1.1 shard_map.32.refs_0_
  127.4 1.6 %collective-permute-done.22.refs_1_ = bf16[4,80,256]{2,1,0:T(8,128)(2,1)S(1)} collective-permute-done((bf16[4,80,256]{2,1,0:T(8,128)(2,1)S(1)}, bf16[4,80,256]{2,1,0:T(8,128)(2,1)S(1)}, u32[]{:S(2)}, u32[]{:S(2)}) %collective-permute-start.22) | collective-permute-done | bytes 163872 | tf_op jit(solution)/shard_map/ppermute | solution.py:60
  129.0 1.3 collective-permute-done.23.refs_2_
  130.3 2.7 %collective-permute-done.24.refs_3_ = bf16[4,80,256]{2,1,0:T(8,128)(2,1)S(1)} collective-permute-done((bf16[4,80,256]{2,1,0:T(8,128)(2,1)S(1)}, bf16[4,80,256]{2,1,0:T(8,128)(2,1)S(1)}, u32[]{:S(2)}, u32[]{:S(2)}) %collective-permute-start.24) | collective-permute-done | bytes 163872 | tf_op jit(solution)/shard_map/ppermute | solution.py:60
  133.0 1.7 %shard_map.34 = bf16[256,1280]{1,0:T(8,128)(2,1)} custom-call(s32[4]{0:T(128)S(1)} %pad_add_fusion.place_ref, bf16[4,80,256]{2,1,0:T(8,128)(2,1)S(1)} %shard_map.32.refs_0_, bf16[4,80,256]{2,1,0:T(8,128)(2,1)S(1)} %collective-permute-done.22.refs_1_, bf16[4,80,256]{2,1,0:T(8,128)(2,1)S(1)} %collective-permute-done.23.refs_2_, ...), custom_call_target="tpu_custom_call" | custom-call | flops 1000 | bytes 1000 | tf_op jit(solution)/shard_map/pallas_call | solution.py:70
  (30 shorter events, 0.1 us)
Async XLA Ops:
  0.0 47.6 %copy-start = (bf16[3,2240,80]{1,2,0:T(8,128)(2,1)S(1)}, bf16[3,2240,80]{1,2,0:T(8,128)(2,1)}, u32[]{:S(2)}) copy-start(bf16[3,2240,80]{1,2,0:T(8,128)(2,1)} %param.3) | copy-start | bytes 3225604
  0.0 34.9 %collective-permute-start.6 = (bf16[240,2240]{1,0:T(8,128)(2,1)}, bf16[240,2240]{1,0:T(8,128)(2,1)}, u32[]{:S(2)}, u32[]{:S(2)}) collective-permute-start(bf16[240,2240]{1,0:T(8,128)(2,1)} %bitcast.12), channel_id=1, source_target_pairs={{0,8},{2,10},{4,12},{6,14},{8,0},{10,2},{12,4},{14,6},{17,25},{19,... | collective-permute-start | bytes 3225608 | tf_op jit(solution)/shard_map/ppermute | solution.py:60
  6.1 43.6 %collective-permute-start.2 = (bf16[240,2240]{1,0:T(8,128)(2,1)}, bf16[240,2240]{1,0:T(8,128)(2,1)S(1)}, u32[]{:S(2)}, u32[]{:S(2)}) collective-permute-start(bf16[240,2240]{1,0:T(8,128)(2,1)} %bitcast.13), channel_id=1, source_target_pairs={{0,4},{2,6},{4,0},{6,2},{8,12},{10,14},{12,8},{14,10},{17,21},{19,... | collective-permute-start | bytes 3225608 | tf_op jit(solution)/shard_map/ppermute | solution.py:60
  9.6 42.5 %collective-permute-start.10 = (bf16[2240,256]{1,0:T(8,128)(2,1)}, bf16[2240,256]{1,0:T(8,128)(2,1)}, u32[]{:S(2)}, u32[]{:S(2)}) collective-permute-start(bf16[2240,256]{1,0:T(8,128)(2,1)} %bitcast.18), channel_id=1, source_target_pairs={{0,2},{1,3},{2,0},{3,1},{4,6},{5,7},{6,4},{7,5},{8,10},{9,11},{10,... | collective-permute-start | bytes 3440648 | tf_op jit(solution)/shard_map/ppermute | solution.py:60
  12.3 26.1 %collective-permute-start.8 = (bf16[32,2240]{1,0:T(8,128)(2,1)S(1)}, bf16[32,2240]{1,0:T(8,128)(2,1)S(1)}, u32[]{:S(2)}, u32[]{:S(2)}) collective-permute-start(bf16[32,2240]{1,0:T(8,128)(2,1)S(1)} %bitcast.22), channel_id=1, source_target_pairs={{1,9},{3,11},{5,13},{7,15},{9,1},{11,3},{13,5},{15,7},{16,24},{18,... | collective-permute-start | bytes 430088 | tf_op jit(solution)/shard_map/ppermute | solution.py:60
  34.9 19.5 %collective-permute-start.12 = (bf16[240,2240]{1,0:T(8,128)(2,1)}, bf16[240,2240]{1,0:T(8,128)(2,1)}, u32[]{:S(2)}, u32[]{:S(2)}) collective-permute-start(bf16[240,2240]{1,0:T(8,128)(2,1)} %collective-permute-done.6.refs_8_), channel_id=1, source_target_pairs={{0,4},{2,6},{4,0},{6,2},{8,12},{10,14},{12,8},{14,10},{17,21},{19,... | collective-permute-start | bytes 3225608 | tf_op jit(solution)/shard_map/ppermute | solution.py:60
  37.7 2.0 %collective-permute-start.4 = (bf16[32,2240]{1,0:T(8,128)(2,1)S(1)}, bf16[32,2240]{1,0:T(8,128)(2,1)S(1)}, u32[]{:S(2)}, u32[]{:S(2)}) collective-permute-start(bf16[32,2240]{1,0:T(8,128)(2,1)S(1)} %bitcast.23), channel_id=1, source_target_pairs={{1,5},{3,7},{5,1},{7,3},{9,13},{11,15},{13,9},{15,11},{16,20},{18,... | collective-permute-start | bytes 430088 | tf_op jit(solution)/shard_map/ppermute | solution.py:60
  38.4 35.9 %copy-start.2 = (bf16[32,2240]{1,0:T(8,128)(2,1)}, bf16[32,2240]{1,0:T(8,128)(2,1)S(1)}, u32[]{:S(2)}) copy-start(bf16[32,2240]{1,0:T(8,128)(2,1)S(1)} %collective-permute-done.8.refs_10_) | copy-start | bytes 430084
  38.4 3.3 %collective-permute-start.1 = (bf16[32,2240]{1,0:T(8,128)(2,1)S(1)}, bf16[32,2240]{1,0:T(8,128)(2,1)S(1)}, u32[]{:S(2)}, u32[]{:S(2)}) collective-permute-start(bf16[32,2240]{1,0:T(8,128)(2,1)S(1)} %bitcast.24), channel_id=1, source_target_pairs={{1,0},{3,2},{5,4},{7,6},{9,8},{11,10},{13,12},{15,14},{16,17},{18,... | collective-permute-start | bytes 430088 | tf_op jit(solution)/shard_map/ppermute | solution.py:60
  39.7 3.3 %collective-permute-start.9 = (bf16[32,2240]{1,0:T(8,128)(2,1)S(1)}, bf16[32,2240]{1,0:T(8,128)(2,1)S(1)}, u32[]{:S(2)}, u32[]{:S(2)}) collective-permute-start(bf16[32,2240]{1,0:T(8,128)(2,1)S(1)} %collective-permute-done.8.refs_10_), channel_id=1, source_target_pairs={{1,0},{3,2},{5,4},{7,6},{9,8},{11,10},{13,12},{15,14},{16,17},{18,... | collective-permute-start | bytes 430088 | tf_op jit(solution)/shard_map/ppermute | solution.py:60
  41.7 0.7 copy-start.7
  42.3 27.9 %collective-permute-start.11 = (bf16[2240,256]{1,0:T(8,128)(2,1)}, bf16[2240,256]{1,0:T(8,128)(2,1)S(1)}, u32[]{:S(2)}, u32[]{:S(2)}) collective-permute-start(bf16[2240,256]{1,0:T(8,128)(2,1)} %bitcast.19), channel_id=1, source_target_pairs={{0,16},{1,17},{2,18},{3,19},{4,20},{5,21},{6,22},{7,23},{8,24},{9,... | collective-permute-start | bytes 3440648 | tf_op jit(solution)/shard_map/ppermute | solution.py:60
  43.0 0.7 copy-start.10
  43.7 3.3 %collective-permute-start.5 = (bf16[32,2240]{1,0:T(8,128)(2,1)S(1)}, bf16[32,2240]{1,0:T(8,128)(2,1)S(1)}, u32[]{:S(2)}, u32[]{:S(2)}) collective-permute-start(bf16[32,2240]{1,0:T(8,128)(2,1)S(1)} %collective-permute-done.4.refs_6_), channel_id=1, source_target_pairs={{1,0},{3,2},{5,4},{7,6},{9,8},{11,10},{13,12},{15,14},{16,17},{18,... | collective-permute-start | bytes 430088 | tf_op jit(solution)/shard_map/ppermute | solution.py:60
  44.9 0.7 copy-start.4
  46.9 0.7 copy-start.12
  47.6 30.1 %collective-permute-start = (bf16[240,2240]{1,0:T(8,128)(2,1)S(1)}, bf16[240,2240]{1,0:T(8,128)(2,1)S(1)}, u32[]{:S(2)}, u32[]{:S(2)}) collective-permute-start(bf16[240,2240]{1,0:T(8,128)(2,1)S(1)} %bitcast.15), channel_id=1, source_target_pairs={{0,1},{2,3},{4,5},{6,7},{8,9},{10,11},{12,13},{14,15},{17,16},{19,... | collective-permute-start | bytes 3225608 | tf_op jit(solution)/shard_map/ppermute | solution.py:60
  49.7 29.5 %collective-permute-start.7 = (bf16[240,2240]{1,0:T(8,128)(2,1)}, bf16[240,2240]{1,0:T(8,128)(2,1)}, u32[]{:S(2)}, u32[]{:S(2)}) collective-permute-start(bf16[240,2240]{1,0:T(8,128)(2,1)} %collective-permute-done.6.refs_8_), channel_id=1, source_target_pairs={{0,1},{2,3},{4,5},{6,7},{8,9},{10,11},{12,13},{14,15},{17,16},{19,... | collective-permute-start | bytes 3225608 | tf_op jit(solution)/shard_map/ppermute | solution.py:60
  52.0 28.5 %collective-permute-start.3 = (bf16[240,2240]{1,0:T(8,128)(2,1)S(1)}, bf16[240,2240]{1,0:T(8,128)(2,1)}, u32[]{:S(2)}, u32[]{:S(2)}) collective-permute-start(bf16[240,2240]{1,0:T(8,128)(2,1)S(1)} %collective-permute-done.2.refs_4_), channel_id=1, source_target_pairs={{0,1},{2,3},{4,5},{6,7},{8,9},{10,11},{12,13},{14,15},{17,16},{19,... | collective-permute-start | bytes 3225608 | tf_op jit(solution)/shard_map/ppermute | solution.py:60
  54.3 45.8 %collective-permute-start.13 = (bf16[240,2240]{1,0:T(8,128)(2,1)}, bf16[240,2240]{1,0:T(8,128)(2,1)}, u32[]{:S(2)}, u32[]{:S(2)}) collective-permute-start(bf16[240,2240]{1,0:T(8,128)(2,1)} %collective-permute-done.12.refs_0_), channel_id=1, source_target_pairs={{0,1},{2,3},{4,5},{6,7},{8,9},{10,11},{12,13},{14,15},{17,16},{19,... | collective-permute-start | bytes 3225608 | tf_op jit(solution)/shard_map/ppermute | solution.py:60
  70.2 4.1 %copy-start.15 = (bf16[2240,256]{1,0:T(8,128)(2,1)}, bf16[2240,256]{1,0:T(8,128)(2,1)S(1)}, u32[]{:S(2)}) copy-start(bf16[2240,256]{1,0:T(8,128)(2,1)S(1)} %collective-permute-done.11.refs_14_.refs_6_) | copy-start | bytes 3440644
  70.2 4.1 %collective-permute-start.14 = (bf16[32,2240]{1,0:T(8,128)(2,1)S(1)}, bf16[32,2240]{1,0:T(8,128)(2,1)}, u32[]{:S(2)}, u32[]{:S(2)}) collective-permute-start(bf16[32,2240]{1,0:T(8,128)(2,1)S(1)} %collective-permute-done.8.refs_10_), channel_id=1, source_target_pairs={{1,5},{3,7},{5,1},{7,3},{9,13},{11,15},{13,9},{15,11},{16,20},{18,... | collective-permute-start | bytes 430088 | tf_op jit(solution)/shard_map/ppermute | solution.py:60
  74.3 20.6 %collective-permute-start.16 = (bf16[1120,256]{1,0:T(8,128)(2,1)}, bf16[1120,256]{1,0:T(8,128)(2,1)}, u32[]{:S(2)}, u32[]{:S(2)}) collective-permute-start(bf16[1120,256]{1,0:T(8,128)(2,1)} %slice.13), channel_id=1, source_target_pairs={{0,16},{1,17},{2,18},{3,19},{4,20},{5,21},{6,22},{7,23},{8,24},{9,... | collective-permute-start | bytes 1720328 | tf_op jit(solution)/shard_map/ppermute | solution.py:60
  77.6 17.3 %collective-permute-start.17 = (bf16[1120,256]{1,0:T(8,128)(2,1)}, bf16[1120,256]{1,0:T(8,128)(2,1)}, u32[]{:S(2)}, u32[]{:S(2)}) collective-permute-start(bf16[1120,256]{1,0:T(8,128)(2,1)} %slice.14), channel_id=1, source_target_pairs={{0,2},{1,3},{2,0},{3,1},{4,6},{5,7},{6,4},{7,5},{8,10},{9,11},{10,... | collective-permute-start | bytes 1720328 | tf_op jit(solution)/shard_map/ppermute | solution.py:60
  79.2 20.9 %collective-permute-start.15 = (bf16[32,2240]{1,0:T(8,128)(2,1)}, bf16[32,2240]{1,0:T(8,128)(2,1)}, u32[]{:S(2)}, u32[]{:S(2)}) collective-permute-start(bf16[32,2240]{1,0:T(8,128)(2,1)} %collective-permute-done.14.refs_2_), channel_id=1, source_target_pairs={{1,0},{3,2},{5,4},{7,6},{9,8},{11,10},{13,12},{15,14},{16,17},{18,... | collective-permute-start | bytes 430088 | tf_op jit(solution)/shard_map/ppermute | solution.py:60
  80.6 0.9 copy-start.3
  81.5 0.9 copy-start.5
  82.4 0.9 copy-start.8
  83.3 0.9 copy-start.11
  84.2 0.9 copy-start.13
  85.1 9.8 %copy-start.6 = (bf16[32,2240]{1,0:T(8,128)(2,1)S(1)}, bf16[32,2240]{1,0:T(8,128)(2,1)}, u32[]{:S(2)}) copy-start(bf16[32,2240]{1,0:T(8,128)(2,1)} %copy-done.4) | copy-start | bytes 430084
  85.1 9.8 %copy-start.9 = (bf16[32,2240]{1,0:T(8,128)(2,1)S(1)}, bf16[32,2240]{1,0:T(8,128)(2,1)}, u32[]{:S(2)}) copy-start(bf16[32,2240]{1,0:T(8,128)(2,1)} %copy-done.7) | copy-start | bytes 430084
  85.1 9.9 %copy-start.14 = (bf16[32,2240]{1,0:T(8,128)(2,1)S(1)}, bf16[32,2240]{1,0:T(8,128)(2,1)}, u32[]{:S(2)}) copy-start(bf16[32,2240]{1,0:T(8,128)(2,1)} %copy-done.12) | copy-start | bytes 430084
  94.9 5.2 %copy-start.1 = (bf16[1,256,2240]{1,2,0:T(8,128)(2,1)S(1)}, bf16[1,256,2240]{1,2,0:T(8,128)(2,1)}, u32[]{:S(2)}) copy-start(bf16[1,256,2240]{1,2,0:T(8,128)(2,1)} %param.2) | copy-start | bytes 3440644
  106.2 2.9 %collective-permute-start.18 = (f32[4,88,128]{2,1,0:T(8,128)S(1)}, f32[4,88,128]{2,1,0:T(8,128)S(1)}, u32[]{:S(2)}, u32[]{:S(2)}) collective-permute-start(f32[4,88,128]{2,1,0:T(8,128)S(1)} %get-tuple-element.19.a_ref.refs_3_), channel_id=1, source_target_pairs={{0,1},{1,0},{2,3},{3,2},{4,5},{5,4},{6,7},{7,6},{8,9},{9,8},{10,11... | collective-permute-start | bytes 540680 | tf_op jit(solution)/shard_map/ppermute | solution.py:60
  109.1 5.0 %collective-permute-start.19 = (f32[2,88,128]{2,1,0:T(8,128)S(1)}, f32[2,88,128]{2,1,0:T(8,128)S(1)}, u32[]{:S(2)}, u32[]{:S(2)}) collective-permute-start(f32[2,88,128]{2,1,0:T(8,128)S(1)} %shard_map.31), channel_id=1, source_target_pairs={{0,4},{1,5},{2,6},{3,7},{4,0},{5,1},{6,2},{7,3},{8,12},{9,13},{10,... | collective-permute-start | bytes 270344 | tf_op jit(solution)/shard_map/ppermute | solution.py:60
  110.6 5.5 %collective-permute-start.20 = (f32[2,88,128]{2,1,0:T(8,128)S(1)}, f32[2,88,128]{2,1,0:T(8,128)S(1)}, u32[]{:S(2)}, u32[]{:S(2)}) collective-permute-start(f32[2,88,128]{2,1,0:T(8,128)S(1)} %shard_map.31), channel_id=1, source_target_pairs={{0,8},{1,9},{2,10},{3,11},{4,12},{5,13},{6,14},{7,15},{8,0},{9,1},... | collective-permute-start | bytes 270344 | tf_op jit(solution)/shard_map/ppermute | solution.py:60
  112.7 8.2 %collective-permute-start.21 = (f32[2,88,128]{2,1,0:T(8,128)S(1)}, f32[2,88,128]{2,1,0:T(8,128)S(1)}, u32[]{:S(2)}, u32[]{:S(2)}) collective-permute-start(f32[2,88,128]{2,1,0:T(8,128)S(1)} %shard_map.31), channel_id=1, source_target_pairs={{0,12},{1,13},{2,14},{3,15},{4,8},{5,9},{6,10},{7,11},{8,4},{9,5},... | collective-permute-start | bytes 270344 | tf_op jit(solution)/shard_map/ppermute | solution.py:60
  122.7 6.3 %collective-permute-start.22 = (bf16[4,80,256]{2,1,0:T(8,128)(2,1)S(1)}, bf16[4,80,256]{2,1,0:T(8,128)(2,1)S(1)}, u32[]{:S(2)}, u32[]{:S(2)}) collective-permute-start(bf16[4,80,256]{2,1,0:T(8,128)(2,1)S(1)} %get-tuple-element.20), channel_id=1, source_target_pairs={{0,2},{1,3},{2,0},{3,1},{4,6},{5,7},{6,4},{7,5},{8,10},{9,11},{10,... | collective-permute-start | bytes 491528 | tf_op jit(solution)/shard_map/ppermute | solution.py:60
  123.2 7.1 %collective-permute-start.23 = (bf16[4,80,256]{2,1,0:T(8,128)(2,1)S(1)}, bf16[4,80,256]{2,1,0:T(8,128)(2,1)S(1)}, u32[]{:S(2)}, u32[]{:S(2)}) collective-permute-start(bf16[4,80,256]{2,1,0:T(8,128)(2,1)S(1)} %get-tuple-element.21), channel_id=1, source_target_pairs={{0,16},{1,17},{2,18},{3,19},{4,20},{5,21},{6,22},{7,23},{8,24},{9,... | collective-permute-start | bytes 491528 | tf_op jit(solution)/shard_map/ppermute | solution.py:60
  123.2 9.8 %collective-permute-start.24 = (bf16[4,80,256]{2,1,0:T(8,128)(2,1)S(1)}, bf16[4,80,256]{2,1,0:T(8,128)(2,1)S(1)}, u32[]{:S(2)}, u32[]{:S(2)}) collective-permute-start(bf16[4,80,256]{2,1,0:T(8,128)(2,1)S(1)} %get-tuple-element.22), channel_id=1, source_target_pairs={{0,18},{1,19},{2,16},{3,17},{4,22},{5,23},{6,20},{7,21},{8,26},{9,... | collective-permute-start | bytes 491528 | tf_op jit(solution)/shard_map/ppermute | solution.py:60

commit v3 on v2

v3 whole, which is shorter than its diff:
```python
import jax
import jax.numpy as jnp
from jax import lax
from jax.experimental import pallas as pl
from jax.experimental.pallas import tpu as pltpu
from jax.sharding import PartitionSpec as P

HEAD_DIM = 32
EPSILON = 1e-06
AXES = ("groups", "frame")


def dot(a, b, dims):
    return lax.dot_general(a, b, (dims, ((), ())), preferred_element_type=jnp.float32)


def gathered_plan(frames_in, qkv_weight):
    tokens = frames_in[0]
    count = tokens.shape[0]
    weights = lax.all_gather(qkv_weight, "frame", axis=2, tiled=True)
    projected = jnp.einsum("td,sdc->stc", tokens, weights, preferred_element_type=jnp.float32)
    heads = weights.shape[2] // HEAD_DIM
    split = lambda a: a.reshape(count, heads, HEAD_DIM)
    queries = split(jax.nn.relu(projected[0]))
    keys = split(jax.nn.relu(projected[1].astype(jnp.bfloat16)))
    values = split(projected[2].astype(jnp.bfloat16))
    state = jnp.einsum("thi,thj->hij", keys, values, preferred_element_type=jnp.float32)
    key_sum = jnp.sum(keys.astype(jnp.float32), axis=0)
    both = jnp.concatenate([state, key_sum[:, :, None]], axis=2)
    everyone = lax.all_gather(both.reshape(heads, -1), "frame")
    upto = jnp.arange(everyone.shape[0]) <= lax.axis_index("frame")
    total = jnp.sum(jnp.where(upto[:, None, None], everyone, 0.0), axis=0).reshape(both.shape)
    result = jnp.einsum("thi,hij->thj", queries, total, precision=lax.Precision.HIGHEST)
    attended = result[..., :HEAD_DIM] / (result[..., HEAD_DIM:] + EPSILON)
    return attended.astype(jnp.bfloat16).reshape(1, count, -1)


class Layout:
    def __init__(self, mesh):
        self.frames = mesh.shape["frame"]
        self.lows = 2
        self.highs = self.frames // 4

    def pairs(self, target, source=lambda g, hi, b, lo: True):
        out = []
        for g in range(2):
            for hi in range(self.highs):
                for b in range(2):
                    for lo in range(self.lows):
                        if source(g, hi, b, lo):
                            to = target(g, hi, b, lo)
                            out.append((self.place(g, hi, b, lo), self.place(*to)))
        return out

    def place(self, g, hi, b, lo):
        return ((g * self.highs + hi) * 2 + b) * self.lows + lo


def send(a, pairs):
    return lax.ppermute(a, AXES, pairs)


ANY = pl.BlockSpec(memory_space=pl.ANY)
VMEM = pl.BlockSpec(memory_space=pltpu.VMEM)
SMEM = pl.BlockSpec(memory_space=pltpu.SMEM)
LIGHT = pl.CostEstimate(flops=1000, bytes_accessed=1000, transcendentals=0)


def call(body, out, ins, scratch, *operands):
    return pl.pallas_call(
        body,
        out_shape=out,
        in_specs=ins,
        out_specs=jax.tree.map(lambda _: VMEM, out),
        scratch_shapes=scratch,
        compiler_params=pltpu.CompilerParams(vmem_limit_bytes=16 * 2**20),
        cost_estimate=LIGHT,
    )(*operands)


def heads_of(g, width, half):
    shape = (width, width + half)
    row = lax.broadcasted_iota(jnp.int32, shape, 0)
    column = lax.broadcasted_iota(jnp.int32, shape, 1)
    turned = column + half * g
    turned = jnp.where(turned >= width + half, turned - (width + half), turned)
    return (width * g + row) // HEAD_DIM == (4 * half * g + turned) // HEAD_DIM


def pick(place, own, swapped, half):
    width, depth = own.shape[0] // 3, own.shape[1]
    part = -(-depth // 256) * 128
    more = width + half
    rows = 2 * more + width

    def body(place_ref, own_ref, swapped_ref, kv_ref, q_ref, all_ref, other_kv_ref, other_q_ref, full):
        g, lo = place_ref[0], place_ref[3]
        mine = lo == g
        full[:, 2 * part - 128 :] = jnp.zeros((rows, 128), full.dtype)
        at = pl.multiple_of(g * (width - half), 16)
        for start, which in ((0, 1), (more, 2), (more + width, 0)):
            shard = pl.ds(which * width, width)
            full[start : start + width, :depth] = jnp.where(mine, own_ref[shard], swapped_ref[shard])
            if which < 2:
                extra = pl.ds(which * width + at, half)
                full[start + width : start + more, :depth] = jnp.where(mine, swapped_ref[extra], own_ref[extra])
        this = full[:, pl.ds(pl.multiple_of(lo * part, 128), part)]
        that = full[:, pl.ds(pl.multiple_of((1 - lo) * part, 128), part)]
        kv_ref[...] = this[: more + width]
        q_ref[...] = this[more + width :]
        all_ref[...] = this
        other_kv_ref[...] = that[: more + width]
        other_q_ref[...] = that[more + width :]

    shape = lambda n: jax.ShapeDtypeStruct((n, part), own.dtype)
    out = [shape(more + width), shape(more), shape(rows), shape(more + width), shape(more)]
    return call(body, out, [SMEM, VMEM, VMEM], [pltpu.VMEM((rows, 2 * part), own.dtype)], place, own, swapped)


def project(place, half, jobs, blocks, frames, carried=()):
    arrays = []

    def index(a):
        for i, b in enumerate(arrays):
            if a is b:
                return i
        arrays.append(a)
        return len(arrays) - 1

    count = frames[jobs[0][1]][0].shape[1]
    depth = sum(p.shape[0] for p in frames[jobs[0][1]])
    part = blocks[jobs[0][0]][jobs[0][2]][0].shape[1]
    n_q = sum(what == "q" for _, _, what in jobs)
    ms = sorted({m for _, m, what in jobs if what == "kv"} | {m for m, _ in carried})
    more = 3 * HEAD_DIM
    width = more - half
    used = {}
    for k, m, what in jobs:
        one, two, first = blocks[k][what]
        used.setdefault((k, what), (index(one), index(two), first, []))[3].append(m)
    parts = {m: [index(p) for p in frames[m]] for _, m, _ in jobs}
    places, order = {}, []
    for (k, what), (_, _, _, on) in used.items():
        for m in on:
            if what == "q":
                places[k, m] = len(order)
                order.append((k, m))
    n_in = len(arrays)

    def body(place_ref, *refs):
        ins, refs = refs[:n_in], list(refs[n_in:])
        c_refs = [refs.pop(0) for _ in carried]
        q_ref = refs.pop(0) if n_q else None
        s_ref = refs.pop(0) if ms else None
        (w_all,) = refs
        g, lo = place_ref[0], place_ref[3]
        first_half = lo == 0
        if ms:
            same = heads_of(g, width, half)
            ones = jnp.ones((8, count), jnp.bfloat16)
            s_ref[...] = jnp.zeros_like(s_ref)
            for (m, a), c_ref in zip(carried, c_refs):
                s_ref[ms.index(m)] = c_ref[a]
        for i, ((k, what), (one, two, first, on)) in enumerate(used.items()):
            n = more if what == "q" else more + width
            w_ref = w_all.at[i % 2]
            one, two = ins[one][first : first + n], ins[two][first : first + n]
            w_ref[:n, :part] = jnp.where(first_half, one, two)
            w_ref[:n, part:] = jnp.where(first_half, two, one)[:, : depth - part]
            for m in on:
                x = [ins[p][...] for p in parts[m]]
                x = jnp.concatenate(x, axis=0) if len(x) > 1 else x[0]
                made = dot(w_ref[:n], x, ((1,), (0,)))
                if what == "q":
                    q_ref[places[k, m]] = jnp.maximum(made, 0.0)
                    continue
                keys = jnp.maximum(made[:more], 0.0).astype(jnp.bfloat16)
                values = made[more:].astype(jnp.bfloat16)
                full = jnp.where(same, dot(values, keys, ((1,), (1,))), 0.0)
                at = ms.index(m)
                s_ref[at, :width, 32 * k : 32 * k + 32] = full[:, :32] + full[:, 32:64] + full[:, 64:]
                s_ref[at, width + k : width + k + 1, :more] = dot(ones, keys, ((1,), (1,)))[:1]

    out = []
    if n_q:
        out.append(jax.ShapeDtypeStruct((n_q, more, count), jnp.float32))
    if ms:
        out.append(jax.ShapeDtypeStruct((len(ms), width + 16, 128), jnp.float32))
    scratch = [pltpu.VMEM((2, more + width, depth), jnp.bfloat16)]
    ins = [SMEM] + [VMEM] * (n_in + len(carried))
    extra = [a for _, (a, _) in carried]
    carried = [(m, at) for m, (_, at) in carried]
    got = list(call(body, out, ins, scratch, place, *arrays, *extra))
    return ([(order, got.pop(0))] if n_q else []) + ([(ms, got[0])] if ms else [])


def plane_sum(mine, others):
    def body(a_ref, b_ref, out_ref):
        both = a_ref[...] + b_ref[...]
        out_ref[0] = (both[0] + both[1]).astype(out_ref.dtype)
        out_ref[1] = (both[2] + both[3]).astype(out_ref.dtype)

    out = jax.ShapeDtypeStruct((2,) + mine.shape[1:], jnp.bfloat16)
    return call(body, out, [VMEM] * 2, [], mine, others)


def apply(place, half, ms, queries, mine, others, planes):
    arrays = []
    where = {}
    for m in ms:
        for k in range(4):
            a, at = queries[k, m]
            if not any(a is b for b in arrays):
                arrays.append(a)
            where[k, m] = ([a is b for b in arrays].index(True), at)
    rows, count = arrays[0].shape[1:]
    width = rows - half

    def body(place_ref, *refs):
        q_refs = refs[: len(arrays)]
        mine_ref, others_ref, *plane_refs = refs[len(arrays) : len(arrays) + 5]
        outs = refs[len(arrays) + 5 :]
        g, hi, b, lo = (place_ref[i] for i in range(4))
        same = heads_of(g, width, half)
        factor = lambda yes: jnp.where(yes, 1.0, 0.0).astype(jnp.float32)
        earlier = [factor(jnp.bitwise_xor(hi, k) < hi) for k in (1, 2, 3)]
        second = factor(lo == 1)

        def split(a):
            high = a.astype(jnp.bfloat16)
            return high, (a - high.astype(jnp.float32)).astype(jnp.bfloat16)

        for out_ref, m in zip(outs, ms):
            after = factor(jnp.bitwise_xor(b, m & 1) == 1)
            upto = mine_ref[m] + second * others_ref[m] + after * (mine_ref[m ^ 1] + others_ref[m ^ 1])
            before = [earlier[i] * plane_refs[i][m // 2].astype(jnp.float32) for i in range(3)]
            for j in range(4):
                part = upto[:width, 32 * j : 32 * j + 32]
                sums = upto[width + j : width + j + 1, :rows]
                for k in (1, 2, 3):
                    i = j ^ k
                    part += before[k - 1][:width, 32 * i : 32 * i + 32]
                    sums += before[k - 1][width + i : width + i + 1, :rows]
                state = jnp.where(same, jnp.concatenate([part] * 3, axis=1), 0.0)
                sums = jnp.where(same, jnp.broadcast_to(sums, (width, rows)), 0.0)
                left, left_low = split(jnp.concatenate([state, sums], axis=0))
                a, at = where[j, m]
                q, q_low = split(q_refs[a][at])
                both = dot(left, q, ((1,), (0,))) + dot(left_low, q, ((1,), (0,))) + dot(left, q_low, ((1,), (0,)))
                out_ref[j] = (both[:width] / (both[width:] + EPSILON)).astype(jnp.bfloat16)

    out = [jax.ShapeDtypeStruct((4, width, count), jnp.bfloat16)] * len(ms)
    ins = [SMEM] + [VMEM] * (len(arrays) + 5)
    return call(body, out, ins, [], place, *arrays, mine, others, *planes)


def assemble(place, got):
    blocks, width, count = got[0].shape

    def body(place_ref, *refs):
        *got_refs, out_ref, every = refs
        g, hi, b = (place_ref[i] for i in range(3))
        for m in range(4):
            this_g, this_b = jnp.bitwise_xor(g, m >> 1), jnp.bitwise_xor(b, m & 1)
            for k in range(blocks):
                at = ((jnp.bitwise_xor(hi, k) * 2 + this_b) * 2 + this_g) * width
                every[pl.ds(pl.multiple_of(at, 16), width)] = got_refs[m][k]
        out_ref[...] = every[...].T

    out = jax.ShapeDtypeStruct((count, 4 * blocks * width), jnp.bfloat16)
    scratch = [pltpu.VMEM((4 * blocks * width, count), jnp.bfloat16)]
    return call(body, out, [SMEM] + [VMEM] * 4, scratch, place, *got)


def shared_plan(layout, frames_in, qkv_weight):
    g = lax.axis_index("groups")
    frame = lax.axis_index("frame")
    lo, b, hi = frame % 2, (frame // 2) % 2, frame // 4
    place = jnp.stack([g, hi, b, lo]).astype(jnp.int32)
    weights = qkv_weight.transpose(0, 2, 1)
    width, depth = weights.shape[1:]
    half = HEAD_DIM // 2
    own = frames_in[0].T

    along = lambda k: layout.pairs(lambda g, hi, b, lo: (g, hi ^ k, b, lo))
    over_b = layout.pairs(lambda g, hi, b, lo: (g, hi, 1 - b, lo))
    over_g = layout.pairs(lambda g, hi, b, lo: (1 - g, hi, b, lo))
    over_gb = layout.pairs(lambda g, hi, b, lo: (1 - g, hi, 1 - b, lo))
    over_lo = layout.pairs(lambda g, hi, b, lo: (g, hi, b, 1 - lo))

    next_b = send(own, over_b)
    next_g = send(own, over_g)

    shard = weights.reshape(3 * width, depth)
    kv, q, whole, other_kv, other_q = pick(place, shard, send(shard, over_lo), half)
    far_kv = send(kv, along(2))
    far_q = send(q, along(2))
    near = send(whole, along(1))
    last_kv = send(far_kv, along(1))
    far_kv, far_q, last_kv, next_b, next_g = lax.optimization_barrier((far_kv, far_q, last_kv, next_b, next_g))
    last_q = send(far_q, along(1))

    cut = depth // 2
    across = [send(next_b[:cut], over_g), send(next_g[cut:], over_b)]
    frames = [[own], [next_b], [next_g], across]

    near_other = send(near, over_lo)
    kv_rows = kv.shape[0]
    blocks = [
        {"kv": (kv, other_kv, 0), "q": (q, other_q, 0)},
        {"kv": (near, near_other, 0), "q": (near, near_other, kv_rows)},
        {"kv": (far_kv, send(far_kv, over_lo), 0), "q": (far_q, send(far_q, over_lo), 0)},
        {"kv": (last_kv, send(last_kv, over_lo), 0), "q": (last_q, send(last_q, over_lo), 0)},
    ]
    queries = {}

    def keep(made):
        order, array = made
        queries.update({km: (array, at) for at, km in enumerate(order)})

    early = [(k, m, what) for k in range(3) for what in ("kv", "q") for m in range(3)]
    made, (_, states) = project(place, half, early, blocks, frames)
    keep(made)
    late = [(3, m, "kv") for m in range(3)] + [(k, 3, "kv") for k in range(4)]
    ((_, mine),) = project(place, half, late, blocks, frames, [(m, (states, m)) for m in range(3)])
    others = send(mine, over_lo)
    plane = plane_sum(mine, others)
    planes = [send(plane, along(k)) for k in (1, 2, 3)]
    last = [(k, 3, "q") for k in range(4)] + [(3, m, "q") for m in range(3)]
    (made,) = project(place, half, last, blocks, frames)
    keep(made)

    out1, out2, out3 = apply(place, half, [1, 2, 3], queries, mine, others, planes)
    (out0,) = apply(place, half, [0], queries, mine, others, planes)
    got = [out0, send(out1, over_b), send(out2, over_g), send(out3, over_gb)]
    return assemble(place, got)[None]


def solution(mesh):
    placed = (P(AXES, None, None), P(None, None, "frame"))

    def shards(frames_in, qkv_weight):
        width = qkv_weight.shape[2]
        if mesh.shape["groups"] == 2 and mesh.shape["frame"] == 16 and width * 2 == 5 * HEAD_DIM:
            return shared_plan(Layout(mesh), frames_in, qkv_weight)
        return gathered_plan(frames_in, qkv_weight)

    return jax.shard_map(
        shards, mesh=mesh, in_specs=placed, out_specs=P(AXES, None, None), check_vma=False
    )
```

time: 135 us -> 90.4 us (0.67)
  starting transfers between devices: 46.2 us -> 26.4 us
  local copies, waits for them, and re-layouts: 11.1 us -> 1.33 us
  waiting for transfers between devices: 51.4 us -> 43.3 us
  Pallas kernels: 25.6 us -> 19.1 us
    ppermute x25 -> x22, starting transfers between devices: 46.2 us -> 26.4 us  [send(): return lax.ppermute(a, AXES, pairs)]
    ppermute x25 -> x22, waiting for transfers between devices: 51.4 us -> 43.3 us  [send(): return lax.ppermute(a, AXES, pairs)]
    pallas_call x7 -> x8, Pallas kernels: 25.6 us -> 19.1 us  [call(): pl.pallas_call(body, out_shape=out, in_specs=ins, out_specs=jax.tree.map(...]
    unnamed x32 -> x4, local copies, waits for them, and re-layouts: 7.2 us -> 1.25 us
    slice x2, local copies, waits for them, and re-layouts: 2.75 us -> 0.08 us  [shared_plan(): across = [send(next_b[:cut], over_g), send(next_g[cut:], over_b)]]
  transfers between devices with their start and end apart: 25 -> 22, of which waited for: 11 -> 12; matrix products, arithmetic and copies ran while one was open for 3% -> 0% of each run, Pallas kernels for 12% -> 17%
where the time goes in v3:
time: 90.4 us; the launch traced here: 90.3 us
  waiting for transfers between devices  43.3 us (48%)
  starting transfers between devices  26.4 us (29%)
  Pallas kernels  19.1 us (21%)
  local copies, waits for them, and re-layouts  1.33 us (1%)
    ppermute x22, waiting for transfers between devices, send(): return lax.ppermute(a, AXES, pairs)  43.3 us
    ppermute x22, starting transfers between devices, send(): return lax.ppermute(a, AXES, pairs)  26.4 us
    pallas_call x8, Pallas kernels, call(): pl.pallas_call(body, out_shape=out, in_specs=ins, out_specs=jax.tree.map(...  19.1 us
  transfers between devices with their start and end apart: 22, of which 12 were waited for; matrix products, arithmetic and copies ran while one was open for 0% of the time, Pallas kernels for 17%

profile of v3, /device:TPU:0, one launch (start us, length us, event | category | flops | bytes accessed | tf_op | source)
XLA Modules:
  0.0 90.3 jit_solution(2194003174127162685)
XLA Ops:
  0.0 0.5 collective-permute-start
  0.5 2.5 %collective-permute-start.6 = (bf16[2240,256]{1,0:T(8,128)(2,1)}, bf16[2240,256]{1,0:T(8,128)(2,1)S(1)}, u32[]{:S(2)}, u32[]{:S(2)}) collective-permute-start(bf16[2240,256]{1,0:T(8,128)(2,1)} %bitcast.11), channel_id=1, source_target_pairs={{0,2},{1,3},{2,0},{3,1},{4,6},{5,7},{6,4},{7,5},{8,10},{9,11},{10,... | collective-permute-start | bytes 3440648 | tf_op jit(solution)/shard_map/ppermute | solution.py:60
  3.0 1.5 %collective-permute-start.7 = (bf16[2240,256]{1,0:T(8,128)(2,1)}, bf16[2240,256]{1,0:T(8,128)(2,1)S(1)}, u32[]{:S(2)}, u32[]{:S(2)}) collective-permute-start(bf16[2240,256]{1,0:T(8,128)(2,1)} %bitcast.12), channel_id=1, source_target_pairs={{0,16},{1,17},{2,18},{3,19},{4,20},{5,21},{6,22},{7,23},{8,24},{9,... | collective-permute-start | bytes 3440648 | tf_op jit(solution)/shard_map/ppermute | solution.py:60
  4.5 0.1 pad_add_fusion.place_ref
  4.5 0.0 collective-permute-done.swapped_ref
  4.5 0.0 copy-start.1
  4.5 1.2 %copy-done.1 = bf16[3,2240,80]{1,2,0:T(8,128)(2,1)S(1)} copy-done((bf16[3,2240,80]{1,2,0:T(8,128)(2,1)S(1)}, bf16[3,2240,80]{1,2,0:T(8,128)(2,1)}, u32[]{:S(2)}) %copy-start.1) | copy-done | bytes 1075224
  5.8 0.8 shard_map.28
  6.6 2.7 %collective-permute-start.3 = (bf16[176,1152]{1,0:T(8,128)(2,1)S(1)}, bf16[176,1152]{1,0:T(8,128)(2,1)S(1)}, u32[]{:S(2)}, u32[]{:S(2)}) collective-permute-start(bf16[176,1152]{1,0:T(8,128)(2,1)S(1)} %get-tuple-element.20.refs_0_.refs_2_), channel_id=1, source_target_pairs={{0,8},{1,9},{2,10},{3,11},{4,12},{5,13},{6,14},{7,15},{8,0},{9,1},... | collective-permute-start | bytes 1216520 | tf_op jit(solution)/shard_map/ppermute | solution.py:60
  9.3 1.6 %collective-permute-start.1 = (bf16[272,1152]{1,0:T(8,128)(2,1)S(1)}, bf16[272,1152]{1,0:T(8,128)(2,1)S(1)}, u32[]{:S(2)}, u32[]{:S(2)}) collective-permute-start(bf16[272,1152]{1,0:T(8,128)(2,1)S(1)} %get-tuple-element.24), channel_id=1, source_target_pairs={{0,4},{1,5},{2,6},{3,7},{4,0},{5,1},{6,2},{7,3},{8,12},{9,13},{10,... | collective-permute-start | bytes 1880072 | tf_op jit(solution)/shard_map/ppermute | solution.py:60
  10.8 16.8 %collective-permute-done.3.refs_6_ = bf16[176,1152]{1,0:T(8,128)(2,1)S(1)} collective-permute-done((bf16[176,1152]{1,0:T(8,128)(2,1)S(1)}, bf16[176,1152]{1,0:T(8,128)(2,1)S(1)}, u32[]{:S(2)}, u32[]{:S(2)}) %collective-permute-start.3) | collective-permute-done | bytes 405536 | tf_op jit(solution)/shard_map/ppermute | solution.py:60
  27.6 0.7 collective-permute-start.5
  28.3 0.0 copy-start
  28.3 3.4 %collective-permute-start.4 = (bf16[96,1152]{1,0:T(8,128)(2,1)S(1)}, bf16[96,1152]{1,0:T(8,128)(2,1)S(1)}, u32[]{:S(2)}, u32[]{:S(2)}) collective-permute-start(bf16[96,1152]{1,0:T(8,128)(2,1)S(1)} %get-tuple-element.22.refs_2_.refs_0_), channel_id=1, source_target_pairs={{0,8},{1,9},{2,10},{3,11},{4,12},{5,13},{6,14},{7,15},{8,0},{9,1},... | collective-permute-start | bytes 663560 | tf_op jit(solution)/shard_map/ppermute | solution.py:60
  31.7 6.9 %collective-permute-done.1.refs_4_.refs_2_ = bf16[272,1152]{1,0:T(8,128)(2,1)S(1)} collective-permute-done((bf16[272,1152]{1,0:T(8,128)(2,1)S(1)}, bf16[272,1152]{1,0:T(8,128)(2,1)S(1)}, u32[]{:S(2)}, u32[]{:S(2)}) %collective-permute-start.1) | collective-permute-done | bytes 626720 | tf_op jit(solution)/shard_map/ppermute | solution.py:60
  38.6 0.0 collective-permute-start.2
  38.6 0.0 collective-permute-done.6.refs_11_.refs_9_
  38.6 0.0 collective-permute-done.7.refs_12_.refs_10_
  38.6 6.4 %collective-permute-done.4.refs_8_.refs_4_ = bf16[96,1152]{1,0:T(8,128)(2,1)S(1)} collective-permute-done((bf16[96,1152]{1,0:T(8,128)(2,1)S(1)}, bf16[96,1152]{1,0:T(8,128)(2,1)S(1)}, u32[]{:S(2)}, u32[]{:S(2)}) %collective-permute-start.4) | collective-permute-done | bytes 221216 | tf_op jit(solution)/shard_map/ppermute | solution.py:60
  45.0 1.0 %collective-permute-done.5.refs_0_ = bf16[176,1152]{1,0:T(8,128)(2,1)S(1)} collective-permute-done((bf16[176,1152]{1,0:T(8,128)(2,1)S(1)}, bf16[176,1152]{1,0:T(8,128)(2,1)S(1)}, u32[]{:S(2)}, u32[]{:S(2)}) %collective-permute-start.5) | collective-permute-done | bytes 405536 | tf_op jit(solution)/shard_map/ppermute | solution.py:60
  46.0 0.0 collective-permute-start.9
  46.0 0.5 collective-permute-start.8
  46.5 1.6 %collective-permute-start.12 = (bf16[1120,256]{1,0:T(8,128)(2,1)S(1)}, bf16[1120,256]{1,0:T(8,128)(2,1)S(1)}, u32[]{:S(2)}, u32[]{:S(2)}) collective-permute-start(bf16[1120,256]{1,0:T(8,128)(2,1)S(1)} %slice.6), channel_id=1, source_target_pairs={{0,16},{1,17},{2,18},{3,19},{4,20},{5,21},{6,22},{7,23},{8,24},{9,... | collective-permute-start | bytes 1720328 | tf_op jit(solution)/shard_map/ppermute | solution.py:60
  48.2 1.6 %collective-permute-start.13 = (bf16[1120,256]{1,0:T(8,128)(2,1)S(1)}, bf16[1120,256]{1,0:T(8,128)(2,1)S(1)}, u32[]{:S(2)}, u32[]{:S(2)}) collective-permute-start(bf16[1120,256]{1,0:T(8,128)(2,1)S(1)} %slice.7), channel_id=1, source_target_pairs={{0,2},{1,3},{2,0},{3,1},{4,6},{5,7},{6,4},{7,5},{8,10},{9,11},{10,... | collective-permute-start | bytes 1720328 | tf_op jit(solution)/shard_map/ppermute | solution.py:60
  49.7 0.0 collective-permute-done.9.refs_9_.refs_5_
  49.7 0.0 collective-permute-start.14
  49.7 0.0 collective-permute-done.8.refs_7_
  49.8 1.4 %collective-permute-start.10 = (bf16[96,1152]{1,0:T(8,128)(2,1)S(1)}, bf16[96,1152]{1,0:T(8,128)(2,1)S(1)}, u32[]{:S(2)}, u32[]{:S(2)}) collective-permute-start(bf16[96,1152]{1,0:T(8,128)(2,1)S(1)} %collective-permute-done.4.refs_8_.refs_4_), channel_id=1, source_target_pairs={{0,4},{1,5},{2,6},{3,7},{4,0},{5,1},{6,2},{7,3},{8,12},{9,13},{10,... | collective-permute-start | bytes 663560 | tf_op jit(solution)/shard_map/ppermute | solution.py:60
  51.1 0.0 collective-permute-done.2.refs_5_.refs_3_
  51.1 0.0 copy-done
  51.2 7.5 %shard_map.29 = (f32[9,96,256]{2,1,0:T(8,128)S(1)}, f32[3,96,128]{2,1,0:T(8,128)S(1)}) custom-call(s32[4]{0:T(128)S(1)} %pad_add_fusion.place_ref, bf16[176,1152]{1,0:T(8,128)(2,1)S(1)} %get-tuple-element.20.refs_0_.refs_2_, bf16[176,1152]{1,0:T(8,128)(2,1)S(1)} %get-tuple-element.21.refs_1_.refs_3_, bf16[96,1152]{1,0:T(8,128)(2,1)S(1)} %get-tuple-element.22.refs_2_.refs_0_, ...), custom_call_target="tpu_custom_call" | custom-call | flops 1000 | bytes 1000 | tf_op jit(solution)/shard_map/pallas_call | solution.py:70
  58.7 0.0 collective-permute-done.14.refs_1_
  58.7 2.7 %collective-permute-done.12.refs_8_.refs_11_ = bf16[1120,256]{1,0:T(8,128)(2,1)S(1)} collective-permute-done((bf16[1120,256]{1,0:T(8,128)(2,1)S(1)}, bf16[1120,256]{1,0:T(8,128)(2,1)S(1)}, u32[]{:S(2)}, u32[]{:S(2)}) %collective-permute-start.12) | collective-permute-done | bytes 573472 | tf_op jit(solution)/shard_map/ppermute | solution.py:60
  61.5 1.4 %collective-permute-done.13.refs_9_.refs_12_ = bf16[1120,256]{1,0:T(8,128)(2,1)S(1)} collective-permute-done((bf16[1120,256]{1,0:T(8,128)(2,1)S(1)}, bf16[1120,256]{1,0:T(8,128)(2,1)S(1)}, u32[]{:S(2)}, u32[]{:S(2)}) %collective-permute-start.13) | collective-permute-done | bytes 573472 | tf_op jit(solution)/shard_map/ppermute | solution.py:60
  62.8 4.3 %shard_map.31.a_ref.refs_2_ = f32[4,96,128]{2,1,0:T(8,128)S(1)} custom-call(s32[4]{0:T(128)S(1)} %pad_add_fusion.place_ref, bf16[176,1152]{1,0:T(8,128)(2,1)S(1)} %collective-permute-done.5.refs_0_, bf16[176,1152]{1,0:T(8,128)(2,1)S(1)} %collective-permute-done.14.refs_1_, bf16[176,1152]{1,0:T(8,128)(2,1)S(1)} %get-tuple-element.20.refs_0_.refs_2_, ...), custom_call_target="tpu_custom_call" | custom-call | flops 1000 | bytes 1000 | tf_op jit(solution)/shard_map/pallas_call | solution.py:70
  67.1 0.1 collective-permute-start.15
  67.2 0.0 collective-permute-done.10.refs_6_
  67.2 0.5 collective-permute-start.11
  67.7 0.9 %collective-permute-done.15.b_ref.refs_3_ = f32[4,96,128]{2,1,0:T(8,128)S(1)} collective-permute-done((f32[4,96,128]{2,1,0:T(8,128)S(1)}, f32[4,96,128]{2,1,0:T(8,128)S(1)}, u32[]{:S(2)}, u32[]{:S(2)}) %collective-permute-start.15) | collective-permute-done | bytes 196640 | tf_op jit(solution)/shard_map/ppermute | solution.py:60
  68.7 1.4 %collective-permute-start.16 = (bf16[2,96,128]{2,1,0:T(8,128)(2,1)S(1)}, bf16[2,96,128]{2,1,0:T(8,128)(2,1)S(1)}, u32[]{:S(2)}, u32[]{:S(2)}) collective-permute-start(bf16[2,96,128]{2,1,0:T(8,128)(2,1)S(1)} %shard_map.32), channel_id=1, source_target_pairs={{0,4},{1,5},{2,6},{3,7},{4,0},{5,1},{6,2},{7,3},{8,12},{9,13},{10,... | collective-permute-start | bytes 147464 | tf_op jit(solution)/shard_map/ppermute | solution.py:60
  70.1 1.7 %collective-permute-start.17 = (bf16[2,96,128]{2,1,0:T(8,128)(2,1)S(1)}, bf16[2,96,128]{2,1,0:T(8,128)(2,1)S(1)}, u32[]{:S(2)}, u32[]{:S(2)}) collective-permute-start(bf16[2,96,128]{2,1,0:T(8,128)(2,1)S(1)} %shard_map.32), channel_id=1, source_target_pairs={{0,8},{1,9},{2,10},{3,11},{4,12},{5,13},{6,14},{7,15},{8,0},{9,1},... | collective-permute-start | bytes 147464 | tf_op jit(solution)/shard_map/ppermute | solution.py:60
  71.8 1.3 %collective-permute-start.18 = (bf16[2,96,128]{2,1,0:T(8,128)(2,1)S(1)}, bf16[2,96,128]{2,1,0:T(8,128)(2,1)S(1)}, u32[]{:S(2)}, u32[]{:S(2)}) collective-permute-start(bf16[2,96,128]{2,1,0:T(8,128)(2,1)S(1)} %shard_map.32), channel_id=1, source_target_pairs={{0,12},{1,13},{2,14},{3,15},{4,8},{5,9},{6,10},{7,11},{8,4},{9,5},... | collective-permute-start | bytes 147464 | tf_op jit(solution)/shard_map/ppermute | solution.py:60
  73.1 0.0 collective-permute-done.11.refs_7_
  73.1 2.0 %shard_map.30.refs_1_ = f32[7,96,256]{2,1,0:T(8,128)S(1)} custom-call(s32[4]{0:T(128)S(1)} %pad_add_fusion.place_ref, bf16[96,1152]{1,0:T(8,128)(2,1)S(1)} %get-tuple-element.22.refs_2_.refs_0_, bf16[96,1152]{1,0:T(8,128)(2,1)S(1)} %get-tuple-element.23.refs_3_.refs_1_, bf16[272,1152]{1,0:T(8,128)(2,1)S(1)} %collective-permute-done.1.refs_4_.refs_2_, ...), custom_call_target="tpu_custom_call" | custom-call | flops 1000 | bytes 1000 | tf_op jit(solution)/shard_map/pallas_call | solution.py:70
  75.1 0.0 collective-permute-done.16.refs_4_
  75.1 1.3 %collective-permute-done.17.refs_5_ = bf16[2,96,128]{2,1,0:T(8,128)(2,1)S(1)} collective-permute-done((bf16[2,96,128]{2,1,0:T(8,128)(2,1)S(1)}, bf16[2,96,128]{2,1,0:T(8,128)(2,1)S(1)}, u32[]{:S(2)}, u32[]{:S(2)}) %collective-permute-start.17) | collective-permute-done | bytes 49184 | tf_op jit(solution)/shard_map/ppermute | solution.py:60
  76.5 1.2 %collective-permute-done.18.refs_6_ = bf16[2,96,128]{2,1,0:T(8,128)(2,1)S(1)} collective-permute-done((bf16[2,96,128]{2,1,0:T(8,128)(2,1)S(1)}, bf16[2,96,128]{2,1,0:T(8,128)(2,1)S(1)}, u32[]{:S(2)}, u32[]{:S(2)}) %collective-permute-start.18) | collective-permute-done | bytes 49184 | tf_op jit(solution)/shard_map/ppermute | solution.py:60
  77.7 1.6 %shard_map.34 = (bf16[4,80,256]{2,1,0:T(8,128)(2,1)S(1)}, bf16[4,80,256]{2,1,0:T(8,128)(2,1)S(1)}, bf16[4,80,256]{2,1,0:T(8,128)(2,1)S(1)}) custom-call(s32[4]{0:T(128)S(1)} %pad_add_fusion.place_ref, f32[9,96,256]{2,1,0:T(8,128)S(1)} %get-tuple-element.29.refs_0_, f32[7,96,256]{2,1,0:T(8,128)S(1)} %shard_map.30.refs_1_, ...), custom_call_target="tpu_custom_call" | custom-call | flops 1000 | bytes 1000 | tf_op jit(solution)/shard_map/pallas_call | solution.py:70
  79.3 1.6 %collective-permute-start.19 = (bf16[4,80,256]{2,1,0:T(8,128)(2,1)S(1)}, bf16[4,80,256]{2,1,0:T(8,128)(2,1)S(1)}, u32[]{:S(2)}, u32[]{:S(2)}) collective-permute-start(bf16[4,80,256]{2,1,0:T(8,128)(2,1)S(1)} %get-tuple-element.32), channel_id=1, source_target_pairs={{0,2},{1,3},{2,0},{3,1},{4,6},{5,7},{6,4},{7,5},{8,10},{9,11},{10,... | collective-permute-start | bytes 491528 | tf_op jit(solution)/shard_map/ppermute | solution.py:60
  80.9 0.5 collective-permute-start.20
  81.5 1.4 %collective-permute-start.21 = (bf16[4,80,256]{2,1,0:T(8,128)(2,1)S(1)}, bf16[4,80,256]{2,1,0:T(8,128)(2,1)S(1)}, u32[]{:S(2)}, u32[]{:S(2)}) collective-permute-start(bf16[4,80,256]{2,1,0:T(8,128)(2,1)S(1)} %get-tuple-element.34), channel_id=1, source_target_pairs={{0,18},{1,19},{2,16},{3,17},{4,22},{5,23},{6,20},{7,21},{8,26},{9,... | collective-permute-start | bytes 491528 | tf_op jit(solution)/shard_map/ppermute | solution.py:60
  82.9 1.1 %shard_map.33.refs_0_ = bf16[4,80,256]{2,1,0:T(8,128)(2,1)S(1)} custom-call(s32[4]{0:T(128)S(1)} %pad_add_fusion.place_ref, f32[9,96,256]{2,1,0:T(8,128)S(1)} %get-tuple-element.29.refs_0_, f32[7,96,256]{2,1,0:T(8,128)S(1)} %shard_map.30.refs_1_, f32[4,96,128]{2,1,0:T(8,128)S(1)} %shard_map.31.a_ref.refs_2_, ...), custom_call_target="tpu_custom_call" | custom-call | flops 1000 | bytes 1000 | tf_op jit(solution)/shard_map/pallas_call | solution.py:70
  84.0 2.5 %collective-permute-done.19.refs_1_ = bf16[4,80,256]{2,1,0:T(8,128)(2,1)S(1)} collective-permute-done((bf16[4,80,256]{2,1,0:T(8,128)(2,1)S(1)}, bf16[4,80,256]{2,1,0:T(8,128)(2,1)S(1)}, u32[]{:S(2)}, u32[]{:S(2)}) %collective-permute-start.19) | collective-permute-done | bytes 163872 | tf_op jit(solution)/shard_map/ppermute | solution.py:60
  86.5 0.5 collective-permute-done.20.refs_2_
  87.0 1.7 %collective-permute-done.21.refs_3_ = bf16[4,80,256]{2,1,0:T(8,128)(2,1)S(1)} collective-permute-done((bf16[4,80,256]{2,1,0:T(8,128)(2,1)S(1)}, bf16[4,80,256]{2,1,0:T(8,128)(2,1)S(1)}, u32[]{:S(2)}, u32[]{:S(2)}) %collective-permute-start.21) | collective-permute-done | bytes 163872 | tf_op jit(solution)/shard_map/ppermute | solution.py:60
  88.6 1.7 %shard_map.35 = bf16[256,1280]{1,0:T(8,128)(2,1)} custom-call(s32[4]{0:T(128)S(1)} %pad_add_fusion.place_ref, bf16[4,80,256]{2,1,0:T(8,128)(2,1)S(1)} %shard_map.33.refs_0_, bf16[4,80,256]{2,1,0:T(8,128)(2,1)S(1)} %collective-permute-done.19.refs_1_, bf16[4,80,256]{2,1,0:T(8,128)(2,1)S(1)} %collective-permute-done.20.refs_2_, ...), custom_call_target="tpu_custom_call" | custom-call | flops 1000 | bytes 1000 | tf_op jit(solution)/shard_map/pallas_call | solution.py:70
  (3 shorter events, 0.1 us)
Async XLA Ops:
  0.0 4.5 %collective-permute-start = (bf16[240,2240]{1,0:T(8,128)(2,1)}, bf16[240,2240]{1,0:T(8,128)(2,1)S(1)}, u32[]{:S(2)}, u32[]{:S(2)}) collective-permute-start(bf16[240,2240]{1,0:T(8,128)(2,1)} %bitcast.16), channel_id=1, source_target_pairs={{0,1},{1,0},{2,3},{3,2},{4,5},{5,4},{6,7},{7,6},{8,9},{9,8},{10,11... | collective-permute-start | bytes 3225608 | tf_op jit(solution)/shard_map/ppermute | solution.py:60
  0.5 38.1 %collective-permute-start.6 = (bf16[2240,256]{1,0:T(8,128)(2,1)}, bf16[2240,256]{1,0:T(8,128)(2,1)S(1)}, u32[]{:S(2)}, u32[]{:S(2)}) collective-permute-start(bf16[2240,256]{1,0:T(8,128)(2,1)} %bitcast.11), channel_id=1, source_target_pairs={{0,2},{1,3},{2,0},{3,1},{4,6},{5,7},{6,4},{7,5},{8,10},{9,11},{10,... | collective-permute-start | bytes 3440648 | tf_op jit(solution)/shard_map/ppermute | solution.py:60
  3.0 35.6 %collective-permute-start.7 = (bf16[2240,256]{1,0:T(8,128)(2,1)}, bf16[2240,256]{1,0:T(8,128)(2,1)S(1)}, u32[]{:S(2)}, u32[]{:S(2)}) collective-permute-start(bf16[2240,256]{1,0:T(8,128)(2,1)} %bitcast.12), channel_id=1, source_target_pairs={{0,16},{1,17},{2,18},{3,19},{4,20},{5,21},{6,22},{7,23},{8,24},{9,... | collective-permute-start | bytes 3440648 | tf_op jit(solution)/shard_map/ppermute | solution.py:60
  4.5 1.2 %copy-start.1 = (bf16[3,2240,80]{1,2,0:T(8,128)(2,1)S(1)}, bf16[3,2240,80]{1,2,0:T(8,128)(2,1)}, u32[]{:S(2)}) copy-start(bf16[3,2240,80]{1,2,0:T(8,128)(2,1)} %param.3) | copy-start | bytes 3225604
  6.6 21.0 %collective-permute-start.3 = (bf16[176,1152]{1,0:T(8,128)(2,1)S(1)}, bf16[176,1152]{1,0:T(8,128)(2,1)S(1)}, u32[]{:S(2)}, u32[]{:S(2)}) collective-permute-start(bf16[176,1152]{1,0:T(8,128)(2,1)S(1)} %get-tuple-element.20.refs_0_.refs_2_), channel_id=1, source_target_pairs={{0,8},{1,9},{2,10},{3,11},{4,12},{5,13},{6,14},{7,15},{8,0},{9,1},... | collective-permute-start | bytes 1216520 | tf_op jit(solution)/shard_map/ppermute | solution.py:60
  9.3 29.3 %collective-permute-start.1 = (bf16[272,1152]{1,0:T(8,128)(2,1)S(1)}, bf16[272,1152]{1,0:T(8,128)(2,1)S(1)}, u32[]{:S(2)}, u32[]{:S(2)}) collective-permute-start(bf16[272,1152]{1,0:T(8,128)(2,1)S(1)} %get-tuple-element.24), channel_id=1, source_target_pairs={{0,4},{1,5},{2,6},{3,7},{4,0},{5,1},{6,2},{7,3},{8,12},{9,13},{10,... | collective-permute-start | bytes 1880072 | tf_op jit(solution)/shard_map/ppermute | solution.py:60
  27.6 18.4 %collective-permute-start.5 = (bf16[176,1152]{1,0:T(8,128)(2,1)S(1)}, bf16[176,1152]{1,0:T(8,128)(2,1)S(1)}, u32[]{:S(2)}, u32[]{:S(2)}) collective-permute-start(bf16[176,1152]{1,0:T(8,128)(2,1)S(1)} %collective-permute-done.3.refs_6_), channel_id=1, source_target_pairs={{0,4},{1,5},{2,6},{3,7},{4,0},{5,1},{6,2},{7,3},{8,12},{9,13},{10,... | collective-permute-start | bytes 1216520 | tf_op jit(solution)/shard_map/ppermute | solution.py:60
  28.3 22.9 %copy-start = (bf16[1,256,2240]{1,2,0:T(8,128)(2,1)S(1)}, bf16[1,256,2240]{1,2,0:T(8,128)(2,1)}, u32[]{:S(2)}) copy-start(bf16[1,256,2240]{1,2,0:T(8,128)(2,1)} %param.2) | copy-start | bytes 3440644
  28.3 16.7 %collective-permute-start.4 = (bf16[96,1152]{1,0:T(8,128)(2,1)S(1)}, bf16[96,1152]{1,0:T(8,128)(2,1)S(1)}, u32[]{:S(2)}, u32[]{:S(2)}) collective-permute-start(bf16[96,1152]{1,0:T(8,128)(2,1)S(1)} %get-tuple-element.22.refs_2_.refs_0_), channel_id=1, source_target_pairs={{0,8},{1,9},{2,10},{3,11},{4,12},{5,13},{6,14},{7,15},{8,0},{9,1},... | collective-permute-start | bytes 663560 | tf_op jit(solution)/shard_map/ppermute | solution.py:60
  38.6 12.6 %collective-permute-start.2 = (bf16[272,1152]{1,0:T(8,128)(2,1)S(1)}, bf16[272,1152]{1,0:T(8,128)(2,1)S(1)}, u32[]{:S(2)}, u32[]{:S(2)}) collective-permute-start(bf16[272,1152]{1,0:T(8,128)(2,1)S(1)} %collective-permute-done.1.refs_4_.refs_2_), channel_id=1, source_target_pairs={{0,1},{1,0},{2,3},{3,2},{4,5},{5,4},{6,7},{7,6},{8,9},{9,8},{10,11... | collective-permute-start | bytes 1880072 | tf_op jit(solution)/shard_map/ppermute | solution.py:60
  46.0 3.8 %collective-permute-start.9 = (bf16[96,1152]{1,0:T(8,128)(2,1)S(1)}, bf16[96,1152]{1,0:T(8,128)(2,1)S(1)}, u32[]{:S(2)}, u32[]{:S(2)}) collective-permute-start(bf16[96,1152]{1,0:T(8,128)(2,1)S(1)} %collective-permute-done.4.refs_8_.refs_4_), channel_id=1, source_target_pairs={{0,1},{1,0},{2,3},{3,2},{4,5},{5,4},{6,7},{7,6},{8,9},{9,8},{10,11... | collective-permute-start | bytes 663560 | tf_op jit(solution)/shard_map/ppermute | solution.py:60
  46.0 3.8 %collective-permute-start.8 = (bf16[176,1152]{1,0:T(8,128)(2,1)S(1)}, bf16[176,1152]{1,0:T(8,128)(2,1)S(1)}, u32[]{:S(2)}, u32[]{:S(2)}) collective-permute-start(bf16[176,1152]{1,0:T(8,128)(2,1)S(1)} %collective-permute-done.3.refs_6_), channel_id=1, source_target_pairs={{0,1},{1,0},{2,3},{3,2},{4,5},{5,4},{6,7},{7,6},{8,9},{9,8},{10,11... | collective-permute-start | bytes 1216520 | tf_op jit(solution)/shard_map/ppermute | solution.py:60
  46.5 15.0 %collective-permute-start.12 = (bf16[1120,256]{1,0:T(8,128)(2,1)S(1)}, bf16[1120,256]{1,0:T(8,128)(2,1)S(1)}, u32[]{:S(2)}, u32[]{:S(2)}) collective-permute-start(bf16[1120,256]{1,0:T(8,128)(2,1)S(1)} %slice.6), channel_id=1, source_target_pairs={{0,16},{1,17},{2,18},{3,19},{4,20},{5,21},{6,22},{7,23},{8,24},{9,... | collective-permute-start | bytes 1720328 | tf_op jit(solution)/shard_map/ppermute | solution.py:60
  48.2 14.7 %collective-permute-start.13 = (bf16[1120,256]{1,0:T(8,128)(2,1)S(1)}, bf16[1120,256]{1,0:T(8,128)(2,1)S(1)}, u32[]{:S(2)}, u32[]{:S(2)}) collective-permute-start(bf16[1120,256]{1,0:T(8,128)(2,1)S(1)} %slice.7), channel_id=1, source_target_pairs={{0,2},{1,3},{2,0},{3,1},{4,6},{5,7},{6,4},{7,5},{8,10},{9,11},{10,... | collective-permute-start | bytes 1720328 | tf_op jit(solution)/shard_map/ppermute | solution.py:60
  49.7 9.0 %collective-permute-start.14 = (bf16[176,1152]{1,0:T(8,128)(2,1)S(1)}, bf16[176,1152]{1,0:T(8,128)(2,1)S(1)}, u32[]{:S(2)}, u32[]{:S(2)}) collective-permute-start(bf16[176,1152]{1,0:T(8,128)(2,1)S(1)} %collective-permute-done.5.refs_0_), channel_id=1, source_target_pairs={{0,1},{1,0},{2,3},{3,2},{4,5},{5,4},{6,7},{7,6},{8,9},{9,8},{10,11... | collective-permute-start | bytes 1216520 | tf_op jit(solution)/shard_map/ppermute | solution.py:60
  49.8 17.4 %collective-permute-start.10 = (bf16[96,1152]{1,0:T(8,128)(2,1)S(1)}, bf16[96,1152]{1,0:T(8,128)(2,1)S(1)}, u32[]{:S(2)}, u32[]{:S(2)}) collective-permute-start(bf16[96,1152]{1,0:T(8,128)(2,1)S(1)} %collective-permute-done.4.refs_8_.refs_4_), channel_id=1, source_target_pairs={{0,4},{1,5},{2,6},{3,7},{4,0},{5,1},{6,2},{7,3},{8,12},{9,13},{10,... | collective-permute-start | bytes 663560 | tf_op jit(solution)/shard_map/ppermute | solution.py:60
  67.1 1.5 %collective-permute-start.15 = (f32[4,96,128]{2,1,0:T(8,128)S(1)}, f32[4,96,128]{2,1,0:T(8,128)S(1)}, u32[]{:S(2)}, u32[]{:S(2)}) collective-permute-start(f32[4,96,128]{2,1,0:T(8,128)S(1)} %shard_map.31.a_ref.refs_2_), channel_id=1, source_target_pairs={{0,1},{1,0},{2,3},{3,2},{4,5},{5,4},{6,7},{7,6},{8,9},{9,8},{10,11... | collective-permute-start | bytes 589832 | tf_op jit(solution)/shard_map/ppermute | solution.py:60
  67.2 5.9 %collective-permute-start.11 = (bf16[96,1152]{1,0:T(8,128)(2,1)S(1)}, bf16[96,1152]{1,0:T(8,128)(2,1)S(1)}, u32[]{:S(2)}, u32[]{:S(2)}) collective-permute-start(bf16[96,1152]{1,0:T(8,128)(2,1)S(1)} %collective-permute-done.10.refs_6_), channel_id=1, source_target_pairs={{0,1},{1,0},{2,3},{3,2},{4,5},{5,4},{6,7},{7,6},{8,9},{9,8},{10,11... | collective-permute-start | bytes 663560 | tf_op jit(solution)/shard_map/ppermute | solution.py:60
  68.7 6.5 %collective-permute-start.16 = (bf16[2,96,128]{2,1,0:T(8,128)(2,1)S(1)}, bf16[2,96,128]{2,1,0:T(8,128)(2,1)S(1)}, u32[]{:S(2)}, u32[]{:S(2)}) collective-permute-start(bf16[2,96,128]{2,1,0:T(8,128)(2,1)S(1)} %shard_map.32), channel_id=1, source_target_pairs={{0,4},{1,5},{2,6},{3,7},{4,0},{5,1},{6,2},{7,3},{8,12},{9,13},{10,... | collective-permute-start | bytes 147464 | tf_op jit(solution)/shard_map/ppermute | solution.py:60
  70.1 6.4 %collective-permute-start.17 = (bf16[2,96,128]{2,1,0:T(8,128)(2,1)S(1)}, bf16[2,96,128]{2,1,0:T(8,128)(2,1)S(1)}, u32[]{:S(2)}, u32[]{:S(2)}) collective-permute-start(bf16[2,96,128]{2,1,0:T(8,128)(2,1)S(1)} %shard_map.32), channel_id=1, source_target_pairs={{0,8},{1,9},{2,10},{3,11},{4,12},{5,13},{6,14},{7,15},{8,0},{9,1},... | collective-permute-start | bytes 147464 | tf_op jit(solution)/shard_map/ppermute | solution.py:60
  71.8 5.9 %collective-permute-start.18 = (bf16[2,96,128]{2,1,0:T(8,128)(2,1)S(1)}, bf16[2,96,128]{2,1,0:T(8,128)(2,1)S(1)}, u32[]{:S(2)}, u32[]{:S(2)}) collective-permute-start(bf16[2,96,128]{2,1,0:T(8,128)(2,1)S(1)} %shard_map.32), channel_id=1, source_target_pairs={{0,12},{1,13},{2,14},{3,15},{4,8},{5,9},{6,10},{7,11},{8,4},{9,5},... | collective-permute-start | bytes 147464 | tf_op jit(solution)/shard_map/ppermute | solution.py:60
  79.3 7.1 %collective-permute-start.19 = (bf16[4,80,256]{2,1,0:T(8,128)(2,1)S(1)}, bf16[4,80,256]{2,1,0:T(8,128)(2,1)S(1)}, u32[]{:S(2)}, u32[]{:S(2)}) collective-permute-start(bf16[4,80,256]{2,1,0:T(8,128)(2,1)S(1)} %get-tuple-element.32), channel_id=1, source_target_pairs={{0,2},{1,3},{2,0},{3,1},{4,6},{5,7},{6,4},{7,5},{8,10},{9,11},{10,... | collective-permute-start | bytes 491528 | tf_op jit(solution)/shard_map/ppermute | solution.py:60
  80.9 6.0 %collective-permute-start.20 = (bf16[4,80,256]{2,1,0:T(8,128)(2,1)S(1)}, bf16[4,80,256]{2,1,0:T(8,128)(2,1)S(1)}, u32[]{:S(2)}, u32[]{:S(2)}) collective-permute-start(bf16[4,80,256]{2,1,0:T(8,128)(2,1)S(1)} %get-tuple-element.33), channel_id=1, source_target_pairs={{0,16},{1,17},{2,18},{3,19},{4,20},{5,21},{6,22},{7,23},{8,24},{9,... | collective-permute-start | bytes 491528 | tf_op jit(solution)/shard_map/ppermute | solution.py:60
  81.5 7.2 %collective-permute-start.21 = (bf16[4,80,256]{2,1,0:T(8,128)(2,1)S(1)}, bf16[4,80,256]{2,1,0:T(8,128)(2,1)S(1)}, u32[]{:S(2)}, u32[]{:S(2)}) collective-permute-start(bf16[4,80,256]{2,1,0:T(8,128)(2,1)S(1)} %get-tuple-element.34), channel_id=1, source_target_pairs={{0,18},{1,19},{2,16},{3,17},{4,22},{5,23},{6,20},{7,21},{8,26},{9,... | collective-permute-start | bytes 491528 | tf_op jit(solution)/shard_map/ppermute | solution.py:60

commit v4 on v3

--- a/solution.py
+++ b/solution.py
@@ -92,12 +92,18 @@
     part = -(-depth // 256) * 128
     more = width + half
     rows = 2 * more + width
-
-    def body(place_ref, own_ref, swapped_ref, kv_ref, q_ref, all_ref, other_kv_ref, other_q_ref, full):
+    chunks = [pl.ds(width * i, width) for i in range(3)]
+
+    def body(place_ref, own_hbm, swapped_ref, kv_ref, q_ref, all_ref, other_kv_ref, other_q_ref, full, own_ref, sems):
+        reads = [pltpu.make_async_copy(own_hbm.at[r], own_ref.at[r], sems.at[i]) for i, r in enumerate(chunks)]
+        for read in reads:
+            read.start()
         g, lo = place_ref[0], place_ref[3]
         mine = lo == g
         full[:, 2 * part - 128 :] = jnp.zeros((rows, 128), full.dtype)
         at = pl.multiple_of(g * (width - half), 16)
+        for read in reads:
+            read.wait()
         for start, which in ((0, 1), (more, 2), (more + width, 0)):
             shard = pl.ds(which * width, width)
             full[start : start + width, :depth] = jnp.where(mine, own_ref[shard], swapped_ref[shard])
@@ -114,11 +120,16 @@
 
     shape = lambda n: jax.ShapeDtypeStruct((n, part), own.dtype)
     out = [shape(more + width), shape(more), shape(rows), shape(more + width), shape(more)]
-    return call(body, out, [SMEM, VMEM, VMEM], [pltpu.VMEM((rows, 2 * part), own.dtype)], place, own, swapped)
-
-
-def project(place, half, jobs, blocks, frames, carried=()):
-    arrays = []
+    scratch = [
+        pltpu.VMEM((rows, 2 * part), own.dtype),
+        pltpu.VMEM(own.shape, own.dtype),
+        pltpu.SemaphoreType.DMA((len(chunks),)),
+    ]
+    return call(body, out, [SMEM, ANY, VMEM], scratch, place, own, swapped)
+
+
+def project(place, half, jobs, blocks, frames, carried=(), keep=False, given=None):
+    arrays, pieces, rows = [], {}, 0
 
     def index(a):
         for i, b in enumerate(arrays):
@@ -127,71 +138,87 @@
         arrays.append(a)
         return len(arrays) - 1
 
-    count = frames[jobs[0][1]][0].shape[1]
-    depth = sum(p.shape[0] for p in frames[jobs[0][1]])
-    part = blocks[jobs[0][0]][jobs[0][2]][0].shape[1]
-    n_q = sum(what == "q" for _, _, what in jobs)
-    ms = sorted({m for _, m, what in jobs if what == "kv"} | {m for m, _ in carried})
     more = 3 * HEAD_DIM
     width = more - half
-    used = {}
-    for k, m, what in jobs:
-        one, two, first = blocks[k][what]
-        used.setdefault((k, what), (index(one), index(two), first, []))[3].append(m)
-    parts = {m: [index(p) for p in frames[m]] for _, m, _ in jobs}
-    places, order = {}, []
-    for (k, what), (_, _, _, on) in used.items():
-        for m in on:
-            if what == "q":
-                places[k, m] = len(order)
-                order.append((k, m))
+    tall = {"kv": more + width, "q": more}
+    for named, ms in jobs:
+        for k, what in named:
+            if (k, what) not in pieces:
+                chunks = [(index(one), index(two), *at) for one, two, *at in blocks[k][what]]
+                pieces[k, what] = (chunks, rows)
+                rows += tall[what]
+    if given is not None:
+        pieces, rows = given[0], 0
+    parts = {m: [index(p) for p in frames[m]] for _, ms in jobs for m in ms}
+    count = frames[0][0].shape[1]
+    depth = frames[0][0].shape[0]
+    part = arrays[0].shape[1]
+    if given is not None:
+        arrays = [given[1]]
+        parts = {m: [index(p) for p in frames[m]] for _, ms in jobs for m in ms}
+    held = sorted({m for named, ms in jobs for m in ms if any(w == "kv" for _, w in named)} | {m for m, _, _ in carried})
+    places = {}
+    for named, ms in jobs:
+        for m in ms:
+            for k, what in named:
+                if what == "q":
+                    places[k, m] = len(places)
     n_in = len(arrays)
 
     def body(place_ref, *refs):
         ins, refs = refs[:n_in], list(refs[n_in:])
         c_refs = [refs.pop(0) for _ in carried]
-        q_ref = refs.pop(0) if n_q else None
-        s_ref = refs.pop(0) if ms else None
-        (w_all,) = refs
+        q_ref = refs.pop(0) if places else None
+        s_ref = refs.pop(0) if held else None
+        w_ref = refs.pop(0) if given is None else ins[0]
         g, lo = place_ref[0], place_ref[3]
         first_half = lo == 0
-        if ms:
+        if held:
             same = heads_of(g, width, half)
             ones = jnp.ones((8, count), jnp.bfloat16)
             s_ref[...] = jnp.zeros_like(s_ref)
-            for (m, a), c_ref in zip(carried, c_refs):
-                s_ref[ms.index(m)] = c_ref[a]
-        for i, ((k, what), (one, two, first, on)) in enumerate(used.items()):
-            n = more if what == "q" else more + width
-            w_ref = w_all.at[i % 2]
-            one, two = ins[one][first : first + n], ins[two][first : first + n]
-            w_ref[:n, :part] = jnp.where(first_half, one, two)
-            w_ref[:n, part:] = jnp.where(first_half, two, one)[:, : depth - part]
-            for m in on:
+            for (m, _, at), c_ref in zip(carried, c_refs):
+                s_ref[held.index(m)] = c_ref[at]
+        for chunks, at in [] if given is not None else pieces.values():
+            for one, two, first, second, n in chunks:
+                one, two = ins[one][first : first + n], ins[two][second : second + n]
+                w_ref[at : at + n, :part] = jnp.where(first_half, one, two)
+                w_ref[at : at + n, part:] = jnp.where(first_half, two, one)[:, : depth - part]
+                at += n
+        for named, ms in jobs:
+            start = pieces[named[0]][1]
+            stop = pieces[named[-1]][1] + tall[named[-1][1]]
+            for m in ms:
                 x = [ins[p][...] for p in parts[m]]
                 x = jnp.concatenate(x, axis=0) if len(x) > 1 else x[0]
-                made = dot(w_ref[:n], x, ((1,), (0,)))
-                if what == "q":
-                    q_ref[places[k, m]] = jnp.maximum(made, 0.0)
-                    continue
-                keys = jnp.maximum(made[:more], 0.0).astype(jnp.bfloat16)
-                values = made[more:].astype(jnp.bfloat16)
-                full = jnp.where(same, dot(values, keys, ((1,), (1,))), 0.0)
-                at = ms.index(m)
-                s_ref[at, :width, 32 * k : 32 * k + 32] = full[:, :32] + full[:, 32:64] + full[:, 64:]
-                s_ref[at, width + k : width + k + 1, :more] = dot(ones, keys, ((1,), (1,)))[:1]
+                all_made = dot(w_ref[start:stop], x, ((1,), (0,)))
+                for k, what in named:
+                    at = pieces[k, what][1] - start
+                    made = all_made[at : at + tall[what]]
+                    if what == "q":
+                        q_ref[places[k, m]] = jnp.maximum(made, 0.0)
+                        continue
+                    keys = jnp.maximum(made[:more], 0.0).astype(jnp.bfloat16)
+                    values = made[more:].astype(jnp.bfloat16)
+                    full = jnp.where(same, dot(values, keys, ((1,), (1,))), 0.0)
+                    at = held.index(m)
+                    s_ref[at, :width, 32 * k : 32 * k + 32] = full[:, :32] + full[:, 32:64] + full[:, 64:]
+                    s_ref[at, width + k : width + k + 1, :more] = dot(ones, keys, ((1,), (1,)))[:1]
 
     out = []
-    if n_q:
-        out.append(jax.ShapeDtypeStruct((n_q, more, count), jnp.float32))
-    if ms:
-        out.append(jax.ShapeDtypeStruct((len(ms), width + 16, 128), jnp.float32))
-    scratch = [pltpu.VMEM((2, more + width, depth), jnp.bfloat16)]
+    if places:
+        out.append(jax.ShapeDtypeStruct((len(places), more, count), jnp.float32))
+    if held:
+        out.append(jax.ShapeDtypeStruct((len(held), width + 16, 128), jnp.float32))
+    scratch = []
+    if keep:
+        out.append(jax.ShapeDtypeStruct((rows, depth), jnp.bfloat16))
+    elif given is None:
+        scratch.append(pltpu.VMEM((rows, depth), jnp.bfloat16))
     ins = [SMEM] + [VMEM] * (n_in + len(carried))
-    extra = [a for _, (a, _) in carried]
-    carried = [(m, at) for m, (_, at) in carried]
-    got = list(call(body, out, ins, scratch, place, *arrays, *extra))
-    return ([(order, got.pop(0))] if n_q else []) + ([(ms, got[0])] if ms else [])
+    got = list(call(body, out, ins, scratch, place, *arrays, *[a for _, a, _ in carried]))
+    made = ([(places, got.pop(0))] if places else []) + ([(held, got.pop(0))] if held else [])
+    return made + ([(pieces, got[0])] if keep else [])
 
 
 def plane_sum(mine, others):
@@ -202,6 +229,22 @@
 
     out = jax.ShapeDtypeStruct((2,) + mine.shape[1:], jnp.bfloat16)
     return call(body, out, [VMEM] * 2, [], mine, others)
+
+
+def turn(a, k):
+    lanes = [a[..., 32 * (j ^ k) : 32 * (j ^ k) + 32] for j in range(4)]
+    rows = a.shape[-2] - 16
+    sums = [a[..., rows + (j ^ k) : rows + (j ^ k) + 1, :] for j in range(4)]
+    return jnp.concatenate([jnp.concatenate(lanes, axis=-1)[..., :rows, :], *sums, a[..., rows + 4 :, :]], axis=-2)
+
+
+def pair_sum(plane, near):
+    def body(a_ref, b_ref, out_ref):
+        for i in range(2):
+            both = a_ref[i].astype(jnp.float32) + turn(b_ref[i].astype(jnp.float32), 1)
+            out_ref[i] = both.astype(out_ref.dtype)
+
+    return call(body, jax.ShapeDtypeStruct(plane.shape, plane.dtype), [VMEM] * 2, [], plane, near)
 
 
 def apply(place, half, ms, queries, mine, others, planes):
@@ -218,12 +261,11 @@
 
     def body(place_ref, *refs):
         q_refs = refs[: len(arrays)]
-        mine_ref, others_ref, *plane_refs = refs[len(arrays) : len(arrays) + 5]
-        outs = refs[len(arrays) + 5 :]
+        mine_ref, others_ref = refs[len(arrays) : len(arrays) + 2]
+        plane_refs, outs = refs[len(arrays) + 2 : -len(ms)], refs[-len(ms) :]
         g, hi, b, lo = (place_ref[i] for i in range(4))
         same = heads_of(g, width, half)
         factor = lambda yes: jnp.where(yes, 1.0, 0.0).astype(jnp.float32)
-        earlier = [factor(jnp.bitwise_xor(hi, k) < hi) for k in (1, 2, 3)]
         second = factor(lo == 1)
 
         def split(a):
@@ -233,14 +275,11 @@
         for out_ref, m in zip(outs, ms):
             after = factor(jnp.bitwise_xor(b, m & 1) == 1)
             upto = mine_ref[m] + second * others_ref[m] + after * (mine_ref[m ^ 1] + others_ref[m ^ 1])
-            before = [earlier[i] * plane_refs[i][m // 2].astype(jnp.float32) for i in range(3)]
+            for ref, (_, k, adds) in zip(plane_refs, planes):
+                upto += factor(adds(hi)) * turn(ref[m // 2].astype(jnp.float32), k)
             for j in range(4):
                 part = upto[:width, 32 * j : 32 * j + 32]
                 sums = upto[width + j : width + j + 1, :rows]
-                for k in (1, 2, 3):
-                    i = j ^ k
-                    part += before[k - 1][:width, 32 * i : 32 * i + 32]
-                    sums += before[k - 1][width + i : width + i + 1, :rows]
                 state = jnp.where(same, jnp.concatenate([part] * 3, axis=1), 0.0)
                 sums = jnp.where(same, jnp.broadcast_to(sums, (width, rows)), 0.0)
                 left, left_low = split(jnp.concatenate([state, sums], axis=0))
@@ -250,8 +289,8 @@
                 out_ref[j] = (both[:width] / (both[width:] + EPSILON)).astype(jnp.bfloat16)
 
     out = [jax.ShapeDtypeStruct((4, width, count), jnp.bfloat16)] * len(ms)
-    ins = [SMEM] + [VMEM] * (len(arrays) + 5)
-    return call(body, out, ins, [], place, *arrays, mine, others, *planes)
+    ins = [SMEM] + [VMEM] * (len(arrays) + 2 + len(planes))
+    return call(body, out, ins, [], place, *arrays, mine, others, *[p for p, _, _ in planes])
 
 
 def assemble(place, got):
@@ -290,50 +329,57 @@
 
     next_b = send(own, over_b)
     next_g = send(own, over_g)
-
     shard = weights.reshape(3 * width, depth)
     kv, q, whole, other_kv, other_q = pick(place, shard, send(shard, over_lo), half)
+    more, kv_rows = q.shape[0], kv.shape[0]
+    queries = {}
+
+    def keep(made):
+        places, array = made
+        queries.update({km: (array, at) for km, at in places.items()})
+
+    def swapped(a, first=0, rows=None):
+        if rows is None:
+            return [(a, send(a, over_lo), 0, 0, a.shape[0])]
+        return [(a, send(a[first : first + rows], over_lo), first, 0, rows)]
+
     far_kv = send(kv, along(2))
     far_q = send(q, along(2))
     near = send(whole, along(1))
+    next_b, next_g = lax.optimization_barrier((next_b, next_g))
     last_kv = send(far_kv, along(1))
-    far_kv, far_q, last_kv, next_b, next_g = lax.optimization_barrier((far_kv, far_q, last_kv, next_b, next_g))
-    last_q = send(far_q, along(1))
-
     cut = depth // 2
     across = [send(next_b[:cut], over_g), send(next_g[cut:], over_b)]
     frames = [[own], [next_b], [next_g], across]
-
-    near_other = send(near, over_lo)
-    kv_rows = kv.shape[0]
-    blocks = [
-        {"kv": (kv, other_kv, 0), "q": (q, other_q, 0)},
-        {"kv": (near, near_other, 0), "q": (near, near_other, kv_rows)},
-        {"kv": (far_kv, send(far_kv, over_lo), 0), "q": (far_q, send(far_q, over_lo), 0)},
-        {"kv": (last_kv, send(last_kv, over_lo), 0), "q": (last_q, send(last_q, over_lo), 0)},
-    ]
-    queries = {}
-
-    def keep(made):
-        order, array = made
-        queries.update({km: (array, at) for at, km in enumerate(order)})
-
-    early = [(k, m, what) for k in range(3) for what in ("kv", "q") for m in range(3)]
-    made, (_, states) = project(place, half, early, blocks, frames)
+    blocks = [{"kv": [(kv, other_kv, 0, 0, kv_rows)], "q": [(q, other_q, 0, 0, more)]} for _ in range(4)]
+    blocks[2]["kv"] = swapped(far_kv)
+    blocks[1]["kv"] = swapped(near, 0, kv_rows)
+    jobs = [([(k, "kv") for k in range(3)] + [(0, "q")], [0, 1, 2])]
+    made, (_, states), given = project(place, half, jobs, blocks, frames, keep=True)
     keep(made)
-    late = [(3, m, "kv") for m in range(3)] + [(k, 3, "kv") for k in range(4)]
-    ((_, mine),) = project(place, half, late, blocks, frames, [(m, (states, m)) for m in range(3)])
+    *across, states = lax.optimization_barrier((*across, states))
+    frames[3] = across
+    ((_, states_3),) = project(place, half, [([(k, "kv") for k in range(3)], [3])], blocks, frames, given=given)
+    last_kv, states_3 = lax.optimization_barrier((last_kv, states_3))
+    blocks[3]["kv"] = swapped(last_kv)
+    last_q = send(far_q, along(1))
+    blocks[2]["q"], blocks[3]["q"] = swapped(far_q), swapped(last_q)
+    blocks[1]["q"] = swapped(near, kv_rows, more)
+    carried = [(m, states, m) for m in range(3)] + [(3, states_3, 0)]
+    ((_, mine),) = project(place, half, [([(3, "kv")], [0, 1, 2, 3])], blocks, frames, carried)
     others = send(mine, over_lo)
     plane = plane_sum(mine, others)
-    planes = [send(plane, along(k)) for k in (1, 2, 3)]
-    last = [(k, 3, "q") for k in range(4)] + [(3, m, "q") for m in range(3)]
+    planes = [(send(plane, along(k)), k, lambda hi, k=k: jnp.bitwise_xor(hi, k) < hi) for k in (1, 2, 3)]
+    last = [([(k, "q") for k in range(4)], [3]), ([(k, "q") for k in (1, 2, 3)], [0, 1, 2])]
     (made,) = project(place, half, last, blocks, frames)
     keep(made)
 
     out1, out2, out3 = apply(place, half, [1, 2, 3], queries, mine, others, planes)
     (out0,) = apply(place, half, [0], queries, mine, others, planes)
-    got = [out0, send(out1, over_b), send(out2, over_g), send(out3, over_gb)]
-    return assemble(place, got)[None]
+    out1 = send(out1, over_b)
+    out2 = send(out2, over_g)
+    out3 = send(out3, over_gb)
+    return assemble(place, [out0, out1, out2, out3])[None]
 
 
 def solution(mesh):

time: 90.4 us -> 80.8 us (0.89)
  waiting for transfers between devices: 43.3 us -> 34.2 us
  Pallas kernels: 19.1 us -> 17.6 us
    ppermute x22 -> x23, waiting for transfers between devices: 43.3 us -> 34.2 us  [send(): return lax.ppermute(a, AXES, pairs)]
    pallas_call x8 -> x9, Pallas kernels: 19.1 us -> 17.6 us  [call(): pl.pallas_call(body, out_shape=out, in_specs=ins, out_specs=jax.tree.map(...]
    ppermute x22 -> x23, starting transfers between devices: 26.4 us -> 27.3 us  [send(): return lax.ppermute(a, AXES, pairs)]
  transfers between devices with their start and end apart: 22 -> 23, of which waited for: 12 -> 11; matrix products, arithmetic and copies ran while one was open for 0% -> 0% of each run, Pallas kernels for 17% -> 18%
where the time goes in v4:
time: 80.8 us; the launch traced here: 80.7 us
  waiting for transfers between devices  34.2 us (42%)
  starting transfers between devices  27.3 us (34%)
  Pallas kernels  17.6 us (22%)
  local copies, waits for them, and re-layouts  1.38 us (2%)
    ppermute x23, waiting for transfers between devices, send(): return lax.ppermute(a, AXES, pairs)  34.2 us
    ppermute x23, starting transfers between devices, send(): return lax.ppermute(a, AXES, pairs)  27.3 us
    pallas_call x9, Pallas kernels, call(): pl.pallas_call(body, out_shape=out, in_specs=ins, out_specs=jax.tree.map(...  17.6 us
  transfers between devices with their start and end apart: 23, of which 11 were waited for; matrix products, arithmetic and copies ran while one was open for 0% of the time, Pallas kernels for 18%

profile of v4, /device:TPU:0, one launch (start us, length us, event | category | flops | bytes accessed | tf_op | source)
XLA Modules:
  0.0 80.7 jit_solution(5366552461502982076)
XLA Ops:
  0.0 0.5 collective-permute-start
  0.5 2.5 %collective-permute-start.5 = (bf16[2240,256]{1,0:T(8,128)(2,1)}, bf16[2240,256]{1,0:T(8,128)(2,1)S(1)}, u32[]{:S(2)}, u32[]{:S(2)}) collective-permute-start(bf16[2240,256]{1,0:T(8,128)(2,1)} %bitcast.11), channel_id=1, source_target_pairs={{0,2},{1,3},{2,0},{3,1},{4,6},{5,7},{6,4},{7,5},{8,10},{9,11},{10,... | collective-permute-start | bytes 3440648 | tf_op jit(solution)/shard_map/ppermute | solution.py:60
  3.0 1.5 %collective-permute-start.6 = (bf16[2240,256]{1,0:T(8,128)(2,1)}, bf16[2240,256]{1,0:T(8,128)(2,1)S(1)}, u32[]{:S(2)}, u32[]{:S(2)}) collective-permute-start(bf16[2240,256]{1,0:T(8,128)(2,1)} %bitcast.12), channel_id=1, source_target_pairs={{0,16},{1,17},{2,18},{3,19},{4,20},{5,21},{6,22},{7,23},{8,24},{9,... | collective-permute-start | bytes 3440648 | tf_op jit(solution)/shard_map/ppermute | solution.py:60
  4.5 0.1 pad_add_fusion.place_ref
  4.5 0.0 collective-permute-done.swapped_ref
  4.5 0.0 copy-start.1
  4.5 1.2 %copy-done.1 = bf16[3,2240,80]{1,2,0:T(8,128)(2,1)S(1)} copy-done((bf16[3,2240,80]{1,2,0:T(8,128)(2,1)S(1)}, bf16[3,2240,80]{1,2,0:T(8,128)(2,1)}, u32[]{:S(2)}) %copy-start.1) | copy-done | bytes 1075224
  5.8 1.3 %shard_map.28 = (bf16[176,1152]{1,0:T(8,128)(2,1)S(1)}, bf16[96,1152]{1,0:T(8,128)(2,1)S(1)}, bf16[272,1152]{1,0:T(8,128)(2,1)S(1)}, bf16[176,1152]{1,0:T(8,128)(2,1)S(1)}, bf16[96,1152]{1,0:T(8,128)(2,1)S(1)}) custom-call(s32[4]{0:T(128)S(1)} %pad_add_fusion.place_ref, bf16[240,2240]{1,0:T(8,128)(2,1)S(1)} %bitcast.17, ...), custom_call_target="tpu_custom_call" | custom-call | flops 1000 | bytes 1000 | tf_op jit(solution)/shard_map/pallas_call | solution.py:70
  7.1 1.6 %collective-permute-start.1 = (bf16[272,1152]{1,0:T(8,128)(2,1)S(1)}, bf16[272,1152]{1,0:T(8,128)(2,1)S(1)}, u32[]{:S(2)}, u32[]{:S(2)}) collective-permute-start(bf16[272,1152]{1,0:T(8,128)(2,1)S(1)} %get-tuple-element.25), channel_id=1, source_target_pairs={{0,4},{1,5},{2,6},{3,7},{4,0},{5,1},{6,2},{7,3},{8,12},{9,13},{10,... | collective-permute-start | bytes 1880072 | tf_op jit(solution)/shard_map/ppermute | solution.py:60
  8.7 2.6 %collective-permute-start.3 = (bf16[176,1152]{1,0:T(8,128)(2,1)S(1)}, bf16[176,1152]{1,0:T(8,128)(2,1)S(1)}, u32[]{:S(2)}, u32[]{:S(2)}) collective-permute-start(bf16[176,1152]{1,0:T(8,128)(2,1)S(1)} %get-tuple-element.23.refs_0_), channel_id=1, source_target_pairs={{0,8},{1,9},{2,10},{3,11},{4,12},{5,13},{6,14},{7,15},{8,0},{9,1},... | collective-permute-start | bytes 1216520 | tf_op jit(solution)/shard_map/ppermute | solution.py:60
  11.3 17.8 %collective-permute-done.5.refs_9_.refs_11_.refs_3_ = bf16[2240,256]{1,0:T(8,128)(2,1)S(1)} collective-permute-done((bf16[2240,256]{1,0:T(8,128)(2,1)}, bf16[2240,256]{1,0:T(8,128)(2,1)S(1)}, u32[]{:S(2)}, u32[]{:S(2)}) %collective-permute-start.5) | collective-permute-done | bytes 1146912 | tf_op jit(solution)/shard_map/ppermute | solution.py:60
  29.1 1.5 %collective-permute-done.6.refs_10_.refs_12_.refs_4_ = bf16[2240,256]{1,0:T(8,128)(2,1)S(1)} collective-permute-done((bf16[2240,256]{1,0:T(8,128)(2,1)}, bf16[2240,256]{1,0:T(8,128)(2,1)S(1)}, u32[]{:S(2)}, u32[]{:S(2)}) %collective-permute-start.6) | collective-permute-done | bytes 1146912 | tf_op jit(solution)/shard_map/ppermute | solution.py:60
  30.6 0.0 copy-start
  30.6 1.6 %collective-permute-start.12 = (bf16[1120,256]{1,0:T(8,128)(2,1)S(1)}, bf16[1120,256]{1,0:T(8,128)(2,1)S(1)}, u32[]{:S(2)}, u32[]{:S(2)}) collective-permute-start(bf16[1120,256]{1,0:T(8,128)(2,1)S(1)} %slice.14), channel_id=1, source_target_pairs={{0,16},{1,17},{2,18},{3,19},{4,20},{5,21},{6,22},{7,23},{8,24},{9,... | collective-permute-start | bytes 1720328 | tf_op jit(solution)/shard_map/ppermute | solution.py:60
  32.2 0.6 collective-permute-start.13
  32.8 0.0 collective-permute-done.3.refs_4_
  32.8 0.0 collective-permute-start.4
  32.8 0.0 collective-permute-done.1.refs_2_
  32.9 0.6 collective-permute-start.2
  33.4 1.7 %collective-permute-start.14 = (bf16[176,1152]{1,0:T(8,128)(2,1)S(1)}, bf16[176,1152]{1,0:T(8,128)(2,1)S(1)}, u32[]{:S(2)}, u32[]{:S(2)}) collective-permute-start(bf16[176,1152]{1,0:T(8,128)(2,1)S(1)} %collective-permute-done.3.refs_4_), channel_id=1, source_target_pairs={{0,4},{1,5},{2,6},{3,7},{4,0},{5,1},{6,2},{7,3},{8,12},{9,13},{10,... | collective-permute-start | bytes 1216520 | tf_op jit(solution)/shard_map/ppermute | solution.py:60
  35.1 0.0 collective-permute-done.4.refs_5_
  35.1 2.5 %collective-permute-start.8 = (bf16[96,1152]{1,0:T(8,128)(2,1)S(1)}, bf16[96,1152]{1,0:T(8,128)(2,1)S(1)}, u32[]{:S(2)}, u32[]{:S(2)}) collective-permute-start(bf16[96,1152]{1,0:T(8,128)(2,1)S(1)} %get-tuple-element.26.refs_6_.refs_0_), channel_id=1, source_target_pairs={{0,8},{1,9},{2,10},{3,11},{4,12},{5,13},{6,14},{7,15},{8,0},{9,1},... | collective-permute-start | bytes 663560 | tf_op jit(solution)/shard_map/ppermute | solution.py:60
  37.6 0.0 collective-permute-done.2.refs_3_
  37.6 0.0 copy-done
  37.6 5.0 %shard_map.29 = (f32[3,96,256]{2,1,0:T(8,128)S(1)}, f32[3,96,128]{2,1,0:T(8,128)S(1)}, bf16[624,2240]{1,0:T(8,128)(2,1)S(1)}) custom-call(s32[4]{0:T(128)S(1)} %pad_add_fusion.place_ref, bf16[176,1152]{1,0:T(8,128)(2,1)S(1)} %get-tuple-element.23.refs_0_, bf16[176,1152]{1,0:T(8,128)(2,1)S(1)} %get-tuple-element.24.refs_1_, ...), custom_call_target="tpu_custom_call" | custom-call | flops 1000 | bytes 1000 | tf_op jit(solution)/shard_map/pallas_call | solution.py:70
  42.6 2.4 %collective-permute-done.12.refs_8_.refs_1_.refs_5_ = bf16[1120,256]{1,0:T(8,128)(2,1)S(1)} collective-permute-done((bf16[1120,256]{1,0:T(8,128)(2,1)S(1)}, bf16[1120,256]{1,0:T(8,128)(2,1)S(1)}, u32[]{:S(2)}, u32[]{:S(2)}) %collective-permute-start.12) | collective-permute-done | bytes 573472 | tf_op jit(solution)/shard_map/ppermute | solution.py:60
  45.0 1.3 %collective-permute-done.13.refs_9_.refs_2_.refs_6_ = bf16[1120,256]{1,0:T(8,128)(2,1)S(1)} collective-permute-done((bf16[1120,256]{1,0:T(8,128)(2,1)S(1)}, bf16[1120,256]{1,0:T(8,128)(2,1)S(1)}, u32[]{:S(2)}, u32[]{:S(2)}) %collective-permute-start.13) | collective-permute-done | bytes 573472 | tf_op jit(solution)/shard_map/ppermute | solution.py:60
  46.3 1.7 %shard_map.31.refs_10_ = f32[1,96,128]{2,1,0:T(8,128)S(1)} custom-call(s32[4]{0:T(128)S(1)} %pad_add_fusion.place_ref, bf16[624,2240]{1,0:T(8,128)(2,1)S(1)} %get-tuple-element.34.refs_0_, bf16[1120,256]{1,0:T(8,128)(2,1)S(1)} %collective-permute-done.12.refs_8_.refs_1_.refs_5_, bf16[1120,256]{1,0:T(8,128)(2,1)S(1)} %collective-permute-done.13.refs_9_.refs_2_.refs_6_), custom_call_target="tpu_custom_call" | custom-call | flops 1000 | bytes 1000 | tf_op jit(solution)/shard_map/pallas_call | solution.py:70
  48.0 1.5 %collective-permute-done.14.refs_0_ = bf16[176,1152]{1,0:T(8,128)(2,1)S(1)} collective-permute-done((bf16[176,1152]{1,0:T(8,128)(2,1)S(1)}, bf16[176,1152]{1,0:T(8,128)(2,1)S(1)}, u32[]{:S(2)}, u32[]{:S(2)}) %collective-permute-start.14) | collective-permute-done | bytes 405536 | tf_op jit(solution)/shard_map/ppermute | solution.py:60
  49.5 0.0 collective-permute-start.15
  49.5 0.0 collective-permute-done.8.refs_4_
  49.5 2.6 %collective-permute-start.10 = (bf16[96,1152]{1,0:T(8,128)(2,1)S(1)}, bf16[96,1152]{1,0:T(8,128)(2,1)S(1)}, u32[]{:S(2)}, u32[]{:S(2)}) collective-permute-start(bf16[96,1152]{1,0:T(8,128)(2,1)S(1)} %collective-permute-done.8.refs_4_), channel_id=1, source_target_pairs={{0,4},{1,5},{2,6},{3,7},{4,0},{5,1},{6,2},{7,3},{8,12},{9,13},{10,... | collective-permute-start | bytes 663560 | tf_op jit(solution)/shard_map/ppermute | solution.py:60
  52.1 0.0 collective-permute-start.9
  52.1 0.0 collective-permute-done.15.refs_1_
  52.1 3.0 %shard_map.32.a_ref.refs_2_ = f32[4,96,128]{2,1,0:T(8,128)S(1)} custom-call(s32[4]{0:T(128)S(1)} %pad_add_fusion.place_ref, bf16[176,1152]{1,0:T(8,128)(2,1)S(1)} %collective-permute-done.14.refs_0_, bf16[176,1152]{1,0:T(8,128)(2,1)S(1)} %collective-permute-done.15.refs_1_, bf16[2240,256]{1,0:T(8,128)(2,1)S(1)} %bitcast.14, ...), custom_call_target="tpu_custom_call" | custom-call | flops 1000 | bytes 1000 | tf_op jit(solution)/shard_map/pallas_call | solution.py:70
  55.1 0.6 collective-permute-start.16
  55.7 1.7 %collective-permute-done.10.refs_6_ = bf16[96,1152]{1,0:T(8,128)(2,1)S(1)} collective-permute-done((bf16[96,1152]{1,0:T(8,128)(2,1)S(1)}, bf16[96,1152]{1,0:T(8,128)(2,1)S(1)}, u32[]{:S(2)}, u32[]{:S(2)}) %collective-permute-start.10) | collective-permute-done | bytes 221216 | tf_op jit(solution)/shard_map/ppermute | solution.py:60
  57.4 0.0 collective-permute-start.11
  57.4 0.6 collective-permute-start.7
  58.0 0.0 collective-permute-done.16.b_ref.refs_3_
  58.0 1.4 %collective-permute-start.17 = (bf16[2,96,128]{2,1,0:T(8,128)(2,1)S(1)}, bf16[2,96,128]{2,1,0:T(8,128)(2,1)S(1)}, u32[]{:S(2)}, u32[]{:S(2)}) collective-permute-start(bf16[2,96,128]{2,1,0:T(8,128)(2,1)S(1)} %shard_map.33), channel_id=1, source_target_pairs={{0,4},{1,5},{2,6},{3,7},{4,0},{5,1},{6,2},{7,3},{8,12},{9,13},{10,... | collective-permute-start | bytes 147464 | tf_op jit(solution)/shard_map/ppermute | solution.py:60
  59.4 2.9 %collective-permute-start.18 = (bf16[2,96,128]{2,1,0:T(8,128)(2,1)S(1)}, bf16[2,96,128]{2,1,0:T(8,128)(2,1)S(1)}, u32[]{:S(2)}, u32[]{:S(2)}) collective-permute-start(bf16[2,96,128]{2,1,0:T(8,128)(2,1)S(1)} %shard_map.33), channel_id=1, source_target_pairs={{0,8},{1,9},{2,10},{3,11},{4,12},{5,13},{6,14},{7,15},{8,0},{9,1},... | collective-permute-start | bytes 147464 | tf_op jit(solution)/shard_map/ppermute | solution.py:60
  62.2 0.0 collective-permute-done.9.refs_5_
  62.2 0.2 collective-permute-start.19
  62.5 0.0 collective-permute-done.11.refs_7_
  62.5 0.0 collective-permute-done.7.refs_3_
  62.5 2.3 %shard_map.30.refs_1_ = f32[13,96,256]{2,1,0:T(8,128)S(1)} custom-call(s32[4]{0:T(128)S(1)} %pad_add_fusion.place_ref, bf16[96,1152]{1,0:T(8,128)(2,1)S(1)} %get-tuple-element.26.refs_6_.refs_0_, bf16[96,1152]{1,0:T(8,128)(2,1)S(1)} %get-tuple-element.27.refs_7_.refs_1_, bf16[272,1152]{1,0:T(8,128)(2,1)S(1)} %collective-permute-done.1.refs_2_, ...), custom_call_target="tpu_custom_call" | custom-call | flops 1000 | bytes 1000 | tf_op jit(solution)/shard_map/pallas_call | solution.py:70
  64.7 0.0 collective-permute-done.17.refs_4_
  64.8 0.5 collective-permute-done.18.refs_5_
  65.2 2.9 %collective-permute-done.19.refs_6_ = bf16[2,96,128]{2,1,0:T(8,128)(2,1)S(1)} collective-permute-done((bf16[2,96,128]{2,1,0:T(8,128)(2,1)S(1)}, bf16[2,96,128]{2,1,0:T(8,128)(2,1)S(1)}, u32[]{:S(2)}, u32[]{:S(2)}) %collective-permute-start.19) | collective-permute-done | bytes 49184 | tf_op jit(solution)/shard_map/ppermute | solution.py:60
  68.1 1.6 %shard_map.35 = (bf16[4,80,256]{2,1,0:T(8,128)(2,1)S(1)}, bf16[4,80,256]{2,1,0:T(8,128)(2,1)S(1)}, bf16[4,80,256]{2,1,0:T(8,128)(2,1)S(1)}) custom-call(s32[4]{0:T(128)S(1)} %pad_add_fusion.place_ref, f32[3,96,256]{2,1,0:T(8,128)S(1)} %get-tuple-element.30.refs_0_, f32[13,96,256]{2,1,0:T(8,128)S(1)} %shard_map.30.refs_1_, ...), custom_call_target="tpu_custom_call" | custom-call | flops 1000 | bytes 1000 | tf_op jit(solution)/shard_map/pallas_call | solution.py:70
  69.8 1.6 %collective-permute-start.20 = (bf16[4,80,256]{2,1,0:T(8,128)(2,1)S(1)}, bf16[4,80,256]{2,1,0:T(8,128)(2,1)S(1)}, u32[]{:S(2)}, u32[]{:S(2)}) collective-permute-start(bf16[4,80,256]{2,1,0:T(8,128)(2,1)S(1)} %get-tuple-element.38), channel_id=1, source_target_pairs={{0,2},{1,3},{2,0},{3,1},{4,6},{5,7},{6,4},{7,5},{8,10},{9,11},{10,... | collective-permute-start | bytes 491528 | tf_op jit(solution)/shard_map/ppermute | solution.py:60
  71.4 0.5 collective-permute-start.21
  71.9 1.4 %collective-permute-start.22 = (bf16[4,80,256]{2,1,0:T(8,128)(2,1)S(1)}, bf16[4,80,256]{2,1,0:T(8,128)(2,1)S(1)}, u32[]{:S(2)}, u32[]{:S(2)}) collective-permute-start(bf16[4,80,256]{2,1,0:T(8,128)(2,1)S(1)} %get-tuple-element.40), channel_id=1, source_target_pairs={{0,18},{1,19},{2,16},{3,17},{4,22},{5,23},{6,20},{7,21},{8,26},{9,... | collective-permute-start | bytes 491528 | tf_op jit(solution)/shard_map/ppermute | solution.py:60
  73.3 1.1 %shard_map.34.refs_0_ = bf16[4,80,256]{2,1,0:T(8,128)(2,1)S(1)} custom-call(s32[4]{0:T(128)S(1)} %pad_add_fusion.place_ref, f32[3,96,256]{2,1,0:T(8,128)S(1)} %get-tuple-element.30.refs_0_, f32[13,96,256]{2,1,0:T(8,128)S(1)} %shard_map.30.refs_1_, f32[4,96,128]{2,1,0:T(8,128)S(1)} %shard_map.32.a_ref.refs_2_, ...), custom_call_target="tpu_custom_call" | custom-call | flops 1000 | bytes 1000 | tf_op jit(solution)/shard_map/pallas_call | solution.py:70
  74.4 2.5 %collective-permute-done.20.refs_1_ = bf16[4,80,256]{2,1,0:T(8,128)(2,1)S(1)} collective-permute-done((bf16[4,80,256]{2,1,0:T(8,128)(2,1)S(1)}, bf16[4,80,256]{2,1,0:T(8,128)(2,1)S(1)}, u32[]{:S(2)}, u32[]{:S(2)}) %collective-permute-start.20) | collective-permute-done | bytes 163872 | tf_op jit(solution)/shard_map/ppermute | solution.py:60
  76.9 0.4 collective-permute-done.21.refs_2_
  77.3 1.7 %collective-permute-done.22.refs_3_ = bf16[4,80,256]{2,1,0:T(8,128)(2,1)S(1)} collective-permute-done((bf16[4,80,256]{2,1,0:T(8,128)(2,1)S(1)}, bf16[4,80,256]{2,1,0:T(8,128)(2,1)S(1)}, u32[]{:S(2)}, u32[]{:S(2)}) %collective-permute-start.22) | collective-permute-done | bytes 163872 | tf_op jit(solution)/shard_map/ppermute | solution.py:60
  79.0 1.7 %shard_map.36 = bf16[256,1280]{1,0:T(8,128)(2,1)} custom-call(s32[4]{0:T(128)S(1)} %pad_add_fusion.place_ref, bf16[4,80,256]{2,1,0:T(8,128)(2,1)S(1)} %shard_map.34.refs_0_, bf16[4,80,256]{2,1,0:T(8,128)(2,1)S(1)} %collective-permute-done.20.refs_1_, bf16[4,80,256]{2,1,0:T(8,128)(2,1)S(1)} %collective-permute-done.21.refs_2_, ...), custom_call_target="tpu_custom_call" | custom-call | flops 1000 | bytes 1000 | tf_op jit(solution)/shard_map/pallas_call | solution.py:70
  (5 shorter events, 0.1 us)
Async XLA Ops:
  0.0 4.5 %collective-permute-start = (bf16[240,2240]{1,0:T(8,128)(2,1)}, bf16[240,2240]{1,0:T(8,128)(2,1)S(1)}, u32[]{:S(2)}, u32[]{:S(2)}) collective-permute-start(bf16[240,2240]{1,0:T(8,128)(2,1)} %bitcast.16), channel_id=1, source_target_pairs={{0,1},{1,0},{2,3},{3,2},{4,5},{5,4},{6,7},{7,6},{8,9},{9,8},{10,11... | collective-permute-start | bytes 3225608 | tf_op jit(solution)/shard_map/ppermute | solution.py:60
  0.5 28.7 %collective-permute-start.5 = (bf16[2240,256]{1,0:T(8,128)(2,1)}, bf16[2240,256]{1,0:T(8,128)(2,1)S(1)}, u32[]{:S(2)}, u32[]{:S(2)}) collective-permute-start(bf16[2240,256]{1,0:T(8,128)(2,1)} %bitcast.11), channel_id=1, source_target_pairs={{0,2},{1,3},{2,0},{3,1},{4,6},{5,7},{6,4},{7,5},{8,10},{9,11},{10,... | collective-permute-start | bytes 3440648 | tf_op jit(solution)/shard_map/ppermute | solution.py:60
  3.0 27.6 %collective-permute-start.6 = (bf16[2240,256]{1,0:T(8,128)(2,1)}, bf16[2240,256]{1,0:T(8,128)(2,1)S(1)}, u32[]{:S(2)}, u32[]{:S(2)}) collective-permute-start(bf16[2240,256]{1,0:T(8,128)(2,1)} %bitcast.12), channel_id=1, source_target_pairs={{0,16},{1,17},{2,18},{3,19},{4,20},{5,21},{6,22},{7,23},{8,24},{9,... | collective-permute-start | bytes 3440648 | tf_op jit(solution)/shard_map/ppermute | solution.py:60
  4.5 1.2 %copy-start.1 = (bf16[3,2240,80]{1,2,0:T(8,128)(2,1)S(1)}, bf16[3,2240,80]{1,2,0:T(8,128)(2,1)}, u32[]{:S(2)}) copy-start(bf16[3,2240,80]{1,2,0:T(8,128)(2,1)} %param.3) | copy-start | bytes 3225604
  7.1 25.7 %collective-permute-start.1 = (bf16[272,1152]{1,0:T(8,128)(2,1)S(1)}, bf16[272,1152]{1,0:T(8,128)(2,1)S(1)}, u32[]{:S(2)}, u32[]{:S(2)}) collective-permute-start(bf16[272,1152]{1,0:T(8,128)(2,1)S(1)} %get-tuple-element.25), channel_id=1, source_target_pairs={{0,4},{1,5},{2,6},{3,7},{4,0},{5,1},{6,2},{7,3},{8,12},{9,13},{10,... | collective-permute-start | bytes 1880072 | tf_op jit(solution)/shard_map/ppermute | solution.py:60
  8.7 24.1 %collective-permute-start.3 = (bf16[176,1152]{1,0:T(8,128)(2,1)S(1)}, bf16[176,1152]{1,0:T(8,128)(2,1)S(1)}, u32[]{:S(2)}, u32[]{:S(2)}) collective-permute-start(bf16[176,1152]{1,0:T(8,128)(2,1)S(1)} %get-tuple-element.23.refs_0_), channel_id=1, source_target_pairs={{0,8},{1,9},{2,10},{3,11},{4,12},{5,13},{6,14},{7,15},{8,0},{9,1},... | collective-permute-start | bytes 1216520 | tf_op jit(solution)/shard_map/ppermute | solution.py:60
  30.6 7.0 %copy-start = (bf16[1,256,2240]{1,2,0:T(8,128)(2,1)S(1)}, bf16[1,256,2240]{1,2,0:T(8,128)(2,1)}, u32[]{:S(2)}) copy-start(bf16[1,256,2240]{1,2,0:T(8,128)(2,1)} %param.2) | copy-start | bytes 3440644
  30.6 14.4 %collective-permute-start.12 = (bf16[1120,256]{1,0:T(8,128)(2,1)S(1)}, bf16[1120,256]{1,0:T(8,128)(2,1)S(1)}, u32[]{:S(2)}, u32[]{:S(2)}) collective-permute-start(bf16[1120,256]{1,0:T(8,128)(2,1)S(1)} %slice.14), channel_id=1, source_target_pairs={{0,16},{1,17},{2,18},{3,19},{4,20},{5,21},{6,22},{7,23},{8,24},{9,... | collective-permute-start | bytes 1720328 | tf_op jit(solution)/shard_map/ppermute | solution.py:60
  32.2 14.1 %collective-permute-start.13 = (bf16[1120,256]{1,0:T(8,128)(2,1)S(1)}, bf16[1120,256]{1,0:T(8,128)(2,1)S(1)}, u32[]{:S(2)}, u32[]{:S(2)}) collective-permute-start(bf16[1120,256]{1,0:T(8,128)(2,1)S(1)} %slice.15), channel_id=1, source_target_pairs={{0,2},{1,3},{2,0},{3,1},{4,6},{5,7},{6,4},{7,5},{8,10},{9,11},{10,... | collective-permute-start | bytes 1720328 | tf_op jit(solution)/shard_map/ppermute | solution.py:60
  32.8 2.3 %collective-permute-start.4 = (bf16[176,1152]{1,0:T(8,128)(2,1)S(1)}, bf16[176,1152]{1,0:T(8,128)(2,1)S(1)}, u32[]{:S(2)}, u32[]{:S(2)}) collective-permute-start(bf16[176,1152]{1,0:T(8,128)(2,1)S(1)} %collective-permute-done.3.refs_4_), channel_id=1, source_target_pairs={{0,1},{1,0},{2,3},{3,2},{4,5},{5,4},{6,7},{7,6},{8,9},{9,8},{10,11... | collective-permute-start | bytes 1216520 | tf_op jit(solution)/shard_map/ppermute | solution.py:60
  32.9 4.7 %collective-permute-start.2 = (bf16[176,1152]{1,0:T(8,128)(2,1)S(1)}, bf16[176,1152]{1,0:T(8,128)(2,1)S(1)}, u32[]{:S(2)}, u32[]{:S(2)}) collective-permute-start(bf16[176,1152]{1,0:T(8,128)(2,1)S(1)} %slice.16), channel_id=1, source_target_pairs={{0,1},{1,0},{2,3},{3,2},{4,5},{5,4},{6,7},{7,6},{8,9},{9,8},{10,11... | collective-permute-start | bytes 1216520 | tf_op jit(solution)/shard_map/ppermute | solution.py:60
  33.4 16.1 %collective-permute-start.14 = (bf16[176,1152]{1,0:T(8,128)(2,1)S(1)}, bf16[176,1152]{1,0:T(8,128)(2,1)S(1)}, u32[]{:S(2)}, u32[]{:S(2)}) collective-permute-start(bf16[176,1152]{1,0:T(8,128)(2,1)S(1)} %collective-permute-done.3.refs_4_), channel_id=1, source_target_pairs={{0,4},{1,5},{2,6},{3,7},{4,0},{5,1},{6,2},{7,3},{8,12},{9,13},{10,... | collective-permute-start | bytes 1216520 | tf_op jit(solution)/shard_map/ppermute | solution.py:60
  35.1 14.4 %collective-permute-start.8 = (bf16[96,1152]{1,0:T(8,128)(2,1)S(1)}, bf16[96,1152]{1,0:T(8,128)(2,1)S(1)}, u32[]{:S(2)}, u32[]{:S(2)}) collective-permute-start(bf16[96,1152]{1,0:T(8,128)(2,1)S(1)} %get-tuple-element.26.refs_6_.refs_0_), channel_id=1, source_target_pairs={{0,8},{1,9},{2,10},{3,11},{4,12},{5,13},{6,14},{7,15},{8,0},{9,1},... | collective-permute-start | bytes 663560 | tf_op jit(solution)/shard_map/ppermute | solution.py:60
  49.5 2.6 %collective-permute-start.15 = (bf16[176,1152]{1,0:T(8,128)(2,1)S(1)}, bf16[176,1152]{1,0:T(8,128)(2,1)S(1)}, u32[]{:S(2)}, u32[]{:S(2)}) collective-permute-start(bf16[176,1152]{1,0:T(8,128)(2,1)S(1)} %collective-permute-done.14.refs_0_), channel_id=1, source_target_pairs={{0,1},{1,0},{2,3},{3,2},{4,5},{5,4},{6,7},{7,6},{8,9},{9,8},{10,11... | collective-permute-start | bytes 1216520 | tf_op jit(solution)/shard_map/ppermute | solution.py:60
  49.5 7.8 %collective-permute-start.10 = (bf16[96,1152]{1,0:T(8,128)(2,1)S(1)}, bf16[96,1152]{1,0:T(8,128)(2,1)S(1)}, u32[]{:S(2)}, u32[]{:S(2)}) collective-permute-start(bf16[96,1152]{1,0:T(8,128)(2,1)S(1)} %collective-permute-done.8.refs_4_), channel_id=1, source_target_pairs={{0,4},{1,5},{2,6},{3,7},{4,0},{5,1},{6,2},{7,3},{8,12},{9,13},{10,... | collective-permute-start | bytes 663560 | tf_op jit(solution)/shard_map/ppermute | solution.py:60
  52.1 10.1 %collective-permute-start.9 = (bf16[96,1152]{1,0:T(8,128)(2,1)S(1)}, bf16[96,1152]{1,0:T(8,128)(2,1)S(1)}, u32[]{:S(2)}, u32[]{:S(2)}) collective-permute-start(bf16[96,1152]{1,0:T(8,128)(2,1)S(1)} %collective-permute-done.8.refs_4_), channel_id=1, source_target_pairs={{0,1},{1,0},{2,3},{3,2},{4,5},{5,4},{6,7},{7,6},{8,9},{9,8},{10,11... | collective-permute-start | bytes 663560 | tf_op jit(solution)/shard_map/ppermute | solution.py:60
  55.1 2.9 %collective-permute-start.16 = (f32[4,96,128]{2,1,0:T(8,128)S(1)}, f32[4,96,128]{2,1,0:T(8,128)S(1)}, u32[]{:S(2)}, u32[]{:S(2)}) collective-permute-start(f32[4,96,128]{2,1,0:T(8,128)S(1)} %shard_map.32.a_ref.refs_2_), channel_id=1, source_target_pairs={{0,1},{1,0},{2,3},{3,2},{4,5},{5,4},{6,7},{7,6},{8,9},{9,8},{10,11... | collective-permute-start | bytes 589832 | tf_op jit(solution)/shard_map/ppermute | solution.py:60
  57.4 5.1 %collective-permute-start.11 = (bf16[96,1152]{1,0:T(8,128)(2,1)S(1)}, bf16[96,1152]{1,0:T(8,128)(2,1)S(1)}, u32[]{:S(2)}, u32[]{:S(2)}) collective-permute-start(bf16[96,1152]{1,0:T(8,128)(2,1)S(1)} %collective-permute-done.10.refs_6_), channel_id=1, source_target_pairs={{0,1},{1,0},{2,3},{3,2},{4,5},{5,4},{6,7},{7,6},{8,9},{9,8},{10,11... | collective-permute-start | bytes 663560 | tf_op jit(solution)/shard_map/ppermute | solution.py:60
  57.4 5.1 %collective-permute-start.7 = (bf16[96,1152]{1,0:T(8,128)(2,1)S(1)}, bf16[96,1152]{1,0:T(8,128)(2,1)S(1)}, u32[]{:S(2)}, u32[]{:S(2)}) collective-permute-start(bf16[96,1152]{1,0:T(8,128)(2,1)S(1)} %slice.17), channel_id=1, source_target_pairs={{0,1},{1,0},{2,3},{3,2},{4,5},{5,4},{6,7},{7,6},{8,9},{9,8},{10,11... | collective-permute-start | bytes 663560 | tf_op jit(solution)/shard_map/ppermute | solution.py:60
  58.0 6.7 %collective-permute-start.17 = (bf16[2,96,128]{2,1,0:T(8,128)(2,1)S(1)}, bf16[2,96,128]{2,1,0:T(8,128)(2,1)S(1)}, u32[]{:S(2)}, u32[]{:S(2)}) collective-permute-start(bf16[2,96,128]{2,1,0:T(8,128)(2,1)S(1)} %shard_map.33), channel_id=1, source_target_pairs={{0,4},{1,5},{2,6},{3,7},{4,0},{5,1},{6,2},{7,3},{8,12},{9,13},{10,... | collective-permute-start | bytes 147464 | tf_op jit(solution)/shard_map/ppermute | solution.py:60
  59.4 5.9 %collective-permute-start.18 = (bf16[2,96,128]{2,1,0:T(8,128)(2,1)S(1)}, bf16[2,96,128]{2,1,0:T(8,128)(2,1)S(1)}, u32[]{:S(2)}, u32[]{:S(2)}) collective-permute-start(bf16[2,96,128]{2,1,0:T(8,128)(2,1)S(1)} %shard_map.33), channel_id=1, source_target_pairs={{0,8},{1,9},{2,10},{3,11},{4,12},{5,13},{6,14},{7,15},{8,0},{9,1},... | collective-permute-start | bytes 147464 | tf_op jit(solution)/shard_map/ppermute | solution.py:60
  62.2 5.9 %collective-permute-start.19 = (bf16[2,96,128]{2,1,0:T(8,128)(2,1)S(1)}, bf16[2,96,128]{2,1,0:T(8,128)(2,1)S(1)}, u32[]{:S(2)}, u32[]{:S(2)}) collective-permute-start(bf16[2,96,128]{2,1,0:T(8,128)(2,1)S(1)} %shard_map.33), channel_id=1, source_target_pairs={{0,12},{1,13},{2,14},{3,15},{4,8},{5,9},{6,10},{7,11},{8,4},{9,5},... | collective-permute-start | bytes 147464 | tf_op jit(solution)/shard_map/ppermute | solution.py:60
  69.8 7.1 %collective-permute-start.20 = (bf16[4,80,256]{2,1,0:T(8,128)(2,1)S(1)}, bf16[4,80,256]{2,1,0:T(8,128)(2,1)S(1)}, u32[]{:S(2)}, u32[]{:S(2)}) collective-permute-start(bf16[4,80,256]{2,1,0:T(8,128)(2,1)S(1)} %get-tuple-element.38), channel_id=1, source_target_pairs={{0,2},{1,3},{2,0},{3,1},{4,6},{5,7},{6,4},{7,5},{8,10},{9,11},{10,... | collective-permute-start | bytes 491528 | tf_op jit(solution)/shard_map/ppermute | solution.py:60
  71.4 5.9 %collective-permute-start.21 = (bf16[4,80,256]{2,1,0:T(8,128)(2,1)S(1)}, bf16[4,80,256]{2,1,0:T(8,128)(2,1)S(1)}, u32[]{:S(2)}, u32[]{:S(2)}) collective-permute-start(bf16[4,80,256]{2,1,0:T(8,128)(2,1)S(1)} %get-tuple-element.39), channel_id=1, source_target_pairs={{0,16},{1,17},{2,18},{3,19},{4,20},{5,21},{6,22},{7,23},{8,24},{9,... | collective-permute-start | bytes 491528 | tf_op jit(solution)/shard_map/ppermute | solution.py:60
  71.9 7.1 %collective-permute-start.22 = (bf16[4,80,256]{2,1,0:T(8,128)(2,1)S(1)}, bf16[4,80,256]{2,1,0:T(8,128)(2,1)S(1)}, u32[]{:S(2)}, u32[]{:S(2)}) collective-permute-start(bf16[4,80,256]{2,1,0:T(8,128)(2,1)S(1)} %get-tuple-element.40), channel_id=1, source_target_pairs={{0,18},{1,19},{2,16},{3,17},{4,22},{5,23},{6,20},{7,21},{8,26},{9,... | collective-permute-start | bytes 491528 | tf_op jit(solution)/shard_map/ppermute | solution.py:60

commit v5 on v4

--- a/solution.py
+++ b/solution.py
@@ -62,8 +62,12 @@
 
 ANY = pl.BlockSpec(memory_space=pl.ANY)
 VMEM = pl.BlockSpec(memory_space=pltpu.VMEM)
-SMEM = pl.BlockSpec(memory_space=pltpu.SMEM)
 LIGHT = pl.CostEstimate(flops=1000, bytes_accessed=1000, transcendentals=0)
+
+
+def position():
+    frame = lax.axis_index("frame")
+    return lax.axis_index("groups"), frame // 4, (frame // 2) % 2, frame % 2
 
 
 def call(body, out, ins, scratch, *operands):
@@ -87,23 +91,17 @@
     return (width * g + row) // HEAD_DIM == (4 * half * g + turned) // HEAD_DIM
 
 
-def pick(place, own, swapped, half):
+def pick(own, swapped, half):
     width, depth = own.shape[0] // 3, own.shape[1]
     part = -(-depth // 256) * 128
     more = width + half
     rows = 2 * more + width
-    chunks = [pl.ds(width * i, width) for i in range(3)]
-
-    def body(place_ref, own_hbm, swapped_ref, kv_ref, q_ref, all_ref, other_kv_ref, other_q_ref, full, own_ref, sems):
-        reads = [pltpu.make_async_copy(own_hbm.at[r], own_ref.at[r], sems.at[i]) for i, r in enumerate(chunks)]
-        for read in reads:
-            read.start()
-        g, lo = place_ref[0], place_ref[3]
+
+    def body(own_ref, swapped_ref, kv_ref, q_ref, all_ref, other_kv_ref, other_q_ref, full):
+        g, _, _, lo = position()
         mine = lo == g
         full[:, 2 * part - 128 :] = jnp.zeros((rows, 128), full.dtype)
         at = pl.multiple_of(g * (width - half), 16)
-        for read in reads:
-            read.wait()
         for start, which in ((0, 1), (more, 2), (more + width, 0)):
             shard = pl.ds(which * width, width)
             full[start : start + width, :depth] = jnp.where(mine, own_ref[shard], swapped_ref[shard])
@@ -120,15 +118,10 @@
 
     shape = lambda n: jax.ShapeDtypeStruct((n, part), own.dtype)
     out = [shape(more + width), shape(more), shape(rows), shape(more + width), shape(more)]
-    scratch = [
-        pltpu.VMEM((rows, 2 * part), own.dtype),
-        pltpu.VMEM(own.shape, own.dtype),
-        pltpu.SemaphoreType.DMA((len(chunks),)),
-    ]
-    return call(body, out, [SMEM, ANY, VMEM], scratch, place, own, swapped)
-
-
-def project(place, half, jobs, blocks, frames, carried=(), keep=False, given=None):
+    return call(body, out, [VMEM, VMEM], [pltpu.VMEM((rows, 2 * part), own.dtype)], own, swapped)
+
+
+def project(half, jobs, blocks, frames, carried=(), keep=False, given=None):
     arrays, pieces, rows = [], {}, 0
 
     def index(a):
@@ -165,13 +158,13 @@
                     places[k, m] = len(places)
     n_in = len(arrays)
 
-    def body(place_ref, *refs):
+    def body(*refs):
         ins, refs = refs[:n_in], list(refs[n_in:])
         c_refs = [refs.pop(0) for _ in carried]
         q_ref = refs.pop(0) if places else None
         s_ref = refs.pop(0) if held else None
         w_ref = refs.pop(0) if given is None else ins[0]
-        g, lo = place_ref[0], place_ref[3]
+        g, _, _, lo = position()
         first_half = lo == 0
         if held:
             same = heads_of(g, width, half)
@@ -215,8 +208,8 @@
         out.append(jax.ShapeDtypeStruct((rows, depth), jnp.bfloat16))
     elif given is None:
         scratch.append(pltpu.VMEM((rows, depth), jnp.bfloat16))
-    ins = [SMEM] + [VMEM] * (n_in + len(carried))
-    got = list(call(body, out, ins, scratch, place, *arrays, *[a for _, a, _ in carried]))
+    ins = [VMEM] * (n_in + len(carried))
+    got = list(call(body, out, ins, scratch, *arrays, *[a for _, a, _ in carried]))
     made = ([(places, got.pop(0))] if places else []) + ([(held, got.pop(0))] if held else [])
     return made + ([(pieces, got[0])] if keep else [])
 
@@ -247,7 +240,7 @@
     return call(body, jax.ShapeDtypeStruct(plane.shape, plane.dtype), [VMEM] * 2, [], plane, near)
 
 
-def apply(place, half, ms, queries, mine, others, planes):
+def apply(half, ms, queries, mine, others, planes):
     arrays = []
     where = {}
     for m in ms:
@@ -259,11 +252,11 @@
     rows, count = arrays[0].shape[1:]
     width = rows - half
 
-    def body(place_ref, *refs):
+    def body(*refs):
         q_refs = refs[: len(arrays)]
         mine_ref, others_ref = refs[len(arrays) : len(arrays) + 2]
         plane_refs, outs = refs[len(arrays) + 2 : -len(ms)], refs[-len(ms) :]
-        g, hi, b, lo = (place_ref[i] for i in range(4))
+        g, hi, b, lo = position()
         same = heads_of(g, width, half)
         factor = lambda yes: jnp.where(yes, 1.0, 0.0).astype(jnp.float32)
         second = factor(lo == 1)
@@ -289,16 +282,16 @@
                 out_ref[j] = (both[:width] / (both[width:] + EPSILON)).astype(jnp.bfloat16)
 
     out = [jax.ShapeDtypeStruct((4, width, count), jnp.bfloat16)] * len(ms)
-    ins = [SMEM] + [VMEM] * (len(arrays) + 2 + len(planes))
-    return call(body, out, ins, [], place, *arrays, mine, others, *[p for p, _, _ in planes])
-
-
-def assemble(place, got):
+    ins = [VMEM] * (len(arrays) + 2 + len(planes))
+    return call(body, out, ins, [], *arrays, mine, others, *[p for p, _, _ in planes])
+
+
+def assemble(got):
     blocks, width, count = got[0].shape
 
-    def body(place_ref, *refs):
+    def body(*refs):
         *got_refs, out_ref, every = refs
-        g, hi, b = (place_ref[i] for i in range(3))
+        g, hi, b, _ = position()
         for m in range(4):
             this_g, this_b = jnp.bitwise_xor(g, m >> 1), jnp.bitwise_xor(b, m & 1)
             for k in range(blocks):
@@ -308,14 +301,10 @@
 
     out = jax.ShapeDtypeStruct((count, 4 * blocks * width), jnp.bfloat16)
     scratch = [pltpu.VMEM((4 * blocks * width, count), jnp.bfloat16)]
-    return call(body, out, [SMEM] + [VMEM] * 4, scratch, place, *got)
+    return call(body, out, [VMEM] * 4, scratch, *got)
 
 
 def shared_plan(layout, frames_in, qkv_weight):
-    g = lax.axis_index("groups")
-    frame = lax.axis_index("frame")
-    lo, b, hi = frame % 2, (frame // 2) % 2, frame // 4
-    place = jnp.stack([g, hi, b, lo]).astype(jnp.int32)
     weights = qkv_weight.transpose(0, 2, 1)
     width, depth = weights.shape[1:]
     half = HEAD_DIM // 2
@@ -330,7 +319,7 @@
     next_b = send(own, over_b)
     next_g = send(own, over_g)
     shard = weights.reshape(3 * width, depth)
-    kv, q, whole, other_kv, other_q = pick(place, shard, send(shard, over_lo), half)
+    kv, q, whole, other_kv, other_q = pick(shard, send(shard, over_lo), half)
     more, kv_rows = q.shape[0], kv.shape[0]
     queries = {}
 
@@ -355,31 +344,33 @@
     blocks[2]["kv"] = swapped(far_kv)
     blocks[1]["kv"] = swapped(near, 0, kv_rows)
     jobs = [([(k, "kv") for k in range(3)] + [(0, "q")], [0, 1, 2])]
-    made, (_, states), given = project(place, half, jobs, blocks, frames, keep=True)
+    made, (_, states), given = project(half, jobs, blocks, frames, keep=True)
     keep(made)
+    last_kv, states = lax.optimization_barrier((last_kv, states))
+    blocks[3]["kv"] = swapped(last_kv)
+    carried = [(m, states, m) for m in range(3)]
+    ((_, states),) = project(half, [([(3, "kv")], [0, 1, 2])], blocks, frames, carried)
     *across, states = lax.optimization_barrier((*across, states))
     frames[3] = across
-    ((_, states_3),) = project(place, half, [([(k, "kv") for k in range(3)], [3])], blocks, frames, given=given)
-    last_kv, states_3 = lax.optimization_barrier((last_kv, states_3))
-    blocks[3]["kv"] = swapped(last_kv)
+    ((_, states_3),) = project(half, [([(k, "kv") for k in range(3)], [3])], blocks, frames, given=given)
     last_q = send(far_q, along(1))
     blocks[2]["q"], blocks[3]["q"] = swapped(far_q), swapped(last_q)
     blocks[1]["q"] = swapped(near, kv_rows, more)
     carried = [(m, states, m) for m in range(3)] + [(3, states_3, 0)]
-    ((_, mine),) = project(place, half, [([(3, "kv")], [0, 1, 2, 3])], blocks, frames, carried)
+    ((_, mine),) = project(half, [([(3, "kv")], [3])], blocks, frames, carried)
     others = send(mine, over_lo)
     plane = plane_sum(mine, others)
     planes = [(send(plane, along(k)), k, lambda hi, k=k: jnp.bitwise_xor(hi, k) < hi) for k in (1, 2, 3)]
     last = [([(k, "q") for k in range(4)], [3]), ([(k, "q") for k in (1, 2, 3)], [0, 1, 2])]
-    (made,) = project(place, half, last, blocks, frames)
+    (made,) = project(half, last, blocks, frames)
     keep(made)
 
-    out1, out2, out3 = apply(place, half, [1, 2, 3], queries, mine, others, planes)
-    (out0,) = apply(place, half, [0], queries, mine, others, planes)
+    out1, out2, out3 = apply(half, [1, 2, 3], queries, mine, others, planes)
+    (out0,) = apply(half, [0], queries, mine, others, planes)
     out1 = send(out1, over_b)
     out2 = send(out2, over_g)
     out3 = send(out3, over_gb)
-    return assemble(place, [out0, out1, out2, out3])[None]
+    return assemble([out0, out1, out2, out3])[None]
 
 
 def solution(mesh):

time: 80.8 us -> 78.1 us (0.967)
  Pallas kernels: 17.6 us -> 12.7 us
  waiting for transfers between devices: 34.2 us -> 36.7 us
    pallas_call x9 -> x10, Pallas kernels: 17.6 us -> 12.7 us  [call(): pl.pallas_call(body, out_shape=out, in_specs=ins, out_specs=jax.tree.map(...]
    ppermute x23, waiting for transfers between devices: 34.2 us -> 36.7 us  [send(): return lax.ppermute(a, AXES, pairs)]
  transfers between devices with their start and end apart: 23 -> 23, of which waited for: 11 -> 9; matrix products, arithmetic and copies ran while one was open for 0% -> 0% of each run, Pallas kernels for 18% -> 13%
where the time goes in v5:
time: 78.1 us; the launch traced here: 78 us
  waiting for transfers between devices  36.7 us (47%)
  starting transfers between devices  27.1 us (35%)
  Pallas kernels  12.7 us (16%)
  local copies, waits for them, and re-layouts  1.38 us (2%)
    ppermute x23, waiting for transfers between devices, send(): return lax.ppermute(a, AXES, pairs)  36.7 us
    ppermute x23, starting transfers between devices, send(): return lax.ppermute(a, AXES, pairs)  27.1 us
    pallas_call x10, Pallas kernels, call(): pl.pallas_call(body, out_shape=out, in_specs=ins, out_specs=jax.tree.map(...  12.7 us
  transfers between devices with their start and end apart: 23, of which 9 were waited for; matrix products, arithmetic and copies ran while one was open for 0% of the time, Pallas kernels for 13%

profile of v5, /device:TPU:0, one launch (start us, length us, event | category | flops | bytes accessed | tf_op | source)
XLA Modules:
  0.0 78.0 jit_solution(5295745262441698628)
XLA Ops:
  0.0 0.5 collective-permute-start
  0.5 2.5 %collective-permute-start.5 = (bf16[2240,256]{1,0:T(8,128)(2,1)}, bf16[2240,256]{1,0:T(8,128)(2,1)S(1)}, u32[]{:S(2)}, u32[]{:S(2)}) collective-permute-start(bf16[2240,256]{1,0:T(8,128)(2,1)} %bitcast.7), channel_id=1, source_target_pairs={{0,2},{1,3},{2,0},{3,1},{4,6},{5,7},{6,4},{7,5},{8,10},{9,11},{10,... | collective-permute-start | bytes 3440648 | tf_op jit(solution)/shard_map/ppermute | solution.py:60
  3.0 1.5 %collective-permute-start.6 = (bf16[2240,256]{1,0:T(8,128)(2,1)}, bf16[2240,256]{1,0:T(8,128)(2,1)S(1)}, u32[]{:S(2)}, u32[]{:S(2)}) collective-permute-start(bf16[2240,256]{1,0:T(8,128)(2,1)} %bitcast.8), channel_id=1, source_target_pairs={{0,16},{1,17},{2,18},{3,19},{4,20},{5,21},{6,22},{7,23},{8,24},{9,... | collective-permute-start | bytes 3440648 | tf_op jit(solution)/shard_map/ppermute | solution.py:60
  4.5 0.0 collective-permute-done.swapped_ref
  4.5 0.0 copy-start.1
  4.5 1.2 %copy-done.1 = bf16[3,2240,80]{1,2,0:T(8,128)(2,1)S(1)} copy-done((bf16[3,2240,80]{1,2,0:T(8,128)(2,1)S(1)}, bf16[3,2240,80]{1,2,0:T(8,128)(2,1)}, u32[]{:S(2)}) %copy-start.1) | copy-done | bytes 1075224
  5.7 0.3 shard_map.28
  6.0 1.6 %collective-permute-start.1 = (bf16[272,1152]{1,0:T(8,128)(2,1)S(1)}, bf16[272,1152]{1,0:T(8,128)(2,1)S(1)}, u32[]{:S(2)}, u32[]{:S(2)}) collective-permute-start(bf16[272,1152]{1,0:T(8,128)(2,1)S(1)} %get-tuple-element.25), channel_id=1, source_target_pairs={{0,4},{1,5},{2,6},{3,7},{4,0},{5,1},{6,2},{7,3},{8,12},{9,13},{10,... | collective-permute-start | bytes 1880072 | tf_op jit(solution)/shard_map/ppermute | solution.py:60
  7.6 2.6 %collective-permute-start.3 = (bf16[176,1152]{1,0:T(8,128)(2,1)S(1)}, bf16[176,1152]{1,0:T(8,128)(2,1)S(1)}, u32[]{:S(2)}, u32[]{:S(2)}) collective-permute-start(bf16[176,1152]{1,0:T(8,128)(2,1)S(1)} %get-tuple-element.23.refs_0_), channel_id=1, source_target_pairs={{0,8},{1,9},{2,10},{3,11},{4,12},{5,13},{6,14},{7,15},{8,0},{9,1},... | collective-permute-start | bytes 1216520 | tf_op jit(solution)/shard_map/ppermute | solution.py:60
  10.2 19.7 %collective-permute-done.3.refs_4_ = bf16[176,1152]{1,0:T(8,128)(2,1)S(1)} collective-permute-done((bf16[176,1152]{1,0:T(8,128)(2,1)S(1)}, bf16[176,1152]{1,0:T(8,128)(2,1)S(1)}, u32[]{:S(2)}, u32[]{:S(2)}) %collective-permute-start.3) | collective-permute-done | bytes 405536 | tf_op jit(solution)/shard_map/ppermute | solution.py:60
  29.9 0.0 collective-permute-start.4
  29.9 0.8 collective-permute-done.1.refs_2_
  30.8 0.0 copy-start
  30.8 0.1 collective-permute-start.2
  30.8 3.2 %collective-permute-start.14 = (bf16[176,1152]{1,0:T(8,128)(2,1)S(1)}, bf16[176,1152]{1,0:T(8,128)(2,1)S(1)}, u32[]{:S(2)}, u32[]{:S(2)}) collective-permute-start(bf16[176,1152]{1,0:T(8,128)(2,1)S(1)} %collective-permute-done.3.refs_4_), channel_id=1, source_target_pairs={{0,4},{1,5},{2,6},{3,7},{4,0},{5,1},{6,2},{7,3},{8,12},{9,13},{10,... | collective-permute-start | bytes 1216520 | tf_op jit(solution)/shard_map/ppermute | solution.py:60
  34.1 0.0 collective-permute-done.5.refs_9_.refs_3_.refs_11_
  34.1 0.0 collective-permute-done.6.refs_10_.refs_4_.refs_12_
  34.1 1.6 %collective-permute-start.12 = (bf16[1120,256]{1,0:T(8,128)(2,1)S(1)}, bf16[1120,256]{1,0:T(8,128)(2,1)S(1)}, u32[]{:S(2)}, u32[]{:S(2)}) collective-permute-start(bf16[1120,256]{1,0:T(8,128)(2,1)S(1)} %slice.14), channel_id=1, source_target_pairs={{0,16},{1,17},{2,18},{3,19},{4,20},{5,21},{6,22},{7,23},{8,24},{9,... | collective-permute-start | bytes 1720328 | tf_op jit(solution)/shard_map/ppermute | solution.py:60
  35.7 1.6 %collective-permute-start.13 = (bf16[1120,256]{1,0:T(8,128)(2,1)S(1)}, bf16[1120,256]{1,0:T(8,128)(2,1)S(1)}, u32[]{:S(2)}, u32[]{:S(2)}) collective-permute-start(bf16[1120,256]{1,0:T(8,128)(2,1)S(1)} %slice.15), channel_id=1, source_target_pairs={{0,2},{1,3},{2,0},{3,1},{4,6},{5,7},{6,4},{7,5},{8,10},{9,11},{10,... | collective-permute-start | bytes 1720328 | tf_op jit(solution)/shard_map/ppermute | solution.py:60
  37.3 0.0 collective-permute-done.4.refs_5_
  37.3 1.1 %collective-permute-start.8 = (bf16[96,1152]{1,0:T(8,128)(2,1)S(1)}, bf16[96,1152]{1,0:T(8,128)(2,1)S(1)}, u32[]{:S(2)}, u32[]{:S(2)}) collective-permute-start(bf16[96,1152]{1,0:T(8,128)(2,1)S(1)} %get-tuple-element.26.refs_6_.refs_0_), channel_id=1, source_target_pairs={{0,8},{1,9},{2,10},{3,11},{4,12},{5,13},{6,14},{7,15},{8,0},{9,1},... | collective-permute-start | bytes 663560 | tf_op jit(solution)/shard_map/ppermute | solution.py:60
  38.4 0.0 collective-permute-done.2.refs_3_
  38.4 0.0 copy-done
  38.4 4.4 %shard_map.29 = (f32[3,96,256]{2,1,0:T(8,128)S(1)}, f32[3,96,128]{2,1,0:T(8,128)S(1)}, bf16[624,2240]{1,0:T(8,128)(2,1)S(1)}) custom-call(bf16[176,1152]{1,0:T(8,128)(2,1)S(1)} %get-tuple-element.23.refs_0_, bf16[176,1152]{1,0:T(8,128)(2,1)S(1)} %get-tuple-element.24.refs_1_, bf16[272,1152]{1,0:T(8,128)(2,1)S(1)} %collective-permute-done.1.refs_2_, ...), custom_call_target="tpu_custom_call" | custom-call | flops 1000 | bytes 1000 | tf_op jit(solution)/shard_map/pallas_call | solution.py:74
  42.8 5.6 %collective-permute-done.14.refs_0_ = bf16[176,1152]{1,0:T(8,128)(2,1)S(1)} collective-permute-done((bf16[176,1152]{1,0:T(8,128)(2,1)S(1)}, bf16[176,1152]{1,0:T(8,128)(2,1)S(1)}, u32[]{:S(2)}, u32[]{:S(2)}) %collective-permute-start.14) | collective-permute-done | bytes 405536 | tf_op jit(solution)/shard_map/ppermute | solution.py:60
  48.4 0.0 collective-permute-start.15
  48.4 0.0 collective-permute-done.8.refs_4_
  48.4 1.7 %collective-permute-start.10 = (bf16[96,1152]{1,0:T(8,128)(2,1)S(1)}, bf16[96,1152]{1,0:T(8,128)(2,1)S(1)}, u32[]{:S(2)}, u32[]{:S(2)}) collective-permute-start(bf16[96,1152]{1,0:T(8,128)(2,1)S(1)} %collective-permute-done.8.refs_4_), channel_id=1, source_target_pairs={{0,4},{1,5},{2,6},{3,7},{4,0},{5,1},{6,2},{7,3},{8,12},{9,13},{10,... | collective-permute-start | bytes 663560 | tf_op jit(solution)/shard_map/ppermute | solution.py:60
  50.1 0.0 collective-permute-start.9
  50.1 0.0 collective-permute-done.15.refs_1_
  50.2 1.7 %shard_map.30.refs_4_.refs_5_.refs_6_ = f32[3,96,128]{2,1,0:T(8,128)S(1)} custom-call(bf16[176,1152]{1,0:T(8,128)(2,1)S(1)} %collective-permute-done.14.refs_0_, bf16[176,1152]{1,0:T(8,128)(2,1)S(1)} %collective-permute-done.15.refs_1_, bf16[2240,256]{1,0:T(8,128)(2,1)S(1)} %bitcast.10, ...), custom_call_target="tpu_custom_call" | custom-call | flops 1000 | bytes 1000 | tf_op jit(solution)/shard_map/pallas_call | solution.py:74
  51.8 0.0 collective-permute-done.12.refs_8_.refs_1_.refs_2_
  51.8 0.0 collective-permute-done.13.refs_9_.refs_2_.refs_3_
  51.9 1.1 %shard_map.32.refs_7_ = f32[1,96,128]{2,1,0:T(8,128)S(1)} custom-call(bf16[624,2240]{1,0:T(8,128)(2,1)S(1)} %get-tuple-element.37.refs_0_, bf16[1120,256]{1,0:T(8,128)(2,1)S(1)} %collective-permute-done.12.refs_8_.refs_1_.refs_2_, bf16[1120,256]{1,0:T(8,128)(2,1)S(1)} %collective-permute-done.13.refs_9_.refs_2_.refs_3_), custom_call_target="tpu_custom_call" | custom-call | flops 1000 | bytes 1000 | tf_op jit(solution)/shard_map/pallas_call | solution.py:74
  53.0 0.7 shard_map.33.a_ref.refs_2_
  53.7 0.5 collective-permute-start.16
  54.2 2.0 %collective-permute-done.10.refs_6_ = bf16[96,1152]{1,0:T(8,128)(2,1)S(1)} collective-permute-done((bf16[96,1152]{1,0:T(8,128)(2,1)S(1)}, bf16[96,1152]{1,0:T(8,128)(2,1)S(1)}, u32[]{:S(2)}, u32[]{:S(2)}) %collective-permute-start.10) | collective-permute-done | bytes 221216 | tf_op jit(solution)/shard_map/ppermute | solution.py:60
  56.3 0.0 collective-permute-start.11
  56.3 0.6 collective-permute-start.7
  56.9 0.0 collective-permute-done.16.b_ref.refs_3_
  56.9 0.4 collective-permute-start.17
  57.3 2.9 %collective-permute-start.18 = (bf16[2,96,128]{2,1,0:T(8,128)(2,1)S(1)}, bf16[2,96,128]{2,1,0:T(8,128)(2,1)S(1)}, u32[]{:S(2)}, u32[]{:S(2)}) collective-permute-start(bf16[2,96,128]{2,1,0:T(8,128)(2,1)S(1)} %shard_map.34), channel_id=1, source_target_pairs={{0,8},{1,9},{2,10},{3,11},{4,12},{5,13},{6,14},{7,15},{8,0},{9,1},... | collective-permute-start | bytes 147464 | tf_op jit(solution)/shard_map/ppermute | solution.py:60
  60.2 0.0 collective-permute-done.9.refs_5_
  60.2 1.1 %collective-permute-start.19 = (bf16[2,96,128]{2,1,0:T(8,128)(2,1)S(1)}, bf16[2,96,128]{2,1,0:T(8,128)(2,1)S(1)}, u32[]{:S(2)}, u32[]{:S(2)}) collective-permute-start(bf16[2,96,128]{2,1,0:T(8,128)(2,1)S(1)} %shard_map.34), channel_id=1, source_target_pairs={{0,12},{1,13},{2,14},{3,15},{4,8},{5,9},{6,10},{7,11},{8,4},{9,5},... | collective-permute-start | bytes 147464 | tf_op jit(solution)/shard_map/ppermute | solution.py:60
  61.4 0.0 collective-permute-done.11.refs_7_
  61.4 0.0 collective-permute-done.7.refs_3_
  61.4 1.8 %shard_map.31.refs_1_ = f32[13,96,256]{2,1,0:T(8,128)S(1)} custom-call(bf16[96,1152]{1,0:T(8,128)(2,1)S(1)} %get-tuple-element.26.refs_6_.refs_0_, bf16[96,1152]{1,0:T(8,128)(2,1)S(1)} %get-tuple-element.27.refs_7_.refs_1_, bf16[272,1152]{1,0:T(8,128)(2,1)S(1)} %collective-permute-done.1.refs_2_, bf16[96,1152]{1,0:T(8,128)(2,1)S(1)} %collective-permute-done.7.refs_3_, ...), custom_call_target="tpu_custom_call" | custom-call | flops 1000 | bytes 1000 | tf_op jit(solution)/shard_map/pallas_call | solution.py:74
  63.1 0.0 collective-permute-done.17.refs_4_
  63.1 0.6 collective-permute-done.18.refs_5_
  63.7 2.4 %collective-permute-done.19.refs_6_ = bf16[2,96,128]{2,1,0:T(8,128)(2,1)S(1)} collective-permute-done((bf16[2,96,128]{2,1,0:T(8,128)(2,1)S(1)}, bf16[2,96,128]{2,1,0:T(8,128)(2,1)S(1)}, u32[]{:S(2)}, u32[]{:S(2)}) %collective-permute-start.19) | collective-permute-done | bytes 49184 | tf_op jit(solution)/shard_map/ppermute | solution.py:60
  66.1 1.1 %shard_map.36 = (bf16[4,80,256]{2,1,0:T(8,128)(2,1)S(1)}, bf16[4,80,256]{2,1,0:T(8,128)(2,1)S(1)}, bf16[4,80,256]{2,1,0:T(8,128)(2,1)S(1)}) custom-call(f32[3,96,256]{2,1,0:T(8,128)S(1)} %get-tuple-element.30.refs_0_, f32[13,96,256]{2,1,0:T(8,128)S(1)} %shard_map.31.refs_1_, f32[4,96,128]{2,1,0:T(8,128)S(1)} %shard_map.33.a_ref.refs_2_, ...), custom_call_target="tpu_custom_call" | custom-call | flops 1000 | bytes 1000 | tf_op jit(solution)/shard_map/pallas_call | solution.py:74
  67.2 1.6 %collective-permute-start.20 = (bf16[4,80,256]{2,1,0:T(8,128)(2,1)S(1)}, bf16[4,80,256]{2,1,0:T(8,128)(2,1)S(1)}, u32[]{:S(2)}, u32[]{:S(2)}) collective-permute-start(bf16[4,80,256]{2,1,0:T(8,128)(2,1)S(1)} %get-tuple-element.38), channel_id=1, source_target_pairs={{0,2},{1,3},{2,0},{3,1},{4,6},{5,7},{6,4},{7,5},{8,10},{9,11},{10,... | collective-permute-start | bytes 491528 | tf_op jit(solution)/shard_map/ppermute | solution.py:60
  68.8 1.5 %collective-permute-start.21 = (bf16[4,80,256]{2,1,0:T(8,128)(2,1)S(1)}, bf16[4,80,256]{2,1,0:T(8,128)(2,1)S(1)}, u32[]{:S(2)}, u32[]{:S(2)}) collective-permute-start(bf16[4,80,256]{2,1,0:T(8,128)(2,1)S(1)} %get-tuple-element.39), channel_id=1, source_target_pairs={{0,16},{1,17},{2,18},{3,19},{4,20},{5,21},{6,22},{7,23},{8,24},{9,... | collective-permute-start | bytes 491528 | tf_op jit(solution)/shard_map/ppermute | solution.py:60
  70.3 0.5 collective-permute-start.22
  70.8 0.6 shard_map.35.refs_0_
  71.3 2.8 %collective-permute-done.20.refs_1_ = bf16[4,80,256]{2,1,0:T(8,128)(2,1)S(1)} collective-permute-done((bf16[4,80,256]{2,1,0:T(8,128)(2,1)S(1)}, bf16[4,80,256]{2,1,0:T(8,128)(2,1)S(1)}, u32[]{:S(2)}, u32[]{:S(2)}) %collective-permute-start.20) | collective-permute-done | bytes 163872 | tf_op jit(solution)/shard_map/ppermute | solution.py:60
  74.1 0.7 collective-permute-done.21.refs_2_
  74.8 2.1 %collective-permute-done.22.refs_3_ = bf16[4,80,256]{2,1,0:T(8,128)(2,1)S(1)} collective-permute-done((bf16[4,80,256]{2,1,0:T(8,128)(2,1)S(1)}, bf16[4,80,256]{2,1,0:T(8,128)(2,1)S(1)}, u32[]{:S(2)}, u32[]{:S(2)}) %collective-permute-start.22) | collective-permute-done | bytes 163872 | tf_op jit(solution)/shard_map/ppermute | solution.py:60
  76.9 1.1 %shard_map.37 = bf16[256,1280]{1,0:T(8,128)(2,1)} custom-call(bf16[4,80,256]{2,1,0:T(8,128)(2,1)S(1)} %shard_map.35.refs_0_, bf16[4,80,256]{2,1,0:T(8,128)(2,1)S(1)} %collective-permute-done.20.refs_1_, bf16[4,80,256]{2,1,0:T(8,128)(2,1)S(1)} %collective-permute-done.21.refs_2_, bf16[4,80,256]{2,1,0:T(8,128)(2,1)S(1)} %collective-permute-done.22.refs_3_), custom_call_target="tpu_custom_call" | custom-call | flops 1000 | bytes 1000 | tf_op jit(solution)/shard_map/pallas_call | solution.py:74
  (5 shorter events, 0.1 us)
Async XLA Ops:
  0.0 4.5 %collective-permute-start = (bf16[240,2240]{1,0:T(8,128)(2,1)}, bf16[240,2240]{1,0:T(8,128)(2,1)S(1)}, u32[]{:S(2)}, u32[]{:S(2)}) collective-permute-start(bf16[240,2240]{1,0:T(8,128)(2,1)} %bitcast.12), channel_id=1, source_target_pairs={{0,1},{1,0},{2,3},{3,2},{4,5},{5,4},{6,7},{7,6},{8,9},{9,8},{10,11... | collective-permute-start | bytes 3225608 | tf_op jit(solution)/shard_map/ppermute | solution.py:60
  0.5 33.6 %collective-permute-start.5 = (bf16[2240,256]{1,0:T(8,128)(2,1)}, bf16[2240,256]{1,0:T(8,128)(2,1)S(1)}, u32[]{:S(2)}, u32[]{:S(2)}) collective-permute-start(bf16[2240,256]{1,0:T(8,128)(2,1)} %bitcast.7), channel_id=1, source_target_pairs={{0,2},{1,3},{2,0},{3,1},{4,6},{5,7},{6,4},{7,5},{8,10},{9,11},{10,... | collective-permute-start | bytes 3440648 | tf_op jit(solution)/shard_map/ppermute | solution.py:60
  3.0 31.1 %collective-permute-start.6 = (bf16[2240,256]{1,0:T(8,128)(2,1)}, bf16[2240,256]{1,0:T(8,128)(2,1)S(1)}, u32[]{:S(2)}, u32[]{:S(2)}) collective-permute-start(bf16[2240,256]{1,0:T(8,128)(2,1)} %bitcast.8), channel_id=1, source_target_pairs={{0,16},{1,17},{2,18},{3,19},{4,20},{5,21},{6,22},{7,23},{8,24},{9,... | collective-permute-start | bytes 3440648 | tf_op jit(solution)/shard_map/ppermute | solution.py:60
  4.5 1.2 %copy-start.1 = (bf16[3,2240,80]{1,2,0:T(8,128)(2,1)S(1)}, bf16[3,2240,80]{1,2,0:T(8,128)(2,1)}, u32[]{:S(2)}) copy-start(bf16[3,2240,80]{1,2,0:T(8,128)(2,1)} %param.3) | copy-start | bytes 3225604
  6.0 24.7 %collective-permute-start.1 = (bf16[272,1152]{1,0:T(8,128)(2,1)S(1)}, bf16[272,1152]{1,0:T(8,128)(2,1)S(1)}, u32[]{:S(2)}, u32[]{:S(2)}) collective-permute-start(bf16[272,1152]{1,0:T(8,128)(2,1)S(1)} %get-tuple-element.25), channel_id=1, source_target_pairs={{0,4},{1,5},{2,6},{3,7},{4,0},{5,1},{6,2},{7,3},{8,12},{9,13},{10,... | collective-permute-start | bytes 1880072 | tf_op jit(solution)/shard_map/ppermute | solution.py:60
  7.6 22.3 %collective-permute-start.3 = (bf16[176,1152]{1,0:T(8,128)(2,1)S(1)}, bf16[176,1152]{1,0:T(8,128)(2,1)S(1)}, u32[]{:S(2)}, u32[]{:S(2)}) collective-permute-start(bf16[176,1152]{1,0:T(8,128)(2,1)S(1)} %get-tuple-element.23.refs_0_), channel_id=1, source_target_pairs={{0,8},{1,9},{2,10},{3,11},{4,12},{5,13},{6,14},{7,15},{8,0},{9,1},... | collective-permute-start | bytes 1216520 | tf_op jit(solution)/shard_map/ppermute | solution.py:60
  29.9 7.4 %collective-permute-start.4 = (bf16[176,1152]{1,0:T(8,128)(2,1)S(1)}, bf16[176,1152]{1,0:T(8,128)(2,1)S(1)}, u32[]{:S(2)}, u32[]{:S(2)}) collective-permute-start(bf16[176,1152]{1,0:T(8,128)(2,1)S(1)} %collective-permute-done.3.refs_4_), channel_id=1, source_target_pairs={{0,1},{1,0},{2,3},{3,2},{4,5},{5,4},{6,7},{7,6},{8,9},{9,8},{10,11... | collective-permute-start | bytes 1216520 | tf_op jit(solution)/shard_map/ppermute | solution.py:60
  30.8 7.7 %copy-start = (bf16[1,256,2240]{1,2,0:T(8,128)(2,1)S(1)}, bf16[1,256,2240]{1,2,0:T(8,128)(2,1)}, u32[]{:S(2)}) copy-start(bf16[1,256,2240]{1,2,0:T(8,128)(2,1)} %param.2) | copy-start | bytes 3440644
  30.8 7.7 %collective-permute-start.2 = (bf16[176,1152]{1,0:T(8,128)(2,1)S(1)}, bf16[176,1152]{1,0:T(8,128)(2,1)S(1)}, u32[]{:S(2)}, u32[]{:S(2)}) collective-permute-start(bf16[176,1152]{1,0:T(8,128)(2,1)S(1)} %slice.16), channel_id=1, source_target_pairs={{0,1},{1,0},{2,3},{3,2},{4,5},{5,4},{6,7},{7,6},{8,9},{9,8},{10,11... | collective-permute-start | bytes 1216520 | tf_op jit(solution)/shard_map/ppermute | solution.py:60
  30.8 17.6 %collective-permute-start.14 = (bf16[176,1152]{1,0:T(8,128)(2,1)S(1)}, bf16[176,1152]{1,0:T(8,128)(2,1)S(1)}, u32[]{:S(2)}, u32[]{:S(2)}) collective-permute-start(bf16[176,1152]{1,0:T(8,128)(2,1)S(1)} %collective-permute-done.3.refs_4_), channel_id=1, source_target_pairs={{0,4},{1,5},{2,6},{3,7},{4,0},{5,1},{6,2},{7,3},{8,12},{9,13},{10,... | collective-permute-start | bytes 1216520 | tf_op jit(solution)/shard_map/ppermute | solution.py:60
  34.1 17.7 %collective-permute-start.12 = (bf16[1120,256]{1,0:T(8,128)(2,1)S(1)}, bf16[1120,256]{1,0:T(8,128)(2,1)S(1)}, u32[]{:S(2)}, u32[]{:S(2)}) collective-permute-start(bf16[1120,256]{1,0:T(8,128)(2,1)S(1)} %slice.14), channel_id=1, source_target_pairs={{0,16},{1,17},{2,18},{3,19},{4,20},{5,21},{6,22},{7,23},{8,24},{9,... | collective-permute-start | bytes 1720328 | tf_op jit(solution)/shard_map/ppermute | solution.py:60
  35.7 16.1 %collective-permute-start.13 = (bf16[1120,256]{1,0:T(8,128)(2,1)S(1)}, bf16[1120,256]{1,0:T(8,128)(2,1)S(1)}, u32[]{:S(2)}, u32[]{:S(2)}) collective-permute-start(bf16[1120,256]{1,0:T(8,128)(2,1)S(1)} %slice.15), channel_id=1, source_target_pairs={{0,2},{1,3},{2,0},{3,1},{4,6},{5,7},{6,4},{7,5},{8,10},{9,11},{10,... | collective-permute-start | bytes 1720328 | tf_op jit(solution)/shard_map/ppermute | solution.py:60
  37.3 11.1 %collective-permute-start.8 = (bf16[96,1152]{1,0:T(8,128)(2,1)S(1)}, bf16[96,1152]{1,0:T(8,128)(2,1)S(1)}, u32[]{:S(2)}, u32[]{:S(2)}) collective-permute-start(bf16[96,1152]{1,0:T(8,128)(2,1)S(1)} %get-tuple-element.26.refs_6_.refs_0_), channel_id=1, source_target_pairs={{0,8},{1,9},{2,10},{3,11},{4,12},{5,13},{6,14},{7,15},{8,0},{9,1},... | collective-permute-start | bytes 663560 | tf_op jit(solution)/shard_map/ppermute | solution.py:60
  48.4 1.7 %collective-permute-start.15 = (bf16[176,1152]{1,0:T(8,128)(2,1)S(1)}, bf16[176,1152]{1,0:T(8,128)(2,1)S(1)}, u32[]{:S(2)}, u32[]{:S(2)}) collective-permute-start(bf16[176,1152]{1,0:T(8,128)(2,1)S(1)} %collective-permute-done.14.refs_0_), channel_id=1, source_target_pairs={{0,1},{1,0},{2,3},{3,2},{4,5},{5,4},{6,7},{7,6},{8,9},{9,8},{10,11... | collective-permute-start | bytes 1216520 | tf_op jit(solution)/shard_map/ppermute | solution.py:60
  48.4 7.8 %collective-permute-start.10 = (bf16[96,1152]{1,0:T(8,128)(2,1)S(1)}, bf16[96,1152]{1,0:T(8,128)(2,1)S(1)}, u32[]{:S(2)}, u32[]{:S(2)}) collective-permute-start(bf16[96,1152]{1,0:T(8,128)(2,1)S(1)} %collective-permute-done.8.refs_4_), channel_id=1, source_target_pairs={{0,4},{1,5},{2,6},{3,7},{4,0},{5,1},{6,2},{7,3},{8,12},{9,13},{10,... | collective-permute-start | bytes 663560 | tf_op jit(solution)/shard_map/ppermute | solution.py:60
  50.1 10.1 %collective-permute-start.9 = (bf16[96,1152]{1,0:T(8,128)(2,1)S(1)}, bf16[96,1152]{1,0:T(8,128)(2,1)S(1)}, u32[]{:S(2)}, u32[]{:S(2)}) collective-permute-start(bf16[96,1152]{1,0:T(8,128)(2,1)S(1)} %collective-permute-done.8.refs_4_), channel_id=1, source_target_pairs={{0,1},{1,0},{2,3},{3,2},{4,5},{5,4},{6,7},{7,6},{8,9},{9,8},{10,11... | collective-permute-start | bytes 663560 | tf_op jit(solution)/shard_map/ppermute | solution.py:60
  53.7 3.2 %collective-permute-start.16 = (f32[4,96,128]{2,1,0:T(8,128)S(1)}, f32[4,96,128]{2,1,0:T(8,128)S(1)}, u32[]{:S(2)}, u32[]{:S(2)}) collective-permute-start(f32[4,96,128]{2,1,0:T(8,128)S(1)} %shard_map.33.a_ref.refs_2_), channel_id=1, source_target_pairs={{0,1},{1,0},{2,3},{3,2},{4,5},{5,4},{6,7},{7,6},{8,9},{9,8},{10,11... | collective-permute-start | bytes 589832 | tf_op jit(solution)/shard_map/ppermute | solution.py:60
  56.3 5.1 %collective-permute-start.11 = (bf16[96,1152]{1,0:T(8,128)(2,1)S(1)}, bf16[96,1152]{1,0:T(8,128)(2,1)S(1)}, u32[]{:S(2)}, u32[]{:S(2)}) collective-permute-start(bf16[96,1152]{1,0:T(8,128)(2,1)S(1)} %collective-permute-done.10.refs_6_), channel_id=1, source_target_pairs={{0,1},{1,0},{2,3},{3,2},{4,5},{5,4},{6,7},{7,6},{8,9},{9,8},{10,11... | collective-permute-start | bytes 663560 | tf_op jit(solution)/shard_map/ppermute | solution.py:60
  56.3 5.1 %collective-permute-start.7 = (bf16[96,1152]{1,0:T(8,128)(2,1)S(1)}, bf16[96,1152]{1,0:T(8,128)(2,1)S(1)}, u32[]{:S(2)}, u32[]{:S(2)}) collective-permute-start(bf16[96,1152]{1,0:T(8,128)(2,1)S(1)} %slice.17), channel_id=1, source_target_pairs={{0,1},{1,0},{2,3},{3,2},{4,5},{5,4},{6,7},{7,6},{8,9},{9,8},{10,11... | collective-permute-start | bytes 663560 | tf_op jit(solution)/shard_map/ppermute | solution.py:60
  56.9 6.2 %collective-permute-start.17 = (bf16[2,96,128]{2,1,0:T(8,128)(2,1)S(1)}, bf16[2,96,128]{2,1,0:T(8,128)(2,1)S(1)}, u32[]{:S(2)}, u32[]{:S(2)}) collective-permute-start(bf16[2,96,128]{2,1,0:T(8,128)(2,1)S(1)} %shard_map.34), channel_id=1, source_target_pairs={{0,4},{1,5},{2,6},{3,7},{4,0},{5,1},{6,2},{7,3},{8,12},{9,13},{10,... | collective-permute-start | bytes 147464 | tf_op jit(solution)/shard_map/ppermute | solution.py:60
  57.3 6.4 %collective-permute-start.18 = (bf16[2,96,128]{2,1,0:T(8,128)(2,1)S(1)}, bf16[2,96,128]{2,1,0:T(8,128)(2,1)S(1)}, u32[]{:S(2)}, u32[]{:S(2)}) collective-permute-start(bf16[2,96,128]{2,1,0:T(8,128)(2,1)S(1)} %shard_map.34), channel_id=1, source_target_pairs={{0,8},{1,9},{2,10},{3,11},{4,12},{5,13},{6,14},{7,15},{8,0},{9,1},... | collective-permute-start | bytes 147464 | tf_op jit(solution)/shard_map/ppermute | solution.py:60
  60.2 5.9 %collective-permute-start.19 = (bf16[2,96,128]{2,1,0:T(8,128)(2,1)S(1)}, bf16[2,96,128]{2,1,0:T(8,128)(2,1)S(1)}, u32[]{:S(2)}, u32[]{:S(2)}) collective-permute-start(bf16[2,96,128]{2,1,0:T(8,128)(2,1)S(1)} %shard_map.34), channel_id=1, source_target_pairs={{0,12},{1,13},{2,14},{3,15},{4,8},{5,9},{6,10},{7,11},{8,4},{9,5},... | collective-permute-start | bytes 147464 | tf_op jit(solution)/shard_map/ppermute | solution.py:60
  67.2 6.9 %collective-permute-start.20 = (bf16[4,80,256]{2,1,0:T(8,128)(2,1)S(1)}, bf16[4,80,256]{2,1,0:T(8,128)(2,1)S(1)}, u32[]{:S(2)}, u32[]{:S(2)}) collective-permute-start(bf16[4,80,256]{2,1,0:T(8,128)(2,1)S(1)} %get-tuple-element.38), channel_id=1, source_target_pairs={{0,2},{1,3},{2,0},{3,1},{4,6},{5,7},{6,4},{7,5},{8,10},{9,11},{10,... | collective-permute-start | bytes 491528 | tf_op jit(solution)/shard_map/ppermute | solution.py:60
  68.8 6.0 %collective-permute-start.21 = (bf16[4,80,256]{2,1,0:T(8,128)(2,1)S(1)}, bf16[4,80,256]{2,1,0:T(8,128)(2,1)S(1)}, u32[]{:S(2)}, u32[]{:S(2)}) collective-permute-start(bf16[4,80,256]{2,1,0:T(8,128)(2,1)S(1)} %get-tuple-element.39), channel_id=1, source_target_pairs={{0,16},{1,17},{2,18},{3,19},{4,20},{5,21},{6,22},{7,23},{8,24},{9,... | collective-permute-start | bytes 491528 | tf_op jit(solution)/shard_map/ppermute | solution.py:60
  70.3 6.6 %collective-permute-start.22 = (bf16[4,80,256]{2,1,0:T(8,128)(2,1)S(1)}, bf16[4,80,256]{2,1,0:T(8,128)(2,1)S(1)}, u32[]{:S(2)}, u32[]{:S(2)}) collective-permute-start(bf16[4,80,256]{2,1,0:T(8,128)(2,1)S(1)} %get-tuple-element.40), channel_id=1, source_target_pairs={{0,18},{1,19},{2,16},{3,17},{4,22},{5,23},{6,20},{7,21},{8,26},{9,... | collective-permute-start | bytes 491528 | tf_op jit(solution)/shard_map/ppermute | solution.py:60

commit v6 on v5

--- a/solution.py
+++ b/solution.py
@@ -231,15 +231,6 @@
     return jnp.concatenate([jnp.concatenate(lanes, axis=-1)[..., :rows, :], *sums, a[..., rows + 4 :, :]], axis=-2)
 
 
-def pair_sum(plane, near):
-    def body(a_ref, b_ref, out_ref):
-        for i in range(2):
-            both = a_ref[i].astype(jnp.float32) + turn(b_ref[i].astype(jnp.float32), 1)
-            out_ref[i] = both.astype(out_ref.dtype)
-
-    return call(body, jax.ShapeDtypeStruct(plane.shape, plane.dtype), [VMEM] * 2, [], plane, near)
-
-
 def apply(half, ms, queries, mine, others, planes):
     arrays = []
     where = {}
@@ -360,12 +351,13 @@
     ((_, mine),) = project(half, [([(3, "kv")], [3])], blocks, frames, carried)
     others = send(mine, over_lo)
     plane = plane_sum(mine, others)
-    planes = [(send(plane, along(k)), k, lambda hi, k=k: jnp.bitwise_xor(hi, k) < hi) for k in (1, 2, 3)]
+    planes = [(send(plane, along(k)), k, lambda hi, k=k: jnp.bitwise_xor(hi, k) < hi) for k in (3, 2, 1)]
     last = [([(k, "q") for k in range(4)], [3]), ([(k, "q") for k in (1, 2, 3)], [0, 1, 2])]
     (made,) = project(half, last, blocks, frames)
     keep(made)
 
-    out1, out2, out3 = apply(half, [1, 2, 3], queries, mine, others, planes)
+    (out3,) = apply(half, [3], queries, mine, others, planes)
+    out2, out1 = apply(half, [2, 1], queries, mine, others, planes)
     (out0,) = apply(half, [0], queries, mine, others, planes)
     out1 = send(out1, over_b)
     out2 = send(out2, over_g)

time: 78.1 us -> 76.5 us (0.980)
  waiting for transfers between devices: 36.7 us -> 34.7 us
    ppermute x23, waiting for transfers between devices: 36.7 us -> 34.7 us  [send(): return lax.ppermute(a, AXES, pairs)]
    pallas_call x10 -> x11, Pallas kernels: 12.7 us -> 13 us  [call(): pl.pallas_call(body, out_shape=out, in_specs=ins, out_specs=jax.tree.map(...]
  transfers between devices with their start and end apart: 23 -> 23, of which waited for: 9 -> 9; matrix products, arithmetic and copies ran while one was open for 0% -> 0% of each run, Pallas kernels for 13% -> 15%
where the time goes in v6:
time: 76.5 us; the launch traced here: 76.3 us
  waiting for transfers between devices  34.7 us (45%)
  starting transfers between devices  27.1 us (35%)
  Pallas kernels  13 us (17%)
  local copies, waits for them, and re-layouts  1.38 us (2%)
    ppermute x23, waiting for transfers between devices, send(): return lax.ppermute(a, AXES, pairs)  34.7 us
    ppermute x23, starting transfers between devices, send(): return lax.ppermute(a, AXES, pairs)  27.1 us
    pallas_call x11, Pallas kernels, call(): pl.pallas_call(body, out_shape=out, in_specs=ins, out_specs=jax.tree.map(...  13 us
  transfers between devices with their start and end apart: 23, of which 9 were waited for; matrix products, arithmetic and copies ran while one was open for 0% of the time, Pallas kernels for 15%

profile of v6, /device:TPU:0, one launch (start us, length us, event | category | flops | bytes accessed | tf_op | source)
XLA Modules:
  0.0 76.3 jit_solution(9007204675945242414)
XLA Ops:
  0.0 0.5 collective-permute-start
  0.5 2.5 %collective-permute-start.5 = (bf16[2240,256]{1,0:T(8,128)(2,1)}, bf16[2240,256]{1,0:T(8,128)(2,1)S(1)}, u32[]{:S(2)}, u32[]{:S(2)}) collective-permute-start(bf16[2240,256]{1,0:T(8,128)(2,1)} %bitcast.7), channel_id=1, source_target_pairs={{0,2},{1,3},{2,0},{3,1},{4,6},{5,7},{6,4},{7,5},{8,10},{9,11},{10,... | collective-permute-start | bytes 3440648 | tf_op jit(solution)/shard_map/ppermute | solution.py:60
  3.0 1.5 %collective-permute-start.6 = (bf16[2240,256]{1,0:T(8,128)(2,1)}, bf16[2240,256]{1,0:T(8,128)(2,1)S(1)}, u32[]{:S(2)}, u32[]{:S(2)}) collective-permute-start(bf16[2240,256]{1,0:T(8,128)(2,1)} %bitcast.8), channel_id=1, source_target_pairs={{0,16},{1,17},{2,18},{3,19},{4,20},{5,21},{6,22},{7,23},{8,24},{9,... | collective-permute-start | bytes 3440648 | tf_op jit(solution)/shard_map/ppermute | solution.py:60
  4.5 0.0 collective-permute-done.swapped_ref
  4.5 0.0 copy-start.1
  4.5 1.2 %copy-done.1 = bf16[3,2240,80]{1,2,0:T(8,128)(2,1)S(1)} copy-done((bf16[3,2240,80]{1,2,0:T(8,128)(2,1)S(1)}, bf16[3,2240,80]{1,2,0:T(8,128)(2,1)}, u32[]{:S(2)}) %copy-start.1) | copy-done | bytes 1075224
  5.7 0.3 shard_map.28
  6.0 1.6 %collective-permute-start.1 = (bf16[272,1152]{1,0:T(8,128)(2,1)S(1)}, bf16[272,1152]{1,0:T(8,128)(2,1)S(1)}, u32[]{:S(2)}, u32[]{:S(2)}) collective-permute-start(bf16[272,1152]{1,0:T(8,128)(2,1)S(1)} %get-tuple-element.24), channel_id=1, source_target_pairs={{0,4},{1,5},{2,6},{3,7},{4,0},{5,1},{6,2},{7,3},{8,12},{9,13},{10,... | collective-permute-start | bytes 1880072 | tf_op jit(solution)/shard_map/ppermute | solution.py:60
  7.6 2.6 %collective-permute-start.3 = (bf16[176,1152]{1,0:T(8,128)(2,1)S(1)}, bf16[176,1152]{1,0:T(8,128)(2,1)S(1)}, u32[]{:S(2)}, u32[]{:S(2)}) collective-permute-start(bf16[176,1152]{1,0:T(8,128)(2,1)S(1)} %get-tuple-element.22.refs_0_), channel_id=1, source_target_pairs={{0,8},{1,9},{2,10},{3,11},{4,12},{5,13},{6,14},{7,15},{8,0},{9,1},... | collective-permute-start | bytes 1216520 | tf_op jit(solution)/shard_map/ppermute | solution.py:60
  10.2 19.7 %collective-permute-done.3.refs_4_ = bf16[176,1152]{1,0:T(8,128)(2,1)S(1)} collective-permute-done((bf16[176,1152]{1,0:T(8,128)(2,1)S(1)}, bf16[176,1152]{1,0:T(8,128)(2,1)S(1)}, u32[]{:S(2)}, u32[]{:S(2)}) %collective-permute-start.3) | collective-permute-done | bytes 405536 | tf_op jit(solution)/shard_map/ppermute | solution.py:60
  29.9 0.0 collective-permute-start.4
  29.9 0.8 %collective-permute-done.1.refs_2_ = bf16[272,1152]{1,0:T(8,128)(2,1)S(1)} collective-permute-done((bf16[272,1152]{1,0:T(8,128)(2,1)S(1)}, bf16[272,1152]{1,0:T(8,128)(2,1)S(1)}, u32[]{:S(2)}, u32[]{:S(2)}) %collective-permute-start.1) | collective-permute-done | bytes 626720 | tf_op jit(solution)/shard_map/ppermute | solution.py:60
  30.8 0.0 copy-start
  30.8 0.1 collective-permute-start.2
  30.8 3.2 %collective-permute-start.14 = (bf16[176,1152]{1,0:T(8,128)(2,1)S(1)}, bf16[176,1152]{1,0:T(8,128)(2,1)S(1)}, u32[]{:S(2)}, u32[]{:S(2)}) collective-permute-start(bf16[176,1152]{1,0:T(8,128)(2,1)S(1)} %collective-permute-done.3.refs_4_), channel_id=1, source_target_pairs={{0,4},{1,5},{2,6},{3,7},{4,0},{5,1},{6,2},{7,3},{8,12},{9,13},{10,... | collective-permute-start | bytes 1216520 | tf_op jit(solution)/shard_map/ppermute | solution.py:60
  34.1 0.0 collective-permute-done.5.refs_9_.refs_3_.refs_11_
  34.1 0.0 collective-permute-done.6.refs_10_.refs_4_.refs_12_
  34.1 1.6 %collective-permute-start.12 = (bf16[1120,256]{1,0:T(8,128)(2,1)S(1)}, bf16[1120,256]{1,0:T(8,128)(2,1)S(1)}, u32[]{:S(2)}, u32[]{:S(2)}) collective-permute-start(bf16[1120,256]{1,0:T(8,128)(2,1)S(1)} %slice.14), channel_id=1, source_target_pairs={{0,16},{1,17},{2,18},{3,19},{4,20},{5,21},{6,22},{7,23},{8,24},{9,... | collective-permute-start | bytes 1720328 | tf_op jit(solution)/shard_map/ppermute | solution.py:60
  35.7 1.6 %collective-permute-start.13 = (bf16[1120,256]{1,0:T(8,128)(2,1)S(1)}, bf16[1120,256]{1,0:T(8,128)(2,1)S(1)}, u32[]{:S(2)}, u32[]{:S(2)}) collective-permute-start(bf16[1120,256]{1,0:T(8,128)(2,1)S(1)} %slice.15), channel_id=1, source_target_pairs={{0,2},{1,3},{2,0},{3,1},{4,6},{5,7},{6,4},{7,5},{8,10},{9,11},{10,... | collective-permute-start | bytes 1720328 | tf_op jit(solution)/shard_map/ppermute | solution.py:60
  37.3 0.0 collective-permute-done.4.refs_5_
  37.3 1.1 %collective-permute-start.8 = (bf16[96,1152]{1,0:T(8,128)(2,1)S(1)}, bf16[96,1152]{1,0:T(8,128)(2,1)S(1)}, u32[]{:S(2)}, u32[]{:S(2)}) collective-permute-start(bf16[96,1152]{1,0:T(8,128)(2,1)S(1)} %get-tuple-element.25.refs_6_.refs_0_), channel_id=1, source_target_pairs={{0,8},{1,9},{2,10},{3,11},{4,12},{5,13},{6,14},{7,15},{8,0},{9,1},... | collective-permute-start | bytes 663560 | tf_op jit(solution)/shard_map/ppermute | solution.py:60
  38.4 0.0 collective-permute-done.2.refs_3_
  38.4 0.0 copy-done
  38.4 4.4 %shard_map.29 = (f32[3,96,256]{2,1,0:T(8,128)S(1)}, f32[3,96,128]{2,1,0:T(8,128)S(1)}, bf16[624,2240]{1,0:T(8,128)(2,1)S(1)}) custom-call(bf16[176,1152]{1,0:T(8,128)(2,1)S(1)} %get-tuple-element.22.refs_0_, bf16[176,1152]{1,0:T(8,128)(2,1)S(1)} %get-tuple-element.23.refs_1_, bf16[272,1152]{1,0:T(8,128)(2,1)S(1)} %collective-permute-done.1.refs_2_, ...), custom_call_target="tpu_custom_call" | custom-call | flops 1000 | bytes 1000 | tf_op jit(solution)/shard_map/pallas_call | solution.py:74
  42.8 5.6 %collective-permute-done.14.refs_0_ = bf16[176,1152]{1,0:T(8,128)(2,1)S(1)} collective-permute-done((bf16[176,1152]{1,0:T(8,128)(2,1)S(1)}, bf16[176,1152]{1,0:T(8,128)(2,1)S(1)}, u32[]{:S(2)}, u32[]{:S(2)}) %collective-permute-start.14) | collective-permute-done | bytes 405536 | tf_op jit(solution)/shard_map/ppermute | solution.py:60
  48.4 0.0 collective-permute-start.15
  48.4 0.0 collective-permute-done.8.refs_4_
  48.4 1.7 %collective-permute-start.10 = (bf16[96,1152]{1,0:T(8,128)(2,1)S(1)}, bf16[96,1152]{1,0:T(8,128)(2,1)S(1)}, u32[]{:S(2)}, u32[]{:S(2)}) collective-permute-start(bf16[96,1152]{1,0:T(8,128)(2,1)S(1)} %collective-permute-done.8.refs_4_), channel_id=1, source_target_pairs={{0,4},{1,5},{2,6},{3,7},{4,0},{5,1},{6,2},{7,3},{8,12},{9,13},{10,... | collective-permute-start | bytes 663560 | tf_op jit(solution)/shard_map/ppermute | solution.py:60
  50.1 0.0 collective-permute-start.9
  50.1 0.0 collective-permute-done.15.refs_1_
  50.2 1.7 %shard_map.30.refs_4_.refs_5_.refs_6_ = f32[3,96,128]{2,1,0:T(8,128)S(1)} custom-call(bf16[176,1152]{1,0:T(8,128)(2,1)S(1)} %collective-permute-done.14.refs_0_, bf16[176,1152]{1,0:T(8,128)(2,1)S(1)} %collective-permute-done.15.refs_1_, bf16[2240,256]{1,0:T(8,128)(2,1)S(1)} %bitcast.10, ...), custom_call_target="tpu_custom_call" | custom-call | flops 1000 | bytes 1000 | tf_op jit(solution)/shard_map/pallas_call | solution.py:74
  51.8 0.0 collective-permute-done.12.refs_8_.refs_1_.refs_2_
  51.8 0.0 collective-permute-done.13.refs_9_.refs_2_.refs_3_
  51.9 1.1 %shard_map.32.refs_7_ = f32[1,96,128]{2,1,0:T(8,128)S(1)} custom-call(bf16[624,2240]{1,0:T(8,128)(2,1)S(1)} %get-tuple-element.36.refs_0_, bf16[1120,256]{1,0:T(8,128)(2,1)S(1)} %collective-permute-done.12.refs_8_.refs_1_.refs_2_, bf16[1120,256]{1,0:T(8,128)(2,1)S(1)} %collective-permute-done.13.refs_9_.refs_2_.refs_3_), custom_call_target="tpu_custom_call" | custom-call | flops 1000 | bytes 1000 | tf_op jit(solution)/shard_map/pallas_call | solution.py:74
  53.0 0.7 shard_map.33.a_ref.refs_2_.refs_1_
  53.7 0.5 collective-permute-start.16
  54.2 2.0 %collective-permute-done.10.refs_6_ = bf16[96,1152]{1,0:T(8,128)(2,1)S(1)} collective-permute-done((bf16[96,1152]{1,0:T(8,128)(2,1)S(1)}, bf16[96,1152]{1,0:T(8,128)(2,1)S(1)}, u32[]{:S(2)}, u32[]{:S(2)}) %collective-permute-start.10) | collective-permute-done | bytes 221216 | tf_op jit(solution)/shard_map/ppermute | solution.py:60
  56.3 0.0 collective-permute-start.11
  56.3 0.6 collective-permute-start.7
  56.9 0.0 collective-permute-done.16.b_ref.refs_3_.refs_2_
  56.9 2.7 %collective-permute-start.17 = (bf16[2,96,128]{2,1,0:T(8,128)(2,1)S(1)}, bf16[2,96,128]{2,1,0:T(8,128)(2,1)S(1)}, u32[]{:S(2)}, u32[]{:S(2)}) collective-permute-start(bf16[2,96,128]{2,1,0:T(8,128)(2,1)S(1)} %shard_map.34), channel_id=1, source_target_pairs={{0,12},{1,13},{2,14},{3,15},{4,8},{5,9},{6,10},{7,11},{8,4},{9,5},... | collective-permute-start | bytes 147464 | tf_op jit(solution)/shard_map/ppermute | solution.py:60
  59.6 0.0 collective-permute-start.18
  59.7 0.0 collective-permute-done.9.refs_5_
  59.7 1.7 %collective-permute-start.19 = (bf16[2,96,128]{2,1,0:T(8,128)(2,1)S(1)}, bf16[2,96,128]{2,1,0:T(8,128)(2,1)S(1)}, u32[]{:S(2)}, u32[]{:S(2)}) collective-permute-start(bf16[2,96,128]{2,1,0:T(8,128)(2,1)S(1)} %shard_map.34), channel_id=1, source_target_pairs={{0,4},{1,5},{2,6},{3,7},{4,0},{5,1},{6,2},{7,3},{8,12},{9,13},{10,... | collective-permute-start | bytes 147464 | tf_op jit(solution)/shard_map/ppermute | solution.py:60
  61.4 0.0 collective-permute-done.11.refs_7_
  61.4 0.0 collective-permute-done.7.refs_3_
  61.4 1.7 %shard_map.31.refs_1_.refs_0_ = f32[13,96,256]{2,1,0:T(8,128)S(1)} custom-call(bf16[96,1152]{1,0:T(8,128)(2,1)S(1)} %get-tuple-element.25.refs_6_.refs_0_, bf16[96,1152]{1,0:T(8,128)(2,1)S(1)} %get-tuple-element.26.refs_7_.refs_1_, bf16[272,1152]{1,0:T(8,128)(2,1)S(1)} %collective-permute-done.1.refs_2_, ...), custom_call_target="tpu_custom_call" | custom-call | flops 1000 | bytes 1000 | tf_op jit(solution)/shard_map/pallas_call | solution.py:74
  63.1 0.0 collective-permute-done.17.refs_4_.refs_3_
  63.1 1.6 %collective-permute-done.18.refs_5_.refs_4_ = bf16[2,96,128]{2,1,0:T(8,128)(2,1)S(1)} collective-permute-done((bf16[2,96,128]{2,1,0:T(8,128)(2,1)S(1)}, bf16[2,96,128]{2,1,0:T(8,128)(2,1)S(1)}, u32[]{:S(2)}, u32[]{:S(2)}) %collective-permute-start.18) | collective-permute-done | bytes 49184 | tf_op jit(solution)/shard_map/ppermute | solution.py:60
  64.7 0.1 collective-permute-done.19.refs_6_.refs_5_
  64.8 0.6 shard_map.37
  65.3 2.5 %collective-permute-start.22 = (bf16[4,80,256]{2,1,0:T(8,128)(2,1)S(1)}, bf16[4,80,256]{2,1,0:T(8,128)(2,1)S(1)}, u32[]{:S(2)}, u32[]{:S(2)}) collective-permute-start(bf16[4,80,256]{2,1,0:T(8,128)(2,1)S(1)} %shard_map.37), channel_id=1, source_target_pairs={{0,18},{1,19},{2,16},{3,17},{4,22},{5,23},{6,20},{7,21},{8,26},{9,... | collective-permute-start | bytes 491528 | tf_op jit(solution)/shard_map/ppermute | solution.py:60
  67.9 0.8 %shard_map.36 = (bf16[4,80,256]{2,1,0:T(8,128)(2,1)S(1)}, bf16[4,80,256]{2,1,0:T(8,128)(2,1)S(1)}) custom-call(f32[3,96,256]{2,1,0:T(8,128)S(1)} %get-tuple-element.29.refs_0_, f32[13,96,256]{2,1,0:T(8,128)S(1)} %shard_map.31.refs_1_.refs_0_, f32[4,96,128]{2,1,0:T(8,128)S(1)} %shard_map.33.a_ref.refs_2_.refs_1_, ...), custom_call_target="tpu_custom_call" | custom-call | flops 1000 | bytes 1000 | tf_op jit(solution)/shard_map/pallas_call | solution.py:74
  68.7 0.6 collective-permute-start.20
  69.3 0.5 collective-permute-start.21
  69.8 0.6 shard_map.35.refs_0_
  70.4 2.0 %collective-permute-done.22.refs_3_ = bf16[4,80,256]{2,1,0:T(8,128)(2,1)S(1)} collective-permute-done((bf16[4,80,256]{2,1,0:T(8,128)(2,1)S(1)}, bf16[4,80,256]{2,1,0:T(8,128)(2,1)S(1)}, u32[]{:S(2)}, u32[]{:S(2)}) %collective-permute-start.22) | collective-permute-done | bytes 163872 | tf_op jit(solution)/shard_map/ppermute | solution.py:60
  72.4 2.8 %collective-permute-done.20.refs_1_ = bf16[4,80,256]{2,1,0:T(8,128)(2,1)S(1)} collective-permute-done((bf16[4,80,256]{2,1,0:T(8,128)(2,1)S(1)}, bf16[4,80,256]{2,1,0:T(8,128)(2,1)S(1)}, u32[]{:S(2)}, u32[]{:S(2)}) %collective-permute-start.20) | collective-permute-done | bytes 163872 | tf_op jit(solution)/shard_map/ppermute | solution.py:60
  75.1 0.1 collective-permute-done.21.refs_2_
  75.2 1.1 %shard_map.38 = bf16[256,1280]{1,0:T(8,128)(2,1)} custom-call(bf16[4,80,256]{2,1,0:T(8,128)(2,1)S(1)} %shard_map.35.refs_0_, bf16[4,80,256]{2,1,0:T(8,128)(2,1)S(1)} %collective-permute-done.20.refs_1_, bf16[4,80,256]{2,1,0:T(8,128)(2,1)S(1)} %collective-permute-done.21.refs_2_, bf16[4,80,256]{2,1,0:T(8,128)(2,1)S(1)} %collective-permute-done.22.refs_3_), custom_call_target="tpu_custom_call" | custom-call | flops 1000 | bytes 1000 | tf_op jit(solution)/shard_map/pallas_call | solution.py:74
  (5 shorter events, 0.1 us)
Async XLA Ops:
  0.0 4.5 %collective-permute-start = (bf16[240,2240]{1,0:T(8,128)(2,1)}, bf16[240,2240]{1,0:T(8,128)(2,1)S(1)}, u32[]{:S(2)}, u32[]{:S(2)}) collective-permute-start(bf16[240,2240]{1,0:T(8,128)(2,1)} %bitcast.12), channel_id=1, source_target_pairs={{0,1},{1,0},{2,3},{3,2},{4,5},{5,4},{6,7},{7,6},{8,9},{9,8},{10,11... | collective-permute-start | bytes 3225608 | tf_op jit(solution)/shard_map/ppermute | solution.py:60
  0.5 33.6 %collective-permute-start.5 = (bf16[2240,256]{1,0:T(8,128)(2,1)}, bf16[2240,256]{1,0:T(8,128)(2,1)S(1)}, u32[]{:S(2)}, u32[]{:S(2)}) collective-permute-start(bf16[2240,256]{1,0:T(8,128)(2,1)} %bitcast.7), channel_id=1, source_target_pairs={{0,2},{1,3},{2,0},{3,1},{4,6},{5,7},{6,4},{7,5},{8,10},{9,11},{10,... | collective-permute-start | bytes 3440648 | tf_op jit(solution)/shard_map/ppermute | solution.py:60
  3.0 31.1 %collective-permute-start.6 = (bf16[2240,256]{1,0:T(8,128)(2,1)}, bf16[2240,256]{1,0:T(8,128)(2,1)S(1)}, u32[]{:S(2)}, u32[]{:S(2)}) collective-permute-start(bf16[2240,256]{1,0:T(8,128)(2,1)} %bitcast.8), channel_id=1, source_target_pairs={{0,16},{1,17},{2,18},{3,19},{4,20},{5,21},{6,22},{7,23},{8,24},{9,... | collective-permute-start | bytes 3440648 | tf_op jit(solution)/shard_map/ppermute | solution.py:60
  4.5 1.2 %copy-start.1 = (bf16[3,2240,80]{1,2,0:T(8,128)(2,1)S(1)}, bf16[3,2240,80]{1,2,0:T(8,128)(2,1)}, u32[]{:S(2)}) copy-start(bf16[3,2240,80]{1,2,0:T(8,128)(2,1)} %param.3) | copy-start | bytes 3225604
  6.0 24.7 %collective-permute-start.1 = (bf16[272,1152]{1,0:T(8,128)(2,1)S(1)}, bf16[272,1152]{1,0:T(8,128)(2,1)S(1)}, u32[]{:S(2)}, u32[]{:S(2)}) collective-permute-start(bf16[272,1152]{1,0:T(8,128)(2,1)S(1)} %get-tuple-element.24), channel_id=1, source_target_pairs={{0,4},{1,5},{2,6},{3,7},{4,0},{5,1},{6,2},{7,3},{8,12},{9,13},{10,... | collective-permute-start | bytes 1880072 | tf_op jit(solution)/shard_map/ppermute | solution.py:60
  7.6 22.3 %collective-permute-start.3 = (bf16[176,1152]{1,0:T(8,128)(2,1)S(1)}, bf16[176,1152]{1,0:T(8,128)(2,1)S(1)}, u32[]{:S(2)}, u32[]{:S(2)}) collective-permute-start(bf16[176,1152]{1,0:T(8,128)(2,1)S(1)} %get-tuple-element.22.refs_0_), channel_id=1, source_target_pairs={{0,8},{1,9},{2,10},{3,11},{4,12},{5,13},{6,14},{7,15},{8,0},{9,1},... | collective-permute-start | bytes 1216520 | tf_op jit(solution)/shard_map/ppermute | solution.py:60
  29.9 7.4 %collective-permute-start.4 = (bf16[176,1152]{1,0:T(8,128)(2,1)S(1)}, bf16[176,1152]{1,0:T(8,128)(2,1)S(1)}, u32[]{:S(2)}, u32[]{:S(2)}) collective-permute-start(bf16[176,1152]{1,0:T(8,128)(2,1)S(1)} %collective-permute-done.3.refs_4_), channel_id=1, source_target_pairs={{0,1},{1,0},{2,3},{3,2},{4,5},{5,4},{6,7},{7,6},{8,9},{9,8},{10,11... | collective-permute-start | bytes 1216520 | tf_op jit(solution)/shard_map/ppermute | solution.py:60
  30.8 7.7 %copy-start = (bf16[1,256,2240]{1,2,0:T(8,128)(2,1)S(1)}, bf16[1,256,2240]{1,2,0:T(8,128)(2,1)}, u32[]{:S(2)}) copy-start(bf16[1,256,2240]{1,2,0:T(8,128)(2,1)} %param.2) | copy-start | bytes 3440644
  30.8 7.7 %collective-permute-start.2 = (bf16[176,1152]{1,0:T(8,128)(2,1)S(1)}, bf16[176,1152]{1,0:T(8,128)(2,1)S(1)}, u32[]{:S(2)}, u32[]{:S(2)}) collective-permute-start(bf16[176,1152]{1,0:T(8,128)(2,1)S(1)} %slice.16), channel_id=1, source_target_pairs={{0,1},{1,0},{2,3},{3,2},{4,5},{5,4},{6,7},{7,6},{8,9},{9,8},{10,11... | collective-permute-start | bytes 1216520 | tf_op jit(solution)/shard_map/ppermute | solution.py:60
  30.8 17.6 %collective-permute-start.14 = (bf16[176,1152]{1,0:T(8,128)(2,1)S(1)}, bf16[176,1152]{1,0:T(8,128)(2,1)S(1)}, u32[]{:S(2)}, u32[]{:S(2)}) collective-permute-start(bf16[176,1152]{1,0:T(8,128)(2,1)S(1)} %collective-permute-done.3.refs_4_), channel_id=1, source_target_pairs={{0,4},{1,5},{2,6},{3,7},{4,0},{5,1},{6,2},{7,3},{8,12},{9,13},{10,... | collective-permute-start | bytes 1216520 | tf_op jit(solution)/shard_map/ppermute | solution.py:60
  34.1 17.7 %collective-permute-start.12 = (bf16[1120,256]{1,0:T(8,128)(2,1)S(1)}, bf16[1120,256]{1,0:T(8,128)(2,1)S(1)}, u32[]{:S(2)}, u32[]{:S(2)}) collective-permute-start(bf16[1120,256]{1,0:T(8,128)(2,1)S(1)} %slice.14), channel_id=1, source_target_pairs={{0,16},{1,17},{2,18},{3,19},{4,20},{5,21},{6,22},{7,23},{8,24},{9,... | collective-permute-start | bytes 1720328 | tf_op jit(solution)/shard_map/ppermute | solution.py:60
  35.7 16.1 %collective-permute-start.13 = (bf16[1120,256]{1,0:T(8,128)(2,1)S(1)}, bf16[1120,256]{1,0:T(8,128)(2,1)S(1)}, u32[]{:S(2)}, u32[]{:S(2)}) collective-permute-start(bf16[1120,256]{1,0:T(8,128)(2,1)S(1)} %slice.15), channel_id=1, source_target_pairs={{0,2},{1,3},{2,0},{3,1},{4,6},{5,7},{6,4},{7,5},{8,10},{9,11},{10,... | collective-permute-start | bytes 1720328 | tf_op jit(solution)/shard_map/ppermute | solution.py:60
  37.3 11.1 %collective-permute-start.8 = (bf16[96,1152]{1,0:T(8,128)(2,1)S(1)}, bf16[96,1152]{1,0:T(8,128)(2,1)S(1)}, u32[]{:S(2)}, u32[]{:S(2)}) collective-permute-start(bf16[96,1152]{1,0:T(8,128)(2,1)S(1)} %get-tuple-element.25.refs_6_.refs_0_), channel_id=1, source_target_pairs={{0,8},{1,9},{2,10},{3,11},{4,12},{5,13},{6,14},{7,15},{8,0},{9,1},... | collective-permute-start | bytes 663560 | tf_op jit(solution)/shard_map/ppermute | solution.py:60
  48.4 1.7 %collective-permute-start.15 = (bf16[176,1152]{1,0:T(8,128)(2,1)S(1)}, bf16[176,1152]{1,0:T(8,128)(2,1)S(1)}, u32[]{:S(2)}, u32[]{:S(2)}) collective-permute-start(bf16[176,1152]{1,0:T(8,128)(2,1)S(1)} %collective-permute-done.14.refs_0_), channel_id=1, source_target_pairs={{0,1},{1,0},{2,3},{3,2},{4,5},{5,4},{6,7},{7,6},{8,9},{9,8},{10,11... | collective-permute-start | bytes 1216520 | tf_op jit(solution)/shard_map/ppermute | solution.py:60
  48.4 7.8 %collective-permute-start.10 = (bf16[96,1152]{1,0:T(8,128)(2,1)S(1)}, bf16[96,1152]{1,0:T(8,128)(2,1)S(1)}, u32[]{:S(2)}, u32[]{:S(2)}) collective-permute-start(bf16[96,1152]{1,0:T(8,128)(2,1)S(1)} %collective-permute-done.8.refs_4_), channel_id=1, source_target_pairs={{0,4},{1,5},{2,6},{3,7},{4,0},{5,1},{6,2},{7,3},{8,12},{9,13},{10,... | collective-permute-start | bytes 663560 | tf_op jit(solution)/shard_map/ppermute | solution.py:60
  50.1 9.5 %collective-permute-start.9 = (bf16[96,1152]{1,0:T(8,128)(2,1)S(1)}, bf16[96,1152]{1,0:T(8,128)(2,1)S(1)}, u32[]{:S(2)}, u32[]{:S(2)}) collective-permute-start(bf16[96,1152]{1,0:T(8,128)(2,1)S(1)} %collective-permute-done.8.refs_4_), channel_id=1, source_target_pairs={{0,1},{1,0},{2,3},{3,2},{4,5},{5,4},{6,7},{7,6},{8,9},{9,8},{10,11... | collective-permute-start | bytes 663560 | tf_op jit(solution)/shard_map/ppermute | solution.py:60
  53.7 3.2 %collective-permute-start.16 = (f32[4,96,128]{2,1,0:T(8,128)S(1)}, f32[4,96,128]{2,1,0:T(8,128)S(1)}, u32[]{:S(2)}, u32[]{:S(2)}) collective-permute-start(f32[4,96,128]{2,1,0:T(8,128)S(1)} %shard_map.33.a_ref.refs_2_.refs_1_), channel_id=1, source_target_pairs={{0,1},{1,0},{2,3},{3,2},{4,5},{5,4},{6,7},{7,6},{8,9},{9,8},{10,11... | collective-permute-start | bytes 589832 | tf_op jit(solution)/shard_map/ppermute | solution.py:60
  56.3 5.1 %collective-permute-start.11 = (bf16[96,1152]{1,0:T(8,128)(2,1)S(1)}, bf16[96,1152]{1,0:T(8,128)(2,1)S(1)}, u32[]{:S(2)}, u32[]{:S(2)}) collective-permute-start(bf16[96,1152]{1,0:T(8,128)(2,1)S(1)} %collective-permute-done.10.refs_6_), channel_id=1, source_target_pairs={{0,1},{1,0},{2,3},{3,2},{4,5},{5,4},{6,7},{7,6},{8,9},{9,8},{10,11... | collective-permute-start | bytes 663560 | tf_op jit(solution)/shard_map/ppermute | solution.py:60
  56.3 5.1 %collective-permute-start.7 = (bf16[96,1152]{1,0:T(8,128)(2,1)S(1)}, bf16[96,1152]{1,0:T(8,128)(2,1)S(1)}, u32[]{:S(2)}, u32[]{:S(2)}) collective-permute-start(bf16[96,1152]{1,0:T(8,128)(2,1)S(1)} %slice.17), channel_id=1, source_target_pairs={{0,1},{1,0},{2,3},{3,2},{4,5},{5,4},{6,7},{7,6},{8,9},{9,8},{10,11... | collective-permute-start | bytes 663560 | tf_op jit(solution)/shard_map/ppermute | solution.py:60
  56.9 6.2 %collective-permute-start.17 = (bf16[2,96,128]{2,1,0:T(8,128)(2,1)S(1)}, bf16[2,96,128]{2,1,0:T(8,128)(2,1)S(1)}, u32[]{:S(2)}, u32[]{:S(2)}) collective-permute-start(bf16[2,96,128]{2,1,0:T(8,128)(2,1)S(1)} %shard_map.34), channel_id=1, source_target_pairs={{0,12},{1,13},{2,14},{3,15},{4,8},{5,9},{6,10},{7,11},{8,4},{9,5},... | collective-permute-start | bytes 147464 | tf_op jit(solution)/shard_map/ppermute | solution.py:60
  59.6 5.0 %collective-permute-start.18 = (bf16[2,96,128]{2,1,0:T(8,128)(2,1)S(1)}, bf16[2,96,128]{2,1,0:T(8,128)(2,1)S(1)}, u32[]{:S(2)}, u32[]{:S(2)}) collective-permute-start(bf16[2,96,128]{2,1,0:T(8,128)(2,1)S(1)} %shard_map.34), channel_id=1, source_target_pairs={{0,8},{1,9},{2,10},{3,11},{4,12},{5,13},{6,14},{7,15},{8,0},{9,1},... | collective-permute-start | bytes 147464 | tf_op jit(solution)/shard_map/ppermute | solution.py:60
  59.7 5.1 %collective-permute-start.19 = (bf16[2,96,128]{2,1,0:T(8,128)(2,1)S(1)}, bf16[2,96,128]{2,1,0:T(8,128)(2,1)S(1)}, u32[]{:S(2)}, u32[]{:S(2)}) collective-permute-start(bf16[2,96,128]{2,1,0:T(8,128)(2,1)S(1)} %shard_map.34), channel_id=1, source_target_pairs={{0,4},{1,5},{2,6},{3,7},{4,0},{5,1},{6,2},{7,3},{8,12},{9,13},{10,... | collective-permute-start | bytes 147464 | tf_op jit(solution)/shard_map/ppermute | solution.py:60
  65.3 7.0 %collective-permute-start.22 = (bf16[4,80,256]{2,1,0:T(8,128)(2,1)S(1)}, bf16[4,80,256]{2,1,0:T(8,128)(2,1)S(1)}, u32[]{:S(2)}, u32[]{:S(2)}) collective-permute-start(bf16[4,80,256]{2,1,0:T(8,128)(2,1)S(1)} %shard_map.37), channel_id=1, source_target_pairs={{0,18},{1,19},{2,16},{3,17},{4,22},{5,23},{6,20},{7,21},{8,26},{9,... | collective-permute-start | bytes 491528 | tf_op jit(solution)/shard_map/ppermute | solution.py:60
  68.7 6.5 %collective-permute-start.20 = (bf16[4,80,256]{2,1,0:T(8,128)(2,1)S(1)}, bf16[4,80,256]{2,1,0:T(8,128)(2,1)S(1)}, u32[]{:S(2)}, u32[]{:S(2)}) collective-permute-start(bf16[4,80,256]{2,1,0:T(8,128)(2,1)S(1)} %get-tuple-element.37), channel_id=1, source_target_pairs={{0,2},{1,3},{2,0},{3,1},{4,6},{5,7},{6,4},{7,5},{8,10},{9,11},{10,... | collective-permute-start | bytes 491528 | tf_op jit(solution)/shard_map/ppermute | solution.py:60
  69.3 5.9 %collective-permute-start.21 = (bf16[4,80,256]{2,1,0:T(8,128)(2,1)S(1)}, bf16[4,80,256]{2,1,0:T(8,128)(2,1)S(1)}, u32[]{:S(2)}, u32[]{:S(2)}) collective-permute-start(bf16[4,80,256]{2,1,0:T(8,128)(2,1)S(1)} %get-tuple-element.38), channel_id=1, source_target_pairs={{0,16},{1,17},{2,18},{3,19},{4,20},{5,21},{6,22},{7,23},{8,24},{9,... | collective-permute-start | bytes 491528 | tf_op jit(solution)/shard_map/ppermute | solution.py:60

commit v7 on v6

--- a/solution.py
+++ b/solution.py
@@ -77,7 +77,7 @@
         in_specs=ins,
         out_specs=jax.tree.map(lambda _: VMEM, out),
         scratch_shapes=scratch,
-        compiler_params=pltpu.CompilerParams(vmem_limit_bytes=16 * 2**20),
+        compiler_params=pltpu.CompilerParams(vmem_limit_bytes=8 * 2**20),
         cost_estimate=LIGHT,
     )(*operands)
 
@@ -182,9 +182,11 @@
             start = pieces[named[0]][1]
             stop = pieces[named[-1]][1] + tall[named[-1][1]]
             for m in ms:
-                x = [ins[p][...] for p in parts[m]]
-                x = jnp.concatenate(x, axis=0) if len(x) > 1 else x[0]
-                all_made = dot(w_ref[start:stop], x, ((1,), (0,)))
+                all_made, at = 0.0, 0
+                for p in parts[m]:
+                    n = ins[p].shape[0]
+                    all_made += dot(w_ref[start:stop, at : at + n], ins[p][...], ((1,), (0,)))
+                    at += n
                 for k, what in named:
                     at = pieces[k, what][1] - start
                     made = all_made[at : at + tall[what]]
@@ -328,7 +330,7 @@
     near = send(whole, along(1))
     next_b, next_g = lax.optimization_barrier((next_b, next_g))
     last_kv = send(far_kv, along(1))
-    cut = depth // 2
+    cut = depth // 512 * 256
     across = [send(next_b[:cut], over_g), send(next_g[cut:], over_b)]
     frames = [[own], [next_b], [next_g], across]
     blocks = [{"kv": [(kv, other_kv, 0, 0, kv_rows)], "q": [(q, other_q, 0, 0, more)]} for _ in range(4)]

time: 76.5 us -> 76.4 us (level)
  transfers between devices with their start and end apart: 23 -> 23, of which waited for: 9 -> 8; matrix products, arithmetic and copies ran while one was open for 0% -> 0% of each run, Pallas kernels for 15% -> 15%
where the time goes in v7:
time: 76.4 us; the launch traced here: 76.3 us
  waiting for transfers between devices  34.7 us (45%)
  starting transfers between devices  27.1 us (35%)
  Pallas kernels  13 us (17%)
  local copies, waits for them, and re-layouts  1.38 us (2%)
    ppermute x23, waiting for transfers between devices, send(): return lax.ppermute(a, AXES, pairs)  34.7 us
    ppermute x23, starting transfers between devices, send(): return lax.ppermute(a, AXES, pairs)  27.1 us
    pallas_call x11, Pallas kernels, call(): pl.pallas_call(body, out_shape=out, in_specs=ins, out_specs=jax.tree.map(...  13 us
  transfers between devices with their start and end apart: 23, of which 8 were waited for; matrix products, arithmetic and copies ran while one was open for 0% of the time, Pallas kernels for 15%

profile of v7, /device:TPU:0, one launch (start us, length us, event | category | flops | bytes accessed | tf_op | source)
XLA Modules:
  0.0 76.3 jit_solution(9687060895614876686)
XLA Ops:
  0.0 0.5 collective-permute-start
  0.5 2.5 %collective-permute-start.5 = (bf16[2240,256]{1,0:T(8,128)(2,1)}, bf16[2240,256]{1,0:T(8,128)(2,1)S(1)}, u32[]{:S(2)}, u32[]{:S(2)}) collective-permute-start(bf16[2240,256]{1,0:T(8,128)(2,1)} %bitcast.7), channel_id=1, source_target_pairs={{0,2},{1,3},{2,0},{3,1},{4,6},{5,7},{6,4},{7,5},{8,10},{9,11},{10,... | collective-permute-start | bytes 3440648 | tf_op jit(solution)/shard_map/ppermute | solution.py:60
  3.0 1.5 %collective-permute-start.6 = (bf16[2240,256]{1,0:T(8,128)(2,1)}, bf16[2240,256]{1,0:T(8,128)(2,1)S(1)}, u32[]{:S(2)}, u32[]{:S(2)}) collective-permute-start(bf16[2240,256]{1,0:T(8,128)(2,1)} %bitcast.8), channel_id=1, source_target_pairs={{0,16},{1,17},{2,18},{3,19},{4,20},{5,21},{6,22},{7,23},{8,24},{9,... | collective-permute-start | bytes 3440648 | tf_op jit(solution)/shard_map/ppermute | solution.py:60
  4.5 0.0 collective-permute-done.swapped_ref
  4.5 0.0 copy-start.1
  4.5 1.2 %copy-done.1 = bf16[3,2240,80]{1,2,0:T(8,128)(2,1)S(1)} copy-done((bf16[3,2240,80]{1,2,0:T(8,128)(2,1)S(1)}, bf16[3,2240,80]{1,2,0:T(8,128)(2,1)}, u32[]{:S(2)}) %copy-start.1) | copy-done | bytes 1075224
  5.7 0.3 shard_map.28
  6.0 1.6 %collective-permute-start.1 = (bf16[272,1152]{1,0:T(8,128)(2,1)S(1)}, bf16[272,1152]{1,0:T(8,128)(2,1)S(1)}, u32[]{:S(2)}, u32[]{:S(2)}) collective-permute-start(bf16[272,1152]{1,0:T(8,128)(2,1)S(1)} %get-tuple-element.24), channel_id=1, source_target_pairs={{0,4},{1,5},{2,6},{3,7},{4,0},{5,1},{6,2},{7,3},{8,12},{9,13},{10,... | collective-permute-start | bytes 1880072 | tf_op jit(solution)/shard_map/ppermute | solution.py:60
  7.6 2.6 %collective-permute-start.3 = (bf16[176,1152]{1,0:T(8,128)(2,1)S(1)}, bf16[176,1152]{1,0:T(8,128)(2,1)S(1)}, u32[]{:S(2)}, u32[]{:S(2)}) collective-permute-start(bf16[176,1152]{1,0:T(8,128)(2,1)S(1)} %get-tuple-element.22.refs_0_), channel_id=1, source_target_pairs={{0,8},{1,9},{2,10},{3,11},{4,12},{5,13},{6,14},{7,15},{8,0},{9,1},... | collective-permute-start | bytes 1216520 | tf_op jit(solution)/shard_map/ppermute | solution.py:60
  10.2 19.7 %collective-permute-done.3.refs_4_ = bf16[176,1152]{1,0:T(8,128)(2,1)S(1)} collective-permute-done((bf16[176,1152]{1,0:T(8,128)(2,1)S(1)}, bf16[176,1152]{1,0:T(8,128)(2,1)S(1)}, u32[]{:S(2)}, u32[]{:S(2)}) %collective-permute-start.3) | collective-permute-done | bytes 405536 | tf_op jit(solution)/shard_map/ppermute | solution.py:60
  29.9 0.0 collective-permute-start.4
  29.9 0.8 %collective-permute-done.1.refs_2_ = bf16[272,1152]{1,0:T(8,128)(2,1)S(1)} collective-permute-done((bf16[272,1152]{1,0:T(8,128)(2,1)S(1)}, bf16[272,1152]{1,0:T(8,128)(2,1)S(1)}, u32[]{:S(2)}, u32[]{:S(2)}) %collective-permute-start.1) | collective-permute-done | bytes 626720 | tf_op jit(solution)/shard_map/ppermute | solution.py:60
  30.8 0.0 copy-start
  30.8 0.1 collective-permute-start.2
  30.8 3.2 %collective-permute-start.14 = (bf16[176,1152]{1,0:T(8,128)(2,1)S(1)}, bf16[176,1152]{1,0:T(8,128)(2,1)S(1)}, u32[]{:S(2)}, u32[]{:S(2)}) collective-permute-start(bf16[176,1152]{1,0:T(8,128)(2,1)S(1)} %collective-permute-done.3.refs_4_), channel_id=1, source_target_pairs={{0,4},{1,5},{2,6},{3,7},{4,0},{5,1},{6,2},{7,3},{8,12},{9,13},{10,... | collective-permute-start | bytes 1216520 | tf_op jit(solution)/shard_map/ppermute | solution.py:60
  34.1 0.0 collective-permute-done.5.refs_9_.refs_3_.refs_11_
  34.1 0.0 collective-permute-done.6.refs_10_.refs_4_.refs_12_
  34.1 1.6 %collective-permute-start.13 = (bf16[1216,256]{1,0:T(8,128)(2,1)S(1)}, bf16[1216,256]{1,0:T(8,128)(2,1)S(1)}, u32[]{:S(2)}, u32[]{:S(2)}) collective-permute-start(bf16[1216,256]{1,0:T(8,128)(2,1)S(1)} %slice.15), channel_id=1, source_target_pairs={{0,2},{1,3},{2,0},{3,1},{4,6},{5,7},{6,4},{7,5},{8,10},{9,11},{10,... | collective-permute-start | bytes 1867784 | tf_op jit(solution)/shard_map/ppermute | solution.py:60
  35.7 1.6 %collective-permute-start.12 = (bf16[1024,256]{1,0:T(8,128)(2,1)S(1)}, bf16[1024,256]{1,0:T(8,128)(2,1)S(1)}, u32[]{:S(2)}, u32[]{:S(2)}) collective-permute-start(bf16[1024,256]{1,0:T(8,128)(2,1)S(1)} %slice.14), channel_id=1, source_target_pairs={{0,16},{1,17},{2,18},{3,19},{4,20},{5,21},{6,22},{7,23},{8,24},{9,... | collective-permute-start | bytes 1572872 | tf_op jit(solution)/shard_map/ppermute | solution.py:60
  37.3 0.0 collective-permute-done.4.refs_5_
  37.3 1.1 %collective-permute-start.8 = (bf16[96,1152]{1,0:T(8,128)(2,1)S(1)}, bf16[96,1152]{1,0:T(8,128)(2,1)S(1)}, u32[]{:S(2)}, u32[]{:S(2)}) collective-permute-start(bf16[96,1152]{1,0:T(8,128)(2,1)S(1)} %get-tuple-element.25.refs_6_.refs_0_), channel_id=1, source_target_pairs={{0,8},{1,9},{2,10},{3,11},{4,12},{5,13},{6,14},{7,15},{8,0},{9,1},... | collective-permute-start | bytes 663560 | tf_op jit(solution)/shard_map/ppermute | solution.py:60
  38.4 0.0 collective-permute-done.2.refs_3_
  38.4 0.0 copy-done
  38.4 4.4 %shard_map.29 = (f32[3,96,256]{2,1,0:T(8,128)S(1)}, f32[3,96,128]{2,1,0:T(8,128)S(1)}, bf16[624,2240]{1,0:T(8,128)(2,1)S(1)}) custom-call(bf16[176,1152]{1,0:T(8,128)(2,1)S(1)} %get-tuple-element.22.refs_0_, bf16[176,1152]{1,0:T(8,128)(2,1)S(1)} %get-tuple-element.23.refs_1_, bf16[272,1152]{1,0:T(8,128)(2,1)S(1)} %collective-permute-done.1.refs_2_, ...), custom_call_target="tpu_custom_call" | custom-call | flops 1000 | bytes 1000 | tf_op jit(solution)/shard_map/pallas_call | solution.py:74
  42.8 5.6 %collective-permute-done.14.refs_0_ = bf16[176,1152]{1,0:T(8,128)(2,1)S(1)} collective-permute-done((bf16[176,1152]{1,0:T(8,128)(2,1)S(1)}, bf16[176,1152]{1,0:T(8,128)(2,1)S(1)}, u32[]{:S(2)}, u32[]{:S(2)}) %collective-permute-start.14) | collective-permute-done | bytes 405536 | tf_op jit(solution)/shard_map/ppermute | solution.py:60
  48.4 0.0 collective-permute-start.15
  48.4 0.0 collective-permute-done.8.refs_4_
  48.4 1.7 %collective-permute-start.10 = (bf16[96,1152]{1,0:T(8,128)(2,1)S(1)}, bf16[96,1152]{1,0:T(8,128)(2,1)S(1)}, u32[]{:S(2)}, u32[]{:S(2)}) collective-permute-start(bf16[96,1152]{1,0:T(8,128)(2,1)S(1)} %collective-permute-done.8.refs_4_), channel_id=1, source_target_pairs={{0,4},{1,5},{2,6},{3,7},{4,0},{5,1},{6,2},{7,3},{8,12},{9,13},{10,... | collective-permute-start | bytes 663560 | tf_op jit(solution)/shard_map/ppermute | solution.py:60
  50.1 0.0 collective-permute-start.9
  50.1 0.0 collective-permute-done.15.refs_1_
  50.2 1.7 %shard_map.30.refs_4_.refs_5_.refs_6_ = f32[3,96,128]{2,1,0:T(8,128)S(1)} custom-call(bf16[176,1152]{1,0:T(8,128)(2,1)S(1)} %collective-permute-done.14.refs_0_, bf16[176,1152]{1,0:T(8,128)(2,1)S(1)} %collective-permute-done.15.refs_1_, bf16[2240,256]{1,0:T(8,128)(2,1)S(1)} %bitcast.10, ...), custom_call_target="tpu_custom_call" | custom-call | flops 1000 | bytes 1000 | tf_op jit(solution)/shard_map/pallas_call | solution.py:74
  51.8 0.0 collective-permute-done.12.refs_8_.refs_1_.refs_2_
  51.9 0.0 collective-permute-done.13.refs_9_.refs_2_.refs_3_
  51.9 1.1 %shard_map.32.refs_7_ = f32[1,96,128]{2,1,0:T(8,128)S(1)} custom-call(bf16[624,2240]{1,0:T(8,128)(2,1)S(1)} %get-tuple-element.36.refs_0_, bf16[1024,256]{1,0:T(8,128)(2,1)S(1)} %collective-permute-done.12.refs_8_.refs_1_.refs_2_, bf16[1216,256]{1,0:T(8,128)(2,1)S(1)} %collective-permute-done.13.refs_9_.refs_2_.refs_3_), custom_call_target="tpu_custom_call" | custom-call | flops 1000 | bytes 1000 | tf_op jit(solution)/shard_map/pallas_call | solution.py:74
  53.0 0.7 shard_map.33.a_ref.refs_2_.refs_1_
  53.7 0.5 collective-permute-start.16
  54.2 2.1 %collective-permute-done.10.refs_6_ = bf16[96,1152]{1,0:T(8,128)(2,1)S(1)} collective-permute-done((bf16[96,1152]{1,0:T(8,128)(2,1)S(1)}, bf16[96,1152]{1,0:T(8,128)(2,1)S(1)}, u32[]{:S(2)}, u32[]{:S(2)}) %collective-permute-start.10) | collective-permute-done | bytes 221216 | tf_op jit(solution)/shard_map/ppermute | solution.py:60
  56.3 0.0 collective-permute-start.11
  56.3 0.6 collective-permute-start.7
  56.9 0.0 collective-permute-done.16.b_ref.refs_3_.refs_2_
  56.9 2.7 %collective-permute-start.17 = (bf16[2,96,128]{2,1,0:T(8,128)(2,1)S(1)}, bf16[2,96,128]{2,1,0:T(8,128)(2,1)S(1)}, u32[]{:S(2)}, u32[]{:S(2)}) collective-permute-start(bf16[2,96,128]{2,1,0:T(8,128)(2,1)S(1)} %shard_map.34), channel_id=1, source_target_pairs={{0,12},{1,13},{2,14},{3,15},{4,8},{5,9},{6,10},{7,11},{8,4},{9,5},... | collective-permute-start | bytes 147464 | tf_op jit(solution)/shard_map/ppermute | solution.py:60
  59.6 0.0 collective-permute-start.18
  59.7 0.0 collective-permute-done.9.refs_5_
  59.7 1.7 %collective-permute-start.19 = (bf16[2,96,128]{2,1,0:T(8,128)(2,1)S(1)}, bf16[2,96,128]{2,1,0:T(8,128)(2,1)S(1)}, u32[]{:S(2)}, u32[]{:S(2)}) collective-permute-start(bf16[2,96,128]{2,1,0:T(8,128)(2,1)S(1)} %shard_map.34), channel_id=1, source_target_pairs={{0,4},{1,5},{2,6},{3,7},{4,0},{5,1},{6,2},{7,3},{8,12},{9,13},{10,... | collective-permute-start | bytes 147464 | tf_op jit(solution)/shard_map/ppermute | solution.py:60
  61.4 0.0 collective-permute-done.11.refs_7_
  61.4 0.0 collective-permute-done.7.refs_3_
  61.4 1.8 %shard_map.31.refs_1_.refs_0_ = f32[13,96,256]{2,1,0:T(8,128)S(1)} custom-call(bf16[96,1152]{1,0:T(8,128)(2,1)S(1)} %get-tuple-element.25.refs_6_.refs_0_, bf16[96,1152]{1,0:T(8,128)(2,1)S(1)} %get-tuple-element.26.refs_7_.refs_1_, bf16[272,1152]{1,0:T(8,128)(2,1)S(1)} %collective-permute-done.1.refs_2_, ...), custom_call_target="tpu_custom_call" | custom-call | flops 1000 | bytes 1000 | tf_op jit(solution)/shard_map/pallas_call | solution.py:74
  63.2 0.0 collective-permute-done.17.refs_4_.refs_3_
  63.2 1.5 %collective-permute-done.18.refs_5_.refs_4_ = bf16[2,96,128]{2,1,0:T(8,128)(2,1)S(1)} collective-permute-done((bf16[2,96,128]{2,1,0:T(8,128)(2,1)S(1)}, bf16[2,96,128]{2,1,0:T(8,128)(2,1)S(1)}, u32[]{:S(2)}, u32[]{:S(2)}) %collective-permute-start.18) | collective-permute-done | bytes 49184 | tf_op jit(solution)/shard_map/ppermute | solution.py:60
  64.7 0.1 collective-permute-done.19.refs_6_.refs_5_
  64.8 0.6 shard_map.37
  65.3 2.5 %collective-permute-start.22 = (bf16[4,80,256]{2,1,0:T(8,128)(2,1)S(1)}, bf16[4,80,256]{2,1,0:T(8,128)(2,1)S(1)}, u32[]{:S(2)}, u32[]{:S(2)}) collective-permute-start(bf16[4,80,256]{2,1,0:T(8,128)(2,1)S(1)} %shard_map.37), channel_id=1, source_target_pairs={{0,18},{1,19},{2,16},{3,17},{4,22},{5,23},{6,20},{7,21},{8,26},{9,... | collective-permute-start | bytes 491528 | tf_op jit(solution)/shard_map/ppermute | solution.py:60
  67.9 0.8 %shard_map.36 = (bf16[4,80,256]{2,1,0:T(8,128)(2,1)S(1)}, bf16[4,80,256]{2,1,0:T(8,128)(2,1)S(1)}) custom-call(f32[3,96,256]{2,1,0:T(8,128)S(1)} %get-tuple-element.29.refs_0_, f32[13,96,256]{2,1,0:T(8,128)S(1)} %shard_map.31.refs_1_.refs_0_, f32[4,96,128]{2,1,0:T(8,128)S(1)} %shard_map.33.a_ref.refs_2_.refs_1_, ...), custom_call_target="tpu_custom_call" | custom-call | flops 1000 | bytes 1000 | tf_op jit(solution)/shard_map/pallas_call | solution.py:74
  68.7 0.6 collective-permute-start.20
  69.3 0.5 collective-permute-start.21
  69.8 0.6 shard_map.35.refs_0_
  70.4 2.0 %collective-permute-done.22.refs_3_ = bf16[4,80,256]{2,1,0:T(8,128)(2,1)S(1)} collective-permute-done((bf16[4,80,256]{2,1,0:T(8,128)(2,1)S(1)}, bf16[4,80,256]{2,1,0:T(8,128)(2,1)S(1)}, u32[]{:S(2)}, u32[]{:S(2)}) %collective-permute-start.22) | collective-permute-done | bytes 163872 | tf_op jit(solution)/shard_map/ppermute | solution.py:60
  72.4 2.8 %collective-permute-done.20.refs_1_ = bf16[4,80,256]{2,1,0:T(8,128)(2,1)S(1)} collective-permute-done((bf16[4,80,256]{2,1,0:T(8,128)(2,1)S(1)}, bf16[4,80,256]{2,1,0:T(8,128)(2,1)S(1)}, u32[]{:S(2)}, u32[]{:S(2)}) %collective-permute-start.20) | collective-permute-done | bytes 163872 | tf_op jit(solution)/shard_map/ppermute | solution.py:60
  75.1 0.1 collective-permute-done.21.refs_2_
  75.2 1.1 %shard_map.38 = bf16[256,1280]{1,0:T(8,128)(2,1)} custom-call(bf16[4,80,256]{2,1,0:T(8,128)(2,1)S(1)} %shard_map.35.refs_0_, bf16[4,80,256]{2,1,0:T(8,128)(2,1)S(1)} %collective-permute-done.20.refs_1_, bf16[4,80,256]{2,1,0:T(8,128)(2,1)S(1)} %collective-permute-done.21.refs_2_, bf16[4,80,256]{2,1,0:T(8,128)(2,1)S(1)} %collective-permute-done.22.refs_3_), custom_call_target="tpu_custom_call" | custom-call | flops 1000 | bytes 1000 | tf_op jit(solution)/shard_map/pallas_call | solution.py:74
  (5 shorter events, 0.1 us)
Async XLA Ops:
  0.0 4.5 %collective-permute-start = (bf16[240,2240]{1,0:T(8,128)(2,1)}, bf16[240,2240]{1,0:T(8,128)(2,1)S(1)}, u32[]{:S(2)}, u32[]{:S(2)}) collective-permute-start(bf16[240,2240]{1,0:T(8,128)(2,1)} %bitcast.12), channel_id=1, source_target_pairs={{0,1},{1,0},{2,3},{3,2},{4,5},{5,4},{6,7},{7,6},{8,9},{9,8},{10,11... | collective-permute-start | bytes 3225608 | tf_op jit(solution)/shard_map/ppermute | solution.py:60
  0.5 33.6 %collective-permute-start.5 = (bf16[2240,256]{1,0:T(8,128)(2,1)}, bf16[2240,256]{1,0:T(8,128)(2,1)S(1)}, u32[]{:S(2)}, u32[]{:S(2)}) collective-permute-start(bf16[2240,256]{1,0:T(8,128)(2,1)} %bitcast.7), channel_id=1, source_target_pairs={{0,2},{1,3},{2,0},{3,1},{4,6},{5,7},{6,4},{7,5},{8,10},{9,11},{10,... | collective-permute-start | bytes 3440648 | tf_op jit(solution)/shard_map/ppermute | solution.py:60
  3.0 31.1 %collective-permute-start.6 = (bf16[2240,256]{1,0:T(8,128)(2,1)}, bf16[2240,256]{1,0:T(8,128)(2,1)S(1)}, u32[]{:S(2)}, u32[]{:S(2)}) collective-permute-start(bf16[2240,256]{1,0:T(8,128)(2,1)} %bitcast.8), channel_id=1, source_target_pairs={{0,16},{1,17},{2,18},{3,19},{4,20},{5,21},{6,22},{7,23},{8,24},{9,... | collective-permute-start | bytes 3440648 | tf_op jit(solution)/shard_map/ppermute | solution.py:60
  4.5 1.2 %copy-start.1 = (bf16[3,2240,80]{1,2,0:T(8,128)(2,1)S(1)}, bf16[3,2240,80]{1,2,0:T(8,128)(2,1)}, u32[]{:S(2)}) copy-start(bf16[3,2240,80]{1,2,0:T(8,128)(2,1)} %param.3) | copy-start | bytes 3225604
  6.0 24.7 %collective-permute-start.1 = (bf16[272,1152]{1,0:T(8,128)(2,1)S(1)}, bf16[272,1152]{1,0:T(8,128)(2,1)S(1)}, u32[]{:S(2)}, u32[]{:S(2)}) collective-permute-start(bf16[272,1152]{1,0:T(8,128)(2,1)S(1)} %get-tuple-element.24), channel_id=1, source_target_pairs={{0,4},{1,5},{2,6},{3,7},{4,0},{5,1},{6,2},{7,3},{8,12},{9,13},{10,... | collective-permute-start | bytes 1880072 | tf_op jit(solution)/shard_map/ppermute | solution.py:60
  7.6 22.3 %collective-permute-start.3 = (bf16[176,1152]{1,0:T(8,128)(2,1)S(1)}, bf16[176,1152]{1,0:T(8,128)(2,1)S(1)}, u32[]{:S(2)}, u32[]{:S(2)}) collective-permute-start(bf16[176,1152]{1,0:T(8,128)(2,1)S(1)} %get-tuple-element.22.refs_0_), channel_id=1, source_target_pairs={{0,8},{1,9},{2,10},{3,11},{4,12},{5,13},{6,14},{7,15},{8,0},{9,1},... | collective-permute-start | bytes 1216520 | tf_op jit(solution)/shard_map/ppermute | solution.py:60
  29.9 7.4 %collective-permute-start.4 = (bf16[176,1152]{1,0:T(8,128)(2,1)S(1)}, bf16[176,1152]{1,0:T(8,128)(2,1)S(1)}, u32[]{:S(2)}, u32[]{:S(2)}) collective-permute-start(bf16[176,1152]{1,0:T(8,128)(2,1)S(1)} %collective-permute-done.3.refs_4_), channel_id=1, source_target_pairs={{0,1},{1,0},{2,3},{3,2},{4,5},{5,4},{6,7},{7,6},{8,9},{9,8},{10,11... | collective-permute-start | bytes 1216520 | tf_op jit(solution)/shard_map/ppermute | solution.py:60
  30.8 7.7 %copy-start = (bf16[1,256,2240]{1,2,0:T(8,128)(2,1)S(1)}, bf16[1,256,2240]{1,2,0:T(8,128)(2,1)}, u32[]{:S(2)}) copy-start(bf16[1,256,2240]{1,2,0:T(8,128)(2,1)} %param.2) | copy-start | bytes 3440644
  30.8 7.7 %collective-permute-start.2 = (bf16[176,1152]{1,0:T(8,128)(2,1)S(1)}, bf16[176,1152]{1,0:T(8,128)(2,1)S(1)}, u32[]{:S(2)}, u32[]{:S(2)}) collective-permute-start(bf16[176,1152]{1,0:T(8,128)(2,1)S(1)} %slice.16), channel_id=1, source_target_pairs={{0,1},{1,0},{2,3},{3,2},{4,5},{5,4},{6,7},{7,6},{8,9},{9,8},{10,11... | collective-permute-start | bytes 1216520 | tf_op jit(solution)/shard_map/ppermute | solution.py:60
  30.8 17.6 %collective-permute-start.14 = (bf16[176,1152]{1,0:T(8,128)(2,1)S(1)}, bf16[176,1152]{1,0:T(8,128)(2,1)S(1)}, u32[]{:S(2)}, u32[]{:S(2)}) collective-permute-start(bf16[176,1152]{1,0:T(8,128)(2,1)S(1)} %collective-permute-done.3.refs_4_), channel_id=1, source_target_pairs={{0,4},{1,5},{2,6},{3,7},{4,0},{5,1},{6,2},{7,3},{8,12},{9,13},{10,... | collective-permute-start | bytes 1216520 | tf_op jit(solution)/shard_map/ppermute | solution.py:60
  34.1 17.7 %collective-permute-start.13 = (bf16[1216,256]{1,0:T(8,128)(2,1)S(1)}, bf16[1216,256]{1,0:T(8,128)(2,1)S(1)}, u32[]{:S(2)}, u32[]{:S(2)}) collective-permute-start(bf16[1216,256]{1,0:T(8,128)(2,1)S(1)} %slice.15), channel_id=1, source_target_pairs={{0,2},{1,3},{2,0},{3,1},{4,6},{5,7},{6,4},{7,5},{8,10},{9,11},{10,... | collective-permute-start | bytes 1867784 | tf_op jit(solution)/shard_map/ppermute | solution.py:60
  35.7 16.1 %collective-permute-start.12 = (bf16[1024,256]{1,0:T(8,128)(2,1)S(1)}, bf16[1024,256]{1,0:T(8,128)(2,1)S(1)}, u32[]{:S(2)}, u32[]{:S(2)}) collective-permute-start(bf16[1024,256]{1,0:T(8,128)(2,1)S(1)} %slice.14), channel_id=1, source_target_pairs={{0,16},{1,17},{2,18},{3,19},{4,20},{5,21},{6,22},{7,23},{8,24},{9,... | collective-permute-start | bytes 1572872 | tf_op jit(solution)/shard_map/ppermute | solution.py:60
  37.3 11.1 %collective-permute-start.8 = (bf16[96,1152]{1,0:T(8,128)(2,1)S(1)}, bf16[96,1152]{1,0:T(8,128)(2,1)S(1)}, u32[]{:S(2)}, u32[]{:S(2)}) collective-permute-start(bf16[96,1152]{1,0:T(8,128)(2,1)S(1)} %get-tuple-element.25.refs_6_.refs_0_), channel_id=1, source_target_pairs={{0,8},{1,9},{2,10},{3,11},{4,12},{5,13},{6,14},{7,15},{8,0},{9,1},... | collective-permute-start | bytes 663560 | tf_op jit(solution)/shard_map/ppermute | solution.py:60
  48.4 1.7 %collective-permute-start.15 = (bf16[176,1152]{1,0:T(8,128)(2,1)S(1)}, bf16[176,1152]{1,0:T(8,128)(2,1)S(1)}, u32[]{:S(2)}, u32[]{:S(2)}) collective-permute-start(bf16[176,1152]{1,0:T(8,128)(2,1)S(1)} %collective-permute-done.14.refs_0_), channel_id=1, source_target_pairs={{0,1},{1,0},{2,3},{3,2},{4,5},{5,4},{6,7},{7,6},{8,9},{9,8},{10,11... | collective-permute-start | bytes 1216520 | tf_op jit(solution)/shard_map/ppermute | solution.py:60
  48.4 7.8 %collective-permute-start.10 = (bf16[96,1152]{1,0:T(8,128)(2,1)S(1)}, bf16[96,1152]{1,0:T(8,128)(2,1)S(1)}, u32[]{:S(2)}, u32[]{:S(2)}) collective-permute-start(bf16[96,1152]{1,0:T(8,128)(2,1)S(1)} %collective-permute-done.8.refs_4_), channel_id=1, source_target_pairs={{0,4},{1,5},{2,6},{3,7},{4,0},{5,1},{6,2},{7,3},{8,12},{9,13},{10,... | collective-permute-start | bytes 663560 | tf_op jit(solution)/shard_map/ppermute | solution.py:60
  50.1 9.5 %collective-permute-start.9 = (bf16[96,1152]{1,0:T(8,128)(2,1)S(1)}, bf16[96,1152]{1,0:T(8,128)(2,1)S(1)}, u32[]{:S(2)}, u32[]{:S(2)}) collective-permute-start(bf16[96,1152]{1,0:T(8,128)(2,1)S(1)} %collective-permute-done.8.refs_4_), channel_id=1, source_target_pairs={{0,1},{1,0},{2,3},{3,2},{4,5},{5,4},{6,7},{7,6},{8,9},{9,8},{10,11... | collective-permute-start | bytes 663560 | tf_op jit(solution)/shard_map/ppermute | solution.py:60
  53.7 3.2 %collective-permute-start.16 = (f32[4,96,128]{2,1,0:T(8,128)S(1)}, f32[4,96,128]{2,1,0:T(8,128)S(1)}, u32[]{:S(2)}, u32[]{:S(2)}) collective-permute-start(f32[4,96,128]{2,1,0:T(8,128)S(1)} %shard_map.33.a_ref.refs_2_.refs_1_), channel_id=1, source_target_pairs={{0,1},{1,0},{2,3},{3,2},{4,5},{5,4},{6,7},{7,6},{8,9},{9,8},{10,11... | collective-permute-start | bytes 589832 | tf_op jit(solution)/shard_map/ppermute | solution.py:60
  56.3 5.1 %collective-permute-start.11 = (bf16[96,1152]{1,0:T(8,128)(2,1)S(1)}, bf16[96,1152]{1,0:T(8,128)(2,1)S(1)}, u32[]{:S(2)}, u32[]{:S(2)}) collective-permute-start(bf16[96,1152]{1,0:T(8,128)(2,1)S(1)} %collective-permute-done.10.refs_6_), channel_id=1, source_target_pairs={{0,1},{1,0},{2,3},{3,2},{4,5},{5,4},{6,7},{7,6},{8,9},{9,8},{10,11... | collective-permute-start | bytes 663560 | tf_op jit(solution)/shard_map/ppermute | solution.py:60
  56.3 5.1 %collective-permute-start.7 = (bf16[96,1152]{1,0:T(8,128)(2,1)S(1)}, bf16[96,1152]{1,0:T(8,128)(2,1)S(1)}, u32[]{:S(2)}, u32[]{:S(2)}) collective-permute-start(bf16[96,1152]{1,0:T(8,128)(2,1)S(1)} %slice.17), channel_id=1, source_target_pairs={{0,1},{1,0},{2,3},{3,2},{4,5},{5,4},{6,7},{7,6},{8,9},{9,8},{10,11... | collective-permute-start | bytes 663560 | tf_op jit(solution)/shard_map/ppermute | solution.py:60
  56.9 6.3 %collective-permute-start.17 = (bf16[2,96,128]{2,1,0:T(8,128)(2,1)S(1)}, bf16[2,96,128]{2,1,0:T(8,128)(2,1)S(1)}, u32[]{:S(2)}, u32[]{:S(2)}) collective-permute-start(bf16[2,96,128]{2,1,0:T(8,128)(2,1)S(1)} %shard_map.34), channel_id=1, source_target_pairs={{0,12},{1,13},{2,14},{3,15},{4,8},{5,9},{6,10},{7,11},{8,4},{9,5},... | collective-permute-start | bytes 147464 | tf_op jit(solution)/shard_map/ppermute | solution.py:60
  59.6 5.0 %collective-permute-start.18 = (bf16[2,96,128]{2,1,0:T(8,128)(2,1)S(1)}, bf16[2,96,128]{2,1,0:T(8,128)(2,1)S(1)}, u32[]{:S(2)}, u32[]{:S(2)}) collective-permute-start(bf16[2,96,128]{2,1,0:T(8,128)(2,1)S(1)} %shard_map.34), channel_id=1, source_target_pairs={{0,8},{1,9},{2,10},{3,11},{4,12},{5,13},{6,14},{7,15},{8,0},{9,1},... | collective-permute-start | bytes 147464 | tf_op jit(solution)/shard_map/ppermute | solution.py:60
  59.7 5.1 %collective-permute-start.19 = (bf16[2,96,128]{2,1,0:T(8,128)(2,1)S(1)}, bf16[2,96,128]{2,1,0:T(8,128)(2,1)S(1)}, u32[]{:S(2)}, u32[]{:S(2)}) collective-permute-start(bf16[2,96,128]{2,1,0:T(8,128)(2,1)S(1)} %shard_map.34), channel_id=1, source_target_pairs={{0,4},{1,5},{2,6},{3,7},{4,0},{5,1},{6,2},{7,3},{8,12},{9,13},{10,... | collective-permute-start | bytes 147464 | tf_op jit(solution)/shard_map/ppermute | solution.py:60
  65.3 7.0 %collective-permute-start.22 = (bf16[4,80,256]{2,1,0:T(8,128)(2,1)S(1)}, bf16[4,80,256]{2,1,0:T(8,128)(2,1)S(1)}, u32[]{:S(2)}, u32[]{:S(2)}) collective-permute-start(bf16[4,80,256]{2,1,0:T(8,128)(2,1)S(1)} %shard_map.37), channel_id=1, source_target_pairs={{0,18},{1,19},{2,16},{3,17},{4,22},{5,23},{6,20},{7,21},{8,26},{9,... | collective-permute-start | bytes 491528 | tf_op jit(solution)/shard_map/ppermute | solution.py:60
  68.7 6.5 %collective-permute-start.20 = (bf16[4,80,256]{2,1,0:T(8,128)(2,1)S(1)}, bf16[4,80,256]{2,1,0:T(8,128)(2,1)S(1)}, u32[]{:S(2)}, u32[]{:S(2)}) collective-permute-start(bf16[4,80,256]{2,1,0:T(8,128)(2,1)S(1)} %get-tuple-element.37), channel_id=1, source_target_pairs={{0,2},{1,3},{2,0},{3,1},{4,6},{5,7},{6,4},{7,5},{8,10},{9,11},{10,... | collective-permute-start | bytes 491528 | tf_op jit(solution)/shard_map/ppermute | solution.py:60
  69.3 5.9 %collective-permute-start.21 = (bf16[4,80,256]{2,1,0:T(8,128)(2,1)S(1)}, bf16[4,80,256]{2,1,0:T(8,128)(2,1)S(1)}, u32[]{:S(2)}, u32[]{:S(2)}) collective-permute-start(bf16[4,80,256]{2,1,0:T(8,128)(2,1)S(1)} %get-tuple-element.38), channel_id=1, source_target_pairs={{0,16},{1,17},{2,18},{3,19},{4,20},{5,21},{6,22},{7,23},{8,24},{9,... | collective-permute-start | bytes 491528 | tf_op jit(solution)/shard_map/ppermute | solution.py:60
